TPU v7x, 32 devices: a whole 2x2x4 slice. The times are simulated.
32 devices in a mesh: groups: 2 (over y), rows: 4 (over z), pipe: 2 (over x), cols: 2 (over core).
Axes of the slice: x: 2, y: 2, z: 4, core: 2. Of those that a mesh axis runs over, the one named last changes fastest.
Arguments:
- inputs: bfloat16 [8, 16, 256, 128], P(None, ('groups', 'rows'), 'cols'), parts along dimension 1, may hold values from -6 to 6
- hidden_init: bfloat16 [2, 16, 256, 128], P('pipe', ('groups', 'rows'), 'cols'), parts along dimension 1, may hold values from -3 to 3
- cell_init: float32 [2, 16, 256, 128], P('pipe', ('groups', 'rows'), 'cols'), parts along dimension 1, may hold values from -4 to 4
- kernels: bfloat16 [2, 2304, 512], P('pipe'), may hold values from -0.5 to 2.5
- biases: float32 [2, 512], P('pipe'), may hold values from -3 to 4.25
Outputs:
- hidden_seq: bfloat16 [2, 8, 16, 256, 128], P('pipe', None, ('groups', 'rows'), 'cols'), parts along dimension 2
- cell_final: float32 [2, 16, 256, 128], P('pipe', ('groups', 'rows'), 'cols'), parts along dimension 1
There are 2 independent parts, one for each index of `groups`. A program takes and returns all parts, laid end to end along the dimension named above; an argument that names none is the same for every part. Nothing has to cross between parts.
All inputs are finite; a program needn't handle non-finite values.
Results may differ from a plain program's by a relative error of at most 0.0038.
Values may be sent and summed in bfloat16 or wider, within the bound.
No kernel may reach another device: no remote copies, remote signals or barrier semaphores. Data moves between devices by JAX's collectives and lax.ppermute only.
A program may use at most 64 MiB of HBM per device.

v0:
```python
import jax
import jax.numpy as jnp
from jax import lax
from jax.sharding import PartitionSpec as P

STEPS = 8


def from_behind(block, axis, distance):
    devices = range(lax.axis_size(axis))
    route = [(i - distance, i) for i in devices if i - distance in devices]
    return lax.ppermute(block, axis, route)


def padded_2(block, sides, width):
    for axis, dim in sides:
        count = lax.axis_size(axis)
        forward = [(i, i + 1) for i in range(count - 1)]
        backward = [(target, source) for source, target in forward]
        low = lax.ppermute(
            lax.slice_in_dim(block, block.shape[dim] - width, None, axis=dim), axis, forward
        )
        high = lax.ppermute(lax.slice_in_dim(block, 0, width, axis=dim), axis, backward)
        block = jnp.concatenate([low, block, high], axis=dim)
    return block


def gate_values(padded, weights, bias_row, rows_n, cols_n):
    chans = padded.shape[-1]
    taps = [
        padded[row_off : row_off + rows_n, col_off : col_off + cols_n]
        for row_off in range(3)
        for col_off in range(3)
    ]
    slab = jnp.concatenate(taps, -1).reshape(rows_n * cols_n, 9 * chans)
    total = jnp.dot(slab, weights, preferred_element_type=jnp.float32)
    return total + bias_row


def advance(padded, cell_state, weights, bias_row):
    rows_n, cols_n, width = cell_state.shape
    gates = gate_values(padded, weights, bias_row, rows_n, cols_n).reshape(
        rows_n, cols_n, 4 * width
    )
    in_gate = jax.nn.sigmoid(gates[..., :width])
    forget = jax.nn.sigmoid(gates[..., width : 2 * width])
    candidate = jnp.tanh(gates[..., 2 * width : 3 * width])
    out_gate = jax.nn.sigmoid(gates[..., 3 * width :])
    new_cell = forget * cell_state + in_gate * candidate
    new_hidden = (out_gate * jnp.tanh(new_cell)).astype(jnp.bfloat16)
    return (new_hidden, new_cell)


def shards(inputs, hidden_init, cell_init, kernels, biases):
    layer_idx = lax.axis_index("pipe")
    section_count = STEPS + lax.axis_size("pipe") - 1
    weights = kernels[0]
    bias_row = biases[0]
    produced = jnp.zeros((STEPS,) + hidden_init.shape[1:], jnp.bfloat16)

    def section(section_no, carry):
        hidden, cell_state, outputs = carry
        time_raw = section_no - layer_idx
        time_idx = jnp.clip(time_raw, 0, STEPS - 1)
        active = jnp.logical_and(time_raw >= 0, time_raw < STEPS)
        incoming = from_behind(hidden, "pipe", 1)
        own_input = lax.dynamic_index_in_dim(inputs, time_idx, 0, keepdims=False)
        x_map = jnp.where(layer_idx == 0, own_input, incoming)
        padded = padded_2(jnp.concatenate([x_map, hidden], -1), (("rows", 0), ("cols", 1)), 1)
        new_hidden, new_cell = lax.cond(
            active,
            lambda: advance(padded, cell_state, weights, bias_row),
            lambda: (hidden, cell_state),
        )
        previous = lax.dynamic_index_in_dim(outputs, time_idx, 0, keepdims=False)
        stored = jnp.where(active, new_hidden, previous)
        outputs = lax.dynamic_update_index_in_dim(outputs, stored, time_idx, 0)
        return (new_hidden, new_cell, outputs)

    hidden, cell_state, produced = lax.fori_loop(
        0, section_count, section, (hidden_init[0], cell_init[0], produced)
    )
    return (produced[None], cell_state[None])


def solution(mesh):
    return jax.shard_map(
        shards,
        mesh=mesh,
        in_specs=(
            P(None, ("groups", "rows"), "cols", None),
            P("pipe", ("groups", "rows"), "cols", None),
            P("pipe", ("groups", "rows"), "cols", None),
            P("pipe", None, None),
            P("pipe", None),
        ),
        out_specs=(
            P("pipe", None, ("groups", "rows"), "cols", None),
            P("pipe", ("groups", "rows"), "cols", None),
        ),
        check_vma=False,
    )
```

profile of v0, /device:TPU:6, one launch (start us, length us, event | category | flops | bytes accessed | tf_op | source)
XLA Modules:
  0.0 208.9 jit_solution(309720816410481618)
XLA Ops:
  2.5 205.6 %while.18 = (s32[]{:T(128)}, bf16[2,128,128]{2,1,0:T(8,128)(2,1)S(1)}, f32[2,128,128]{2,1,0:T(8,128)S(1)}, bf16[8,2,128,128]{3,2,1,0:T(8,128)(2,1)S(1)}, s32[]{:...) while((s32[]{:T(128)}, ...), condition=%wide.region_3.4_spmd, body=%wide.region_0.3_spmd.sunk | while | flops 607805440 | bytes 19638800 | solution.py:80
  2.5 1.3 collective-permute-start
  3.8 4.8 %collective-permute-done = bf16[2,128,128]{2,1,0:T(8,128)(2,1)S(1)} collective-permute-done((bf16[2,128,128]{2,1,0:T(8,128)(2,1)S(1)}, bf16[2,128,128]{2,1,0:T(8,128)(2,1)S(1)}, u32[]{:S(2)}, u32[]{:S(2)}) %collective-permute-start) | collective-permute-done | bytes 65568 | tf_op jit(solution)/shard_map/while/body/eval_jaxpr/ppermute | solution.py:12
  10.8 4.5 %collective-permute-start.2 = (bf16[1,128,256]{2,1,0:T(8,128)(2,1)S(1)}, bf16[1,128,256]{2,1,0:T(8,128)(2,1)S(1)}, u32[]{:S(2)}, u32[]{:S(2)}) collective-permute-start(bf16[1,128,256]{2,1,0:T(8,128)(2,1)S(1)} %get-tuple-element.297), channel_id=1, source_target_pairs={{0,4},{4,8},{8,12},{1,5},{5,9},{9,13},{2,6},{6,10},{10,14},{3,7},{... | collective-permute-start | bytes 196616 | tf_op jit(solution)/shard_map/while/body/eval_jaxpr/ppermute | solution.py:20
  15.7 1.6 collective-permute-done.2
  18.6 3.0 %collective-permute-start.4 = (bf16[4,1,256]{2,1,0:T(2,128)(2,1)S(1)}, bf16[4,1,256]{2,1,0:T(2,128)(2,1)S(1)}, u32[]{:S(2)}, u32[]{:S(2)}) collective-permute-start(bf16[4,1,256]{2,1,0:T(2,128)(2,1)S(1)} %get-tuple-element.299), channel_id=1, source_target_pairs={{0,1},{2,3},{4,5},{6,7},{8,9},{10,11},{12,13},{14,15},{16,17},{18,... | collective-permute-start | bytes 6152 | tf_op jit(solution)/shard_map/while/body/eval_jaxpr/ppermute | solution.py:20
  24.0 4.9 %collective-permute-done = bf16[2,128,128]{2,1,0:T(8,128)(2,1)S(1)} collective-permute-done((bf16[2,128,128]{2,1,0:T(8,128)(2,1)S(1)}, bf16[2,128,128]{2,1,0:T(8,128)(2,1)S(1)}, u32[]{:S(2)}, u32[]{:S(2)}) %collective-permute-start) | collective-permute-done | bytes 65568 | tf_op jit(solution)/shard_map/while/body/eval_jaxpr/ppermute | solution.py:12
  29.8 1.3 collective-permute-start.1
  31.1 4.9 %collective-permute-start.2 = (bf16[1,128,256]{2,1,0:T(8,128)(2,1)S(1)}, bf16[1,128,256]{2,1,0:T(8,128)(2,1)S(1)}, u32[]{:S(2)}, u32[]{:S(2)}) collective-permute-start(bf16[1,128,256]{2,1,0:T(8,128)(2,1)S(1)} %get-tuple-element.297), channel_id=1, source_target_pairs={{0,4},{4,8},{8,12},{1,5},{5,9},{9,13},{2,6},{6,10},{10,14},{3,7},{... | collective-permute-start | bytes 196616 | tf_op jit(solution)/shard_map/while/body/eval_jaxpr/ppermute | solution.py:20
  36.3 1.6 collective-permute-done.2
  39.2 3.0 %collective-permute-start.4 = (bf16[4,1,256]{2,1,0:T(2,128)(2,1)S(1)}, bf16[4,1,256]{2,1,0:T(2,128)(2,1)S(1)}, u32[]{:S(2)}, u32[]{:S(2)}) collective-permute-start(bf16[4,1,256]{2,1,0:T(2,128)(2,1)S(1)} %get-tuple-element.299), channel_id=1, source_target_pairs={{0,1},{2,3},{4,5},{6,7},{8,9},{10,11},{12,13},{14,15},{16,17},{18,... | collective-permute-start | bytes 6152 | tf_op jit(solution)/shard_map/while/body/eval_jaxpr/ppermute | solution.py:20
  43.1 2.6 %conditional.2 = ((bf16[2,128,128]{2,1,0:T(8,128)(2,1)S(1)}, f32[2,128,128]{2,1,0:T(8,128)S(1)})) conditional(s32[]{:T(128)} %convert_element_type.13, (bf16[2,128,128]{2,1,0:T(8,128)(2,1)S(1)}, f32[2,128,128]{2,1,0:T(8,128)S(1)}) %tuple.52, (bf16[4,130,256]{2,1,0:T(8,128)(2,1)S(1)}, bf16[4,128,256]{2,1,0:T(8,128)(2,1)S(1)}, ...), branch_computations={%region_1.1_spmd, %region_2.2_spmd} | conditional | flops 604569600 | bytes 16713764 | solution.py:70
  43.4 1.4 copy-done.2
  47.1 4.9 %collective-permute-done = bf16[2,128,128]{2,1,0:T(8,128)(2,1)S(1)} collective-permute-done((bf16[2,128,128]{2,1,0:T(8,128)(2,1)S(1)}, bf16[2,128,128]{2,1,0:T(8,128)(2,1)S(1)}, u32[]{:S(2)}, u32[]{:S(2)}) %collective-permute-start) | collective-permute-done | bytes 65568 | tf_op jit(solution)/shard_map/while/body/eval_jaxpr/ppermute | solution.py:12
  52.9 1.3 collective-permute-start.1
  54.2 4.9 %collective-permute-start.2 = (bf16[1,128,256]{2,1,0:T(8,128)(2,1)S(1)}, bf16[1,128,256]{2,1,0:T(8,128)(2,1)S(1)}, u32[]{:S(2)}, u32[]{:S(2)}) collective-permute-start(bf16[1,128,256]{2,1,0:T(8,128)(2,1)S(1)} %get-tuple-element.297), channel_id=1, source_target_pairs={{0,4},{4,8},{8,12},{1,5},{5,9},{9,13},{2,6},{6,10},{10,14},{3,7},{... | collective-permute-start | bytes 196616 | tf_op jit(solution)/shard_map/while/body/eval_jaxpr/ppermute | solution.py:20
  59.4 1.6 collective-permute-done.2
  62.4 3.0 %collective-permute-start.4 = (bf16[4,1,256]{2,1,0:T(2,128)(2,1)S(1)}, bf16[4,1,256]{2,1,0:T(2,128)(2,1)S(1)}, u32[]{:S(2)}, u32[]{:S(2)}) collective-permute-start(bf16[4,1,256]{2,1,0:T(2,128)(2,1)S(1)} %get-tuple-element.299), channel_id=1, source_target_pairs={{0,1},{2,3},{4,5},{6,7},{8,9},{10,11},{12,13},{14,15},{16,17},{18,... | collective-permute-start | bytes 6152 | tf_op jit(solution)/shard_map/while/body/eval_jaxpr/ppermute | solution.py:20
  66.3 2.6 %conditional.2 = ((bf16[2,128,128]{2,1,0:T(8,128)(2,1)S(1)}, f32[2,128,128]{2,1,0:T(8,128)S(1)})) conditional(s32[]{:T(128)} %convert_element_type.13, (bf16[2,128,128]{2,1,0:T(8,128)(2,1)S(1)}, f32[2,128,128]{2,1,0:T(8,128)S(1)}) %tuple.52, (bf16[4,130,256]{2,1,0:T(8,128)(2,1)S(1)}, bf16[4,128,256]{2,1,0:T(8,128)(2,1)S(1)}, ...), branch_computations={%region_1.1_spmd, %region_2.2_spmd} | conditional | flops 604569600 | bytes 16713764 | solution.py:70
  66.6 1.4 copy-done.2
  69.0 1.3 collective-permute-start
  70.3 4.9 %collective-permute-done = bf16[2,128,128]{2,1,0:T(8,128)(2,1)S(1)} collective-permute-done((bf16[2,128,128]{2,1,0:T(8,128)(2,1)S(1)}, bf16[2,128,128]{2,1,0:T(8,128)(2,1)S(1)}, u32[]{:S(2)}, u32[]{:S(2)}) %collective-permute-start) | collective-permute-done | bytes 65568 | tf_op jit(solution)/shard_map/while/body/eval_jaxpr/ppermute | solution.py:12
  77.4 4.9 %collective-permute-start.2 = (bf16[1,128,256]{2,1,0:T(8,128)(2,1)S(1)}, bf16[1,128,256]{2,1,0:T(8,128)(2,1)S(1)}, u32[]{:S(2)}, u32[]{:S(2)}) collective-permute-start(bf16[1,128,256]{2,1,0:T(8,128)(2,1)S(1)} %get-tuple-element.297), channel_id=1, source_target_pairs={{0,4},{4,8},{8,12},{1,5},{5,9},{9,13},{2,6},{6,10},{10,14},{3,7},{... | collective-permute-start | bytes 196616 | tf_op jit(solution)/shard_map/while/body/eval_jaxpr/ppermute | solution.py:20
  82.6 1.6 collective-permute-done.2
  84.2 1.3 collective-permute-start.3
  85.5 3.0 %collective-permute-start.4 = (bf16[4,1,256]{2,1,0:T(2,128)(2,1)S(1)}, bf16[4,1,256]{2,1,0:T(2,128)(2,1)S(1)}, u32[]{:S(2)}, u32[]{:S(2)}) collective-permute-start(bf16[4,1,256]{2,1,0:T(2,128)(2,1)S(1)} %get-tuple-element.299), channel_id=1, source_target_pairs={{0,1},{2,3},{4,5},{6,7},{8,9},{10,11},{12,13},{14,15},{16,17},{18,... | collective-permute-start | bytes 6152 | tf_op jit(solution)/shard_map/while/body/eval_jaxpr/ppermute | solution.py:20
  89.5 2.6 %conditional.2 = ((bf16[2,128,128]{2,1,0:T(8,128)(2,1)S(1)}, f32[2,128,128]{2,1,0:T(8,128)S(1)})) conditional(s32[]{:T(128)} %convert_element_type.13, (bf16[2,128,128]{2,1,0:T(8,128)(2,1)S(1)}, f32[2,128,128]{2,1,0:T(8,128)S(1)}) %tuple.52, (bf16[4,130,256]{2,1,0:T(8,128)(2,1)S(1)}, bf16[4,128,256]{2,1,0:T(8,128)(2,1)S(1)}, ...), branch_computations={%region_1.1_spmd, %region_2.2_spmd} | conditional | flops 604569600 | bytes 16713764 | solution.py:70
  89.8 1.4 copy-done.2
  93.5 4.9 %collective-permute-done = bf16[2,128,128]{2,1,0:T(8,128)(2,1)S(1)} collective-permute-done((bf16[2,128,128]{2,1,0:T(8,128)(2,1)S(1)}, bf16[2,128,128]{2,1,0:T(8,128)(2,1)S(1)}, u32[]{:S(2)}, u32[]{:S(2)}) %collective-permute-start) | collective-permute-done | bytes 65568 | tf_op jit(solution)/shard_map/while/body/eval_jaxpr/ppermute | solution.py:12
  99.3 1.3 collective-permute-start.1
  100.6 4.9 %collective-permute-start.2 = (bf16[1,128,256]{2,1,0:T(8,128)(2,1)S(1)}, bf16[1,128,256]{2,1,0:T(8,128)(2,1)S(1)}, u32[]{:S(2)}, u32[]{:S(2)}) collective-permute-start(bf16[1,128,256]{2,1,0:T(8,128)(2,1)S(1)} %get-tuple-element.297), channel_id=1, source_target_pairs={{0,4},{4,8},{8,12},{1,5},{5,9},{9,13},{2,6},{6,10},{10,14},{3,7},{... | collective-permute-start | bytes 196616 | tf_op jit(solution)/shard_map/while/body/eval_jaxpr/ppermute | solution.py:20
  105.8 1.6 collective-permute-done.2
  107.4 1.3 collective-permute-start.3
  108.7 3.0 %collective-permute-start.4 = (bf16[4,1,256]{2,1,0:T(2,128)(2,1)S(1)}, bf16[4,1,256]{2,1,0:T(2,128)(2,1)S(1)}, u32[]{:S(2)}, u32[]{:S(2)}) collective-permute-start(bf16[4,1,256]{2,1,0:T(2,128)(2,1)S(1)} %get-tuple-element.299), channel_id=1, source_target_pairs={{0,1},{2,3},{4,5},{6,7},{8,9},{10,11},{12,13},{14,15},{16,17},{18,... | collective-permute-start | bytes 6152 | tf_op jit(solution)/shard_map/while/body/eval_jaxpr/ppermute | solution.py:20
  112.7 2.6 %conditional.2 = ((bf16[2,128,128]{2,1,0:T(8,128)(2,1)S(1)}, f32[2,128,128]{2,1,0:T(8,128)S(1)})) conditional(s32[]{:T(128)} %convert_element_type.13, (bf16[2,128,128]{2,1,0:T(8,128)(2,1)S(1)}, f32[2,128,128]{2,1,0:T(8,128)S(1)}) %tuple.52, (bf16[4,130,256]{2,1,0:T(8,128)(2,1)S(1)}, bf16[4,128,256]{2,1,0:T(8,128)(2,1)S(1)}, ...), branch_computations={%region_1.1_spmd, %region_2.2_spmd} | conditional | flops 604569600 | bytes 16713764 | solution.py:70
  112.9 1.4 copy-done.2
  116.7 4.9 %collective-permute-done = bf16[2,128,128]{2,1,0:T(8,128)(2,1)S(1)} collective-permute-done((bf16[2,128,128]{2,1,0:T(8,128)(2,1)S(1)}, bf16[2,128,128]{2,1,0:T(8,128)(2,1)S(1)}, u32[]{:S(2)}, u32[]{:S(2)}) %collective-permute-start) | collective-permute-done | bytes 65568 | tf_op jit(solution)/shard_map/while/body/eval_jaxpr/ppermute | solution.py:12
  122.5 1.3 collective-permute-start.1
  123.8 4.9 %collective-permute-start.2 = (bf16[1,128,256]{2,1,0:T(8,128)(2,1)S(1)}, bf16[1,128,256]{2,1,0:T(8,128)(2,1)S(1)}, u32[]{:S(2)}, u32[]{:S(2)}) collective-permute-start(bf16[1,128,256]{2,1,0:T(8,128)(2,1)S(1)} %get-tuple-element.297), channel_id=1, source_target_pairs={{0,4},{4,8},{8,12},{1,5},{5,9},{9,13},{2,6},{6,10},{10,14},{3,7},{... | collective-permute-start | bytes 196616 | tf_op jit(solution)/shard_map/while/body/eval_jaxpr/ppermute | solution.py:20
  129.0 1.6 collective-permute-done.2
  131.9 3.0 %collective-permute-start.4 = (bf16[4,1,256]{2,1,0:T(2,128)(2,1)S(1)}, bf16[4,1,256]{2,1,0:T(2,128)(2,1)S(1)}, u32[]{:S(2)}, u32[]{:S(2)}) collective-permute-start(bf16[4,1,256]{2,1,0:T(2,128)(2,1)S(1)} %get-tuple-element.299), channel_id=1, source_target_pairs={{0,1},{2,3},{4,5},{6,7},{8,9},{10,11},{12,13},{14,15},{16,17},{18,... | collective-permute-start | bytes 6152 | tf_op jit(solution)/shard_map/while/body/eval_jaxpr/ppermute | solution.py:20
  135.8 2.6 %conditional.2 = ((bf16[2,128,128]{2,1,0:T(8,128)(2,1)S(1)}, f32[2,128,128]{2,1,0:T(8,128)S(1)})) conditional(s32[]{:T(128)} %convert_element_type.13, (bf16[2,128,128]{2,1,0:T(8,128)(2,1)S(1)}, f32[2,128,128]{2,1,0:T(8,128)S(1)}) %tuple.52, (bf16[4,130,256]{2,1,0:T(8,128)(2,1)S(1)}, bf16[4,128,256]{2,1,0:T(8,128)(2,1)S(1)}, ...), branch_computations={%region_1.1_spmd, %region_2.2_spmd} | conditional | flops 604569600 | bytes 16713764 | solution.py:70
  136.1 1.4 copy-done.2
  139.9 4.9 %collective-permute-done = bf16[2,128,128]{2,1,0:T(8,128)(2,1)S(1)} collective-permute-done((bf16[2,128,128]{2,1,0:T(8,128)(2,1)S(1)}, bf16[2,128,128]{2,1,0:T(8,128)(2,1)S(1)}, u32[]{:S(2)}, u32[]{:S(2)}) %collective-permute-start) | collective-permute-done | bytes 65568 | tf_op jit(solution)/shard_map/while/body/eval_jaxpr/ppermute | solution.py:12
  146.9 4.9 %collective-permute-start.2 = (bf16[1,128,256]{2,1,0:T(8,128)(2,1)S(1)}, bf16[1,128,256]{2,1,0:T(8,128)(2,1)S(1)}, u32[]{:S(2)}, u32[]{:S(2)}) collective-permute-start(bf16[1,128,256]{2,1,0:T(8,128)(2,1)S(1)} %get-tuple-element.297), channel_id=1, source_target_pairs={{0,4},{4,8},{8,12},{1,5},{5,9},{9,13},{2,6},{6,10},{10,14},{3,7},{... | collective-permute-start | bytes 196616 | tf_op jit(solution)/shard_map/while/body/eval_jaxpr/ppermute | solution.py:20
  152.1 1.6 collective-permute-done.2
  155.1 3.0 %collective-permute-start.4 = (bf16[4,1,256]{2,1,0:T(2,128)(2,1)S(1)}, bf16[4,1,256]{2,1,0:T(2,128)(2,1)S(1)}, u32[]{:S(2)}, u32[]{:S(2)}) collective-permute-start(bf16[4,1,256]{2,1,0:T(2,128)(2,1)S(1)} %get-tuple-element.299), channel_id=1, source_target_pairs={{0,1},{2,3},{4,5},{6,7},{8,9},{10,11},{12,13},{14,15},{16,17},{18,... | collective-permute-start | bytes 6152 | tf_op jit(solution)/shard_map/while/body/eval_jaxpr/ppermute | solution.py:20
  159.0 2.6 %conditional.2 = ((bf16[2,128,128]{2,1,0:T(8,128)(2,1)S(1)}, f32[2,128,128]{2,1,0:T(8,128)S(1)})) conditional(s32[]{:T(128)} %convert_element_type.13, (bf16[2,128,128]{2,1,0:T(8,128)(2,1)S(1)}, f32[2,128,128]{2,1,0:T(8,128)S(1)}) %tuple.52, (bf16[4,130,256]{2,1,0:T(8,128)(2,1)S(1)}, bf16[4,128,256]{2,1,0:T(8,128)(2,1)S(1)}, ...), branch_computations={%region_1.1_spmd, %region_2.2_spmd} | conditional | flops 604569600 | bytes 16713764 | solution.py:70
  159.3 1.4 copy-done.2
  163.0 4.9 %collective-permute-done = bf16[2,128,128]{2,1,0:T(8,128)(2,1)S(1)} collective-permute-done((bf16[2,128,128]{2,1,0:T(8,128)(2,1)S(1)}, bf16[2,128,128]{2,1,0:T(8,128)(2,1)S(1)}, u32[]{:S(2)}, u32[]{:S(2)}) %collective-permute-start) | collective-permute-done | bytes 65568 | tf_op jit(solution)/shard_map/while/body/eval_jaxpr/ppermute | solution.py:12
  168.8 1.3 collective-permute-start.1
  170.1 4.9 %collective-permute-start.2 = (bf16[1,128,256]{2,1,0:T(8,128)(2,1)S(1)}, bf16[1,128,256]{2,1,0:T(8,128)(2,1)S(1)}, u32[]{:S(2)}, u32[]{:S(2)}) collective-permute-start(bf16[1,128,256]{2,1,0:T(8,128)(2,1)S(1)} %get-tuple-element.297), channel_id=1, source_target_pairs={{0,4},{4,8},{8,12},{1,5},{5,9},{9,13},{2,6},{6,10},{10,14},{3,7},{... | collective-permute-start | bytes 196616 | tf_op jit(solution)/shard_map/while/body/eval_jaxpr/ppermute | solution.py:20
  175.3 1.6 collective-permute-done.2
  177.0 1.3 collective-permute-start.3
  178.3 3.0 %collective-permute-start.4 = (bf16[4,1,256]{2,1,0:T(2,128)(2,1)S(1)}, bf16[4,1,256]{2,1,0:T(2,128)(2,1)S(1)}, u32[]{:S(2)}, u32[]{:S(2)}) collective-permute-start(bf16[4,1,256]{2,1,0:T(2,128)(2,1)S(1)} %get-tuple-element.299), channel_id=1, source_target_pairs={{0,1},{2,3},{4,5},{6,7},{8,9},{10,11},{12,13},{14,15},{16,17},{18,... | collective-permute-start | bytes 6152 | tf_op jit(solution)/shard_map/while/body/eval_jaxpr/ppermute | solution.py:20
  182.2 2.6 %conditional.2 = ((bf16[2,128,128]{2,1,0:T(8,128)(2,1)S(1)}, f32[2,128,128]{2,1,0:T(8,128)S(1)})) conditional(s32[]{:T(128)} %convert_element_type.13, (bf16[2,128,128]{2,1,0:T(8,128)(2,1)S(1)}, f32[2,128,128]{2,1,0:T(8,128)S(1)}) %tuple.52, (bf16[4,130,256]{2,1,0:T(8,128)(2,1)S(1)}, bf16[4,128,256]{2,1,0:T(8,128)(2,1)S(1)}, ...), branch_computations={%region_1.1_spmd, %region_2.2_spmd} | conditional | flops 604569600 | bytes 16713764 | solution.py:70
  182.5 1.4 copy-done.2
  184.9 1.3 collective-permute-start
  186.2 4.9 %collective-permute-done = bf16[2,128,128]{2,1,0:T(8,128)(2,1)S(1)} collective-permute-done((bf16[2,128,128]{2,1,0:T(8,128)(2,1)S(1)}, bf16[2,128,128]{2,1,0:T(8,128)(2,1)S(1)}, u32[]{:S(2)}, u32[]{:S(2)}) %collective-permute-start) | collective-permute-done | bytes 65568 | tf_op jit(solution)/shard_map/while/body/eval_jaxpr/ppermute | solution.py:12
  193.3 4.9 %collective-permute-start.2 = (bf16[1,128,256]{2,1,0:T(8,128)(2,1)S(1)}, bf16[1,128,256]{2,1,0:T(8,128)(2,1)S(1)}, u32[]{:S(2)}, u32[]{:S(2)}) collective-permute-start(bf16[1,128,256]{2,1,0:T(8,128)(2,1)S(1)} %get-tuple-element.297), channel_id=1, source_target_pairs={{0,4},{4,8},{8,12},{1,5},{5,9},{9,13},{2,6},{6,10},{10,14},{3,7},{... | collective-permute-start | bytes 196616 | tf_op jit(solution)/shard_map/while/body/eval_jaxpr/ppermute | solution.py:20
  198.5 1.6 collective-permute-done.2
  201.4 3.0 %collective-permute-start.4 = (bf16[4,1,256]{2,1,0:T(2,128)(2,1)S(1)}, bf16[4,1,256]{2,1,0:T(2,128)(2,1)S(1)}, u32[]{:S(2)}, u32[]{:S(2)}) collective-permute-start(bf16[4,1,256]{2,1,0:T(2,128)(2,1)S(1)} %get-tuple-element.299), channel_id=1, source_target_pairs={{0,1},{2,3},{4,5},{6,7},{8,9},{10,11},{12,13},{14,15},{16,17},{18,... | collective-permute-start | bytes 6152 | tf_op jit(solution)/shard_map/while/body/eval_jaxpr/ppermute | solution.py:20
  205.4 2.6 %conditional.2 = ((bf16[2,128,128]{2,1,0:T(8,128)(2,1)S(1)}, f32[2,128,128]{2,1,0:T(8,128)S(1)})) conditional(s32[]{:T(128)} %convert_element_type.13, (bf16[2,128,128]{2,1,0:T(8,128)(2,1)S(1)}, f32[2,128,128]{2,1,0:T(8,128)S(1)}) %tuple.52, (bf16[4,130,256]{2,1,0:T(8,128)(2,1)S(1)}, bf16[4,128,256]{2,1,0:T(8,128)(2,1)S(1)}, ...), branch_computations={%region_1.1_spmd, %region_2.2_spmd} | conditional | flops 604569600 | bytes 16713764 | solution.py:70
  205.6 1.4 copy-done.2
  (237 shorter events, 51.2 us)
Async XLA Ops:
  2.5 20.1 %copy-start.3 = (f32[1,512]{1,0:T(1,128)S(1)}, f32[1,512]{1,0:T(1,128)}, u32[]{:S(2)}) copy-start(f32[1,512]{1,0:T(1,128)} %get-tuple-element.340) | copy-start | bytes 6148 | tf_op jit(solution)/shard_map/while
  2.5 6.2 %collective-permute-start = (bf16[2,128,128]{2,1,0:T(8,128)(2,1)S(1)}, bf16[2,128,128]{2,1,0:T(8,128)(2,1)S(1)}, u32[]{:S(2)}, u32[]{:S(2)}) collective-permute-start(bf16[2,128,128]{2,1,0:T(8,128)(2,1)S(1)} %get-tuple-element.320), channel_id=1, source_target_pairs={{0,2},{1,3},{4,6},{5,7},{8,10},{9,11},{12,14},{13,15},{16,18},{17,... | collective-permute-start | bytes 196616 | tf_op jit(solution)/shard_map/while/body/eval_jaxpr/ppermute | solution.py:12
  9.5 6.2 %collective-permute-start.1 = (bf16[1,128,256]{2,1,0:T(8,128)(2,1)S(1)}, bf16[1,128,256]{2,1,0:T(8,128)(2,1)S(1)}, u32[]{:S(2)}, u32[]{:S(2)}) collective-permute-start(bf16[1,128,256]{2,1,0:T(8,128)(2,1)S(1)} %get-tuple-element.296), channel_id=1, source_target_pairs={{4,0},{8,4},{12,8},{5,1},{9,5},{13,9},{6,2},{10,6},{14,10},{7,3},{... | collective-permute-start | bytes 196616 | tf_op jit(solution)/shard_map/while/body/eval_jaxpr/ppermute | solution.py:23
  10.8 6.4 %collective-permute-start.2 = (bf16[1,128,256]{2,1,0:T(8,128)(2,1)S(1)}, bf16[1,128,256]{2,1,0:T(8,128)(2,1)S(1)}, u32[]{:S(2)}, u32[]{:S(2)}) collective-permute-start(bf16[1,128,256]{2,1,0:T(8,128)(2,1)S(1)} %get-tuple-element.297), channel_id=1, source_target_pairs={{0,4},{4,8},{8,12},{1,5},{5,9},{9,13},{2,6},{6,10},{10,14},{3,7},{... | collective-permute-start | bytes 196616 | tf_op jit(solution)/shard_map/while/body/eval_jaxpr/ppermute | solution.py:20
  17.3 4.4 %collective-permute-start.3 = (bf16[4,1,256]{2,1,0:T(2,128)(2,1)S(1)}, bf16[4,1,256]{2,1,0:T(2,128)(2,1)S(1)}, u32[]{:S(2)}, u32[]{:S(2)}) collective-permute-start(bf16[4,1,256]{2,1,0:T(2,128)(2,1)S(1)} %get-tuple-element.298), channel_id=1, source_target_pairs={{1,0},{3,2},{5,4},{7,6},{9,8},{11,10},{13,12},{15,14},{17,16},{19,... | collective-permute-start | bytes 6152 | tf_op jit(solution)/shard_map/while/body/eval_jaxpr/ppermute | solution.py:23
  18.6 3.8 %collective-permute-start.4 = (bf16[4,1,256]{2,1,0:T(2,128)(2,1)S(1)}, bf16[4,1,256]{2,1,0:T(2,128)(2,1)S(1)}, u32[]{:S(2)}, u32[]{:S(2)}) collective-permute-start(bf16[4,1,256]{2,1,0:T(2,128)(2,1)S(1)} %get-tuple-element.299), channel_id=1, source_target_pairs={{0,1},{2,3},{4,5},{6,7},{8,9},{10,11},{12,13},{14,15},{16,17},{18,... | collective-permute-start | bytes 6152 | tf_op jit(solution)/shard_map/while/body/eval_jaxpr/ppermute | solution.py:20
  22.6 20.5 %copy-start.3 = (f32[1,512]{1,0:T(1,128)S(1)}, f32[1,512]{1,0:T(1,128)}, u32[]{:S(2)}) copy-start(f32[1,512]{1,0:T(1,128)} %get-tuple-element.340) | copy-start | bytes 6148 | tf_op jit(solution)/shard_map/while
  22.7 6.2 %collective-permute-start = (bf16[2,128,128]{2,1,0:T(8,128)(2,1)S(1)}, bf16[2,128,128]{2,1,0:T(8,128)(2,1)S(1)}, u32[]{:S(2)}, u32[]{:S(2)}) collective-permute-start(bf16[2,128,128]{2,1,0:T(8,128)(2,1)S(1)} %get-tuple-element.320), channel_id=1, source_target_pairs={{0,2},{1,3},{4,6},{5,7},{8,10},{9,11},{12,14},{13,15},{16,18},{17,... | collective-permute-start | bytes 196616 | tf_op jit(solution)/shard_map/while/body/eval_jaxpr/ppermute | solution.py:12
  29.8 6.5 %collective-permute-start.1 = (bf16[1,128,256]{2,1,0:T(8,128)(2,1)S(1)}, bf16[1,128,256]{2,1,0:T(8,128)(2,1)S(1)}, u32[]{:S(2)}, u32[]{:S(2)}) collective-permute-start(bf16[1,128,256]{2,1,0:T(8,128)(2,1)S(1)} %get-tuple-element.296), channel_id=1, source_target_pairs={{4,0},{8,4},{12,8},{5,1},{9,5},{13,9},{6,2},{10,6},{14,10},{7,3},{... | collective-permute-start | bytes 196616 | tf_op jit(solution)/shard_map/while/body/eval_jaxpr/ppermute | solution.py:23
  31.1 6.8 %collective-permute-start.2 = (bf16[1,128,256]{2,1,0:T(8,128)(2,1)S(1)}, bf16[1,128,256]{2,1,0:T(8,128)(2,1)S(1)}, u32[]{:S(2)}, u32[]{:S(2)}) collective-permute-start(bf16[1,128,256]{2,1,0:T(8,128)(2,1)S(1)} %get-tuple-element.297), channel_id=1, source_target_pairs={{0,4},{4,8},{8,12},{1,5},{5,9},{9,13},{2,6},{6,10},{10,14},{3,7},{... | collective-permute-start | bytes 196616 | tf_op jit(solution)/shard_map/while/body/eval_jaxpr/ppermute | solution.py:20
  37.9 4.4 %collective-permute-start.3 = (bf16[4,1,256]{2,1,0:T(2,128)(2,1)S(1)}, bf16[4,1,256]{2,1,0:T(2,128)(2,1)S(1)}, u32[]{:S(2)}, u32[]{:S(2)}) collective-permute-start(bf16[4,1,256]{2,1,0:T(2,128)(2,1)S(1)} %get-tuple-element.298), channel_id=1, source_target_pairs={{1,0},{3,2},{5,4},{7,6},{9,8},{11,10},{13,12},{15,14},{17,16},{19,... | collective-permute-start | bytes 6152 | tf_op jit(solution)/shard_map/while/body/eval_jaxpr/ppermute | solution.py:23
  39.2 3.8 %collective-permute-start.4 = (bf16[4,1,256]{2,1,0:T(2,128)(2,1)S(1)}, bf16[4,1,256]{2,1,0:T(2,128)(2,1)S(1)}, u32[]{:S(2)}, u32[]{:S(2)}) collective-permute-start(bf16[4,1,256]{2,1,0:T(2,128)(2,1)S(1)} %get-tuple-element.299), channel_id=1, source_target_pairs={{0,1},{2,3},{4,5},{6,7},{8,9},{10,11},{12,13},{14,15},{16,17},{18,... | collective-permute-start | bytes 6152 | tf_op jit(solution)/shard_map/while/body/eval_jaxpr/ppermute | solution.py:20
  43.2 1.7 copy-start.2
  45.8 20.5 %copy-start.3 = (f32[1,512]{1,0:T(1,128)S(1)}, f32[1,512]{1,0:T(1,128)}, u32[]{:S(2)}) copy-start(f32[1,512]{1,0:T(1,128)} %get-tuple-element.340) | copy-start | bytes 6148 | tf_op jit(solution)/shard_map/while
  45.8 6.2 %collective-permute-start = (bf16[2,128,128]{2,1,0:T(8,128)(2,1)S(1)}, bf16[2,128,128]{2,1,0:T(8,128)(2,1)S(1)}, u32[]{:S(2)}, u32[]{:S(2)}) collective-permute-start(bf16[2,128,128]{2,1,0:T(8,128)(2,1)S(1)} %get-tuple-element.320), channel_id=1, source_target_pairs={{0,2},{1,3},{4,6},{5,7},{8,10},{9,11},{12,14},{13,15},{16,18},{17,... | collective-permute-start | bytes 196616 | tf_op jit(solution)/shard_map/while/body/eval_jaxpr/ppermute | solution.py:12
  52.9 6.5 %collective-permute-start.1 = (bf16[1,128,256]{2,1,0:T(8,128)(2,1)S(1)}, bf16[1,128,256]{2,1,0:T(8,128)(2,1)S(1)}, u32[]{:S(2)}, u32[]{:S(2)}) collective-permute-start(bf16[1,128,256]{2,1,0:T(8,128)(2,1)S(1)} %get-tuple-element.296), channel_id=1, source_target_pairs={{4,0},{8,4},{12,8},{5,1},{9,5},{13,9},{6,2},{10,6},{14,10},{7,3},{... | collective-permute-start | bytes 196616 | tf_op jit(solution)/shard_map/while/body/eval_jaxpr/ppermute | solution.py:23
  54.2 6.8 %collective-permute-start.2 = (bf16[1,128,256]{2,1,0:T(8,128)(2,1)S(1)}, bf16[1,128,256]{2,1,0:T(8,128)(2,1)S(1)}, u32[]{:S(2)}, u32[]{:S(2)}) collective-permute-start(bf16[1,128,256]{2,1,0:T(8,128)(2,1)S(1)} %get-tuple-element.297), channel_id=1, source_target_pairs={{0,4},{4,8},{8,12},{1,5},{5,9},{9,13},{2,6},{6,10},{10,14},{3,7},{... | collective-permute-start | bytes 196616 | tf_op jit(solution)/shard_map/while/body/eval_jaxpr/ppermute | solution.py:20
  61.1 4.4 %collective-permute-start.3 = (bf16[4,1,256]{2,1,0:T(2,128)(2,1)S(1)}, bf16[4,1,256]{2,1,0:T(2,128)(2,1)S(1)}, u32[]{:S(2)}, u32[]{:S(2)}) collective-permute-start(bf16[4,1,256]{2,1,0:T(2,128)(2,1)S(1)} %get-tuple-element.298), channel_id=1, source_target_pairs={{1,0},{3,2},{5,4},{7,6},{9,8},{11,10},{13,12},{15,14},{17,16},{19,... | collective-permute-start | bytes 6152 | tf_op jit(solution)/shard_map/while/body/eval_jaxpr/ppermute | solution.py:23
  62.4 3.8 %collective-permute-start.4 = (bf16[4,1,256]{2,1,0:T(2,128)(2,1)S(1)}, bf16[4,1,256]{2,1,0:T(2,128)(2,1)S(1)}, u32[]{:S(2)}, u32[]{:S(2)}) collective-permute-start(bf16[4,1,256]{2,1,0:T(2,128)(2,1)S(1)} %get-tuple-element.299), channel_id=1, source_target_pairs={{0,1},{2,3},{4,5},{6,7},{8,9},{10,11},{12,13},{14,15},{16,17},{18,... | collective-permute-start | bytes 6152 | tf_op jit(solution)/shard_map/while/body/eval_jaxpr/ppermute | solution.py:20
  66.3 1.7 copy-start.2
  69.0 20.5 %copy-start.3 = (f32[1,512]{1,0:T(1,128)S(1)}, f32[1,512]{1,0:T(1,128)}, u32[]{:S(2)}) copy-start(f32[1,512]{1,0:T(1,128)} %get-tuple-element.340) | copy-start | bytes 6148 | tf_op jit(solution)/shard_map/while
  69.0 6.2 %collective-permute-start = (bf16[2,128,128]{2,1,0:T(8,128)(2,1)S(1)}, bf16[2,128,128]{2,1,0:T(8,128)(2,1)S(1)}, u32[]{:S(2)}, u32[]{:S(2)}) collective-permute-start(bf16[2,128,128]{2,1,0:T(8,128)(2,1)S(1)} %get-tuple-element.320), channel_id=1, source_target_pairs={{0,2},{1,3},{4,6},{5,7},{8,10},{9,11},{12,14},{13,15},{16,18},{17,... | collective-permute-start | bytes 196616 | tf_op jit(solution)/shard_map/while/body/eval_jaxpr/ppermute | solution.py:12
  76.1 6.5 %collective-permute-start.1 = (bf16[1,128,256]{2,1,0:T(8,128)(2,1)S(1)}, bf16[1,128,256]{2,1,0:T(8,128)(2,1)S(1)}, u32[]{:S(2)}, u32[]{:S(2)}) collective-permute-start(bf16[1,128,256]{2,1,0:T(8,128)(2,1)S(1)} %get-tuple-element.296), channel_id=1, source_target_pairs={{4,0},{8,4},{12,8},{5,1},{9,5},{13,9},{6,2},{10,6},{14,10},{7,3},{... | collective-permute-start | bytes 196616 | tf_op jit(solution)/shard_map/while/body/eval_jaxpr/ppermute | solution.py:23
  77.4 6.8 %collective-permute-start.2 = (bf16[1,128,256]{2,1,0:T(8,128)(2,1)S(1)}, bf16[1,128,256]{2,1,0:T(8,128)(2,1)S(1)}, u32[]{:S(2)}, u32[]{:S(2)}) collective-permute-start(bf16[1,128,256]{2,1,0:T(8,128)(2,1)S(1)} %get-tuple-element.297), channel_id=1, source_target_pairs={{0,4},{4,8},{8,12},{1,5},{5,9},{9,13},{2,6},{6,10},{10,14},{3,7},{... | collective-permute-start | bytes 196616 | tf_op jit(solution)/shard_map/while/body/eval_jaxpr/ppermute | solution.py:20
  84.2 4.4 %collective-permute-start.3 = (bf16[4,1,256]{2,1,0:T(2,128)(2,1)S(1)}, bf16[4,1,256]{2,1,0:T(2,128)(2,1)S(1)}, u32[]{:S(2)}, u32[]{:S(2)}) collective-permute-start(bf16[4,1,256]{2,1,0:T(2,128)(2,1)S(1)} %get-tuple-element.298), channel_id=1, source_target_pairs={{1,0},{3,2},{5,4},{7,6},{9,8},{11,10},{13,12},{15,14},{17,16},{19,... | collective-permute-start | bytes 6152 | tf_op jit(solution)/shard_map/while/body/eval_jaxpr/ppermute | solution.py:23
  85.5 3.8 %collective-permute-start.4 = (bf16[4,1,256]{2,1,0:T(2,128)(2,1)S(1)}, bf16[4,1,256]{2,1,0:T(2,128)(2,1)S(1)}, u32[]{:S(2)}, u32[]{:S(2)}) collective-permute-start(bf16[4,1,256]{2,1,0:T(2,128)(2,1)S(1)} %get-tuple-element.299), channel_id=1, source_target_pairs={{0,1},{2,3},{4,5},{6,7},{8,9},{10,11},{12,13},{14,15},{16,17},{18,... | collective-permute-start | bytes 6152 | tf_op jit(solution)/shard_map/while/body/eval_jaxpr/ppermute | solution.py:20
  89.5 1.7 copy-start.2
  92.2 20.5 %copy-start.3 = (f32[1,512]{1,0:T(1,128)S(1)}, f32[1,512]{1,0:T(1,128)}, u32[]{:S(2)}) copy-start(f32[1,512]{1,0:T(1,128)} %get-tuple-element.340) | copy-start | bytes 6148 | tf_op jit(solution)/shard_map/while
  92.2 6.2 %collective-permute-start = (bf16[2,128,128]{2,1,0:T(8,128)(2,1)S(1)}, bf16[2,128,128]{2,1,0:T(8,128)(2,1)S(1)}, u32[]{:S(2)}, u32[]{:S(2)}) collective-permute-start(bf16[2,128,128]{2,1,0:T(8,128)(2,1)S(1)} %get-tuple-element.320), channel_id=1, source_target_pairs={{0,2},{1,3},{4,6},{5,7},{8,10},{9,11},{12,14},{13,15},{16,18},{17,... | collective-permute-start | bytes 196616 | tf_op jit(solution)/shard_map/while/body/eval_jaxpr/ppermute | solution.py:12
  99.3 6.5 %collective-permute-start.1 = (bf16[1,128,256]{2,1,0:T(8,128)(2,1)S(1)}, bf16[1,128,256]{2,1,0:T(8,128)(2,1)S(1)}, u32[]{:S(2)}, u32[]{:S(2)}) collective-permute-start(bf16[1,128,256]{2,1,0:T(8,128)(2,1)S(1)} %get-tuple-element.296), channel_id=1, source_target_pairs={{4,0},{8,4},{12,8},{5,1},{9,5},{13,9},{6,2},{10,6},{14,10},{7,3},{... | collective-permute-start | bytes 196616 | tf_op jit(solution)/shard_map/while/body/eval_jaxpr/ppermute | solution.py:23
  100.6 6.8 %collective-permute-start.2 = (bf16[1,128,256]{2,1,0:T(8,128)(2,1)S(1)}, bf16[1,128,256]{2,1,0:T(8,128)(2,1)S(1)}, u32[]{:S(2)}, u32[]{:S(2)}) collective-permute-start(bf16[1,128,256]{2,1,0:T(8,128)(2,1)S(1)} %get-tuple-element.297), channel_id=1, source_target_pairs={{0,4},{4,8},{8,12},{1,5},{5,9},{9,13},{2,6},{6,10},{10,14},{3,7},{... | collective-permute-start | bytes 196616 | tf_op jit(solution)/shard_map/while/body/eval_jaxpr/ppermute | solution.py:20
  107.4 4.4 %collective-permute-start.3 = (bf16[4,1,256]{2,1,0:T(2,128)(2,1)S(1)}, bf16[4,1,256]{2,1,0:T(2,128)(2,1)S(1)}, u32[]{:S(2)}, u32[]{:S(2)}) collective-permute-start(bf16[4,1,256]{2,1,0:T(2,128)(2,1)S(1)} %get-tuple-element.298), channel_id=1, source_target_pairs={{1,0},{3,2},{5,4},{7,6},{9,8},{11,10},{13,12},{15,14},{17,16},{19,... | collective-permute-start | bytes 6152 | tf_op jit(solution)/shard_map/while/body/eval_jaxpr/ppermute | solution.py:23
  108.7 3.8 %collective-permute-start.4 = (bf16[4,1,256]{2,1,0:T(2,128)(2,1)S(1)}, bf16[4,1,256]{2,1,0:T(2,128)(2,1)S(1)}, u32[]{:S(2)}, u32[]{:S(2)}) collective-permute-start(bf16[4,1,256]{2,1,0:T(2,128)(2,1)S(1)} %get-tuple-element.299), channel_id=1, source_target_pairs={{0,1},{2,3},{4,5},{6,7},{8,9},{10,11},{12,13},{14,15},{16,17},{18,... | collective-permute-start | bytes 6152 | tf_op jit(solution)/shard_map/while/body/eval_jaxpr/ppermute | solution.py:20
  112.7 1.7 copy-start.2
  115.3 20.5 %copy-start.3 = (f32[1,512]{1,0:T(1,128)S(1)}, f32[1,512]{1,0:T(1,128)}, u32[]{:S(2)}) copy-start(f32[1,512]{1,0:T(1,128)} %get-tuple-element.340) | copy-start | bytes 6148 | tf_op jit(solution)/shard_map/while
  115.4 6.2 %collective-permute-start = (bf16[2,128,128]{2,1,0:T(8,128)(2,1)S(1)}, bf16[2,128,128]{2,1,0:T(8,128)(2,1)S(1)}, u32[]{:S(2)}, u32[]{:S(2)}) collective-permute-start(bf16[2,128,128]{2,1,0:T(8,128)(2,1)S(1)} %get-tuple-element.320), channel_id=1, source_target_pairs={{0,2},{1,3},{4,6},{5,7},{8,10},{9,11},{12,14},{13,15},{16,18},{17,... | collective-permute-start | bytes 196616 | tf_op jit(solution)/shard_map/while/body/eval_jaxpr/ppermute | solution.py:12
  122.5 6.5 %collective-permute-start.1 = (bf16[1,128,256]{2,1,0:T(8,128)(2,1)S(1)}, bf16[1,128,256]{2,1,0:T(8,128)(2,1)S(1)}, u32[]{:S(2)}, u32[]{:S(2)}) collective-permute-start(bf16[1,128,256]{2,1,0:T(8,128)(2,1)S(1)} %get-tuple-element.296), channel_id=1, source_target_pairs={{4,0},{8,4},{12,8},{5,1},{9,5},{13,9},{6,2},{10,6},{14,10},{7,3},{... | collective-permute-start | bytes 196616 | tf_op jit(solution)/shard_map/while/body/eval_jaxpr/ppermute | solution.py:23
  123.8 6.8 %collective-permute-start.2 = (bf16[1,128,256]{2,1,0:T(8,128)(2,1)S(1)}, bf16[1,128,256]{2,1,0:T(8,128)(2,1)S(1)}, u32[]{:S(2)}, u32[]{:S(2)}) collective-permute-start(bf16[1,128,256]{2,1,0:T(8,128)(2,1)S(1)} %get-tuple-element.297), channel_id=1, source_target_pairs={{0,4},{4,8},{8,12},{1,5},{5,9},{9,13},{2,6},{6,10},{10,14},{3,7},{... | collective-permute-start | bytes 196616 | tf_op jit(solution)/shard_map/while/body/eval_jaxpr/ppermute | solution.py:20
  130.6 4.4 %collective-permute-start.3 = (bf16[4,1,256]{2,1,0:T(2,128)(2,1)S(1)}, bf16[4,1,256]{2,1,0:T(2,128)(2,1)S(1)}, u32[]{:S(2)}, u32[]{:S(2)}) collective-permute-start(bf16[4,1,256]{2,1,0:T(2,128)(2,1)S(1)} %get-tuple-element.298), channel_id=1, source_target_pairs={{1,0},{3,2},{5,4},{7,6},{9,8},{11,10},{13,12},{15,14},{17,16},{19,... | collective-permute-start | bytes 6152 | tf_op jit(solution)/shard_map/while/body/eval_jaxpr/ppermute | solution.py:23
  131.9 3.8 %collective-permute-start.4 = (bf16[4,1,256]{2,1,0:T(2,128)(2,1)S(1)}, bf16[4,1,256]{2,1,0:T(2,128)(2,1)S(1)}, u32[]{:S(2)}, u32[]{:S(2)}) collective-permute-start(bf16[4,1,256]{2,1,0:T(2,128)(2,1)S(1)} %get-tuple-element.299), channel_id=1, source_target_pairs={{0,1},{2,3},{4,5},{6,7},{8,9},{10,11},{12,13},{14,15},{16,17},{18,... | collective-permute-start | bytes 6152 | tf_op jit(solution)/shard_map/while/body/eval_jaxpr/ppermute | solution.py:20
  135.9 1.7 copy-start.2
  138.5 20.5 %copy-start.3 = (f32[1,512]{1,0:T(1,128)S(1)}, f32[1,512]{1,0:T(1,128)}, u32[]{:S(2)}) copy-start(f32[1,512]{1,0:T(1,128)} %get-tuple-element.340) | copy-start | bytes 6148 | tf_op jit(solution)/shard_map/while
  138.5 6.2 %collective-permute-start = (bf16[2,128,128]{2,1,0:T(8,128)(2,1)S(1)}, bf16[2,128,128]{2,1,0:T(8,128)(2,1)S(1)}, u32[]{:S(2)}, u32[]{:S(2)}) collective-permute-start(bf16[2,128,128]{2,1,0:T(8,128)(2,1)S(1)} %get-tuple-element.320), channel_id=1, source_target_pairs={{0,2},{1,3},{4,6},{5,7},{8,10},{9,11},{12,14},{13,15},{16,18},{17,... | collective-permute-start | bytes 196616 | tf_op jit(solution)/shard_map/while/body/eval_jaxpr/ppermute | solution.py:12
  145.6 6.5 %collective-permute-start.1 = (bf16[1,128,256]{2,1,0:T(8,128)(2,1)S(1)}, bf16[1,128,256]{2,1,0:T(8,128)(2,1)S(1)}, u32[]{:S(2)}, u32[]{:S(2)}) collective-permute-start(bf16[1,128,256]{2,1,0:T(8,128)(2,1)S(1)} %get-tuple-element.296), channel_id=1, source_target_pairs={{4,0},{8,4},{12,8},{5,1},{9,5},{13,9},{6,2},{10,6},{14,10},{7,3},{... | collective-permute-start | bytes 196616 | tf_op jit(solution)/shard_map/while/body/eval_jaxpr/ppermute | solution.py:23
  146.9 6.8 %collective-permute-start.2 = (bf16[1,128,256]{2,1,0:T(8,128)(2,1)S(1)}, bf16[1,128,256]{2,1,0:T(8,128)(2,1)S(1)}, u32[]{:S(2)}, u32[]{:S(2)}) collective-permute-start(bf16[1,128,256]{2,1,0:T(8,128)(2,1)S(1)} %get-tuple-element.297), channel_id=1, source_target_pairs={{0,4},{4,8},{8,12},{1,5},{5,9},{9,13},{2,6},{6,10},{10,14},{3,7},{... | collective-permute-start | bytes 196616 | tf_op jit(solution)/shard_map/while/body/eval_jaxpr/ppermute | solution.py:20
  153.8 4.4 %collective-permute-start.3 = (bf16[4,1,256]{2,1,0:T(2,128)(2,1)S(1)}, bf16[4,1,256]{2,1,0:T(2,128)(2,1)S(1)}, u32[]{:S(2)}, u32[]{:S(2)}) collective-permute-start(bf16[4,1,256]{2,1,0:T(2,128)(2,1)S(1)} %get-tuple-element.298), channel_id=1, source_target_pairs={{1,0},{3,2},{5,4},{7,6},{9,8},{11,10},{13,12},{15,14},{17,16},{19,... | collective-permute-start | bytes 6152 | tf_op jit(solution)/shard_map/while/body/eval_jaxpr/ppermute | solution.py:23
  155.1 3.8 %collective-permute-start.4 = (bf16[4,1,256]{2,1,0:T(2,128)(2,1)S(1)}, bf16[4,1,256]{2,1,0:T(2,128)(2,1)S(1)}, u32[]{:S(2)}, u32[]{:S(2)}) collective-permute-start(bf16[4,1,256]{2,1,0:T(2,128)(2,1)S(1)} %get-tuple-element.299), channel_id=1, source_target_pairs={{0,1},{2,3},{4,5},{6,7},{8,9},{10,11},{12,13},{14,15},{16,17},{18,... | collective-permute-start | bytes 6152 | tf_op jit(solution)/shard_map/while/body/eval_jaxpr/ppermute | solution.py:20
  159.0 1.7 copy-start.2
  161.7 20.5 %copy-start.3 = (f32[1,512]{1,0:T(1,128)S(1)}, f32[1,512]{1,0:T(1,128)}, u32[]{:S(2)}) copy-start(f32[1,512]{1,0:T(1,128)} %get-tuple-element.340) | copy-start | bytes 6148 | tf_op jit(solution)/shard_map/while
  161.7 6.2 %collective-permute-start = (bf16[2,128,128]{2,1,0:T(8,128)(2,1)S(1)}, bf16[2,128,128]{2,1,0:T(8,128)(2,1)S(1)}, u32[]{:S(2)}, u32[]{:S(2)}) collective-permute-start(bf16[2,128,128]{2,1,0:T(8,128)(2,1)S(1)} %get-tuple-element.320), channel_id=1, source_target_pairs={{0,2},{1,3},{4,6},{5,7},{8,10},{9,11},{12,14},{13,15},{16,18},{17,... | collective-permute-start | bytes 196616 | tf_op jit(solution)/shard_map/while/body/eval_jaxpr/ppermute | solution.py:12
  168.8 6.5 %collective-permute-start.1 = (bf16[1,128,256]{2,1,0:T(8,128)(2,1)S(1)}, bf16[1,128,256]{2,1,0:T(8,128)(2,1)S(1)}, u32[]{:S(2)}, u32[]{:S(2)}) collective-permute-start(bf16[1,128,256]{2,1,0:T(8,128)(2,1)S(1)} %get-tuple-element.296), channel_id=1, source_target_pairs={{4,0},{8,4},{12,8},{5,1},{9,5},{13,9},{6,2},{10,6},{14,10},{7,3},{... | collective-permute-start | bytes 196616 | tf_op jit(solution)/shard_map/while/body/eval_jaxpr/ppermute | solution.py:23
  170.1 6.8 %collective-permute-start.2 = (bf16[1,128,256]{2,1,0:T(8,128)(2,1)S(1)}, bf16[1,128,256]{2,1,0:T(8,128)(2,1)S(1)}, u32[]{:S(2)}, u32[]{:S(2)}) collective-permute-start(bf16[1,128,256]{2,1,0:T(8,128)(2,1)S(1)} %get-tuple-element.297), channel_id=1, source_target_pairs={{0,4},{4,8},{8,12},{1,5},{5,9},{9,13},{2,6},{6,10},{10,14},{3,7},{... | collective-permute-start | bytes 196616 | tf_op jit(solution)/shard_map/while/body/eval_jaxpr/ppermute | solution.py:20
  177.0 4.4 %collective-permute-start.3 = (bf16[4,1,256]{2,1,0:T(2,128)(2,1)S(1)}, bf16[4,1,256]{2,1,0:T(2,128)(2,1)S(1)}, u32[]{:S(2)}, u32[]{:S(2)}) collective-permute-start(bf16[4,1,256]{2,1,0:T(2,128)(2,1)S(1)} %get-tuple-element.298), channel_id=1, source_target_pairs={{1,0},{3,2},{5,4},{7,6},{9,8},{11,10},{13,12},{15,14},{17,16},{19,... | collective-permute-start | bytes 6152 | tf_op jit(solution)/shard_map/while/body/eval_jaxpr/ppermute | solution.py:23
  178.3 3.8 %collective-permute-start.4 = (bf16[4,1,256]{2,1,0:T(2,128)(2,1)S(1)}, bf16[4,1,256]{2,1,0:T(2,128)(2,1)S(1)}, u32[]{:S(2)}, u32[]{:S(2)}) collective-permute-start(bf16[4,1,256]{2,1,0:T(2,128)(2,1)S(1)} %get-tuple-element.299), channel_id=1, source_target_pairs={{0,1},{2,3},{4,5},{6,7},{8,9},{10,11},{12,13},{14,15},{16,17},{18,... | collective-permute-start | bytes 6152 | tf_op jit(solution)/shard_map/while/body/eval_jaxpr/ppermute | solution.py:20
  182.2 1.7 copy-start.2
  184.9 20.5 %copy-start.3 = (f32[1,512]{1,0:T(1,128)S(1)}, f32[1,512]{1,0:T(1,128)}, u32[]{:S(2)}) copy-start(f32[1,512]{1,0:T(1,128)} %get-tuple-element.340) | copy-start | bytes 6148 | tf_op jit(solution)/shard_map/while
  184.9 6.2 %collective-permute-start = (bf16[2,128,128]{2,1,0:T(8,128)(2,1)S(1)}, bf16[2,128,128]{2,1,0:T(8,128)(2,1)S(1)}, u32[]{:S(2)}, u32[]{:S(2)}) collective-permute-start(bf16[2,128,128]{2,1,0:T(8,128)(2,1)S(1)} %get-tuple-element.320), channel_id=1, source_target_pairs={{0,2},{1,3},{4,6},{5,7},{8,10},{9,11},{12,14},{13,15},{16,18},{17,... | collective-permute-start | bytes 196616 | tf_op jit(solution)/shard_map/while/body/eval_jaxpr/ppermute | solution.py:12
  192.0 6.5 %collective-permute-start.1 = (bf16[1,128,256]{2,1,0:T(8,128)(2,1)S(1)}, bf16[1,128,256]{2,1,0:T(8,128)(2,1)S(1)}, u32[]{:S(2)}, u32[]{:S(2)}) collective-permute-start(bf16[1,128,256]{2,1,0:T(8,128)(2,1)S(1)} %get-tuple-element.296), channel_id=1, source_target_pairs={{4,0},{8,4},{12,8},{5,1},{9,5},{13,9},{6,2},{10,6},{14,10},{7,3},{... | collective-permute-start | bytes 196616 | tf_op jit(solution)/shard_map/while/body/eval_jaxpr/ppermute | solution.py:23
  193.3 6.8 %collective-permute-start.2 = (bf16[1,128,256]{2,1,0:T(8,128)(2,1)S(1)}, bf16[1,128,256]{2,1,0:T(8,128)(2,1)S(1)}, u32[]{:S(2)}, u32[]{:S(2)}) collective-permute-start(bf16[1,128,256]{2,1,0:T(8,128)(2,1)S(1)} %get-tuple-element.297), channel_id=1, source_target_pairs={{0,4},{4,8},{8,12},{1,5},{5,9},{9,13},{2,6},{6,10},{10,14},{3,7},{... | collective-permute-start | bytes 196616 | tf_op jit(solution)/shard_map/while/body/eval_jaxpr/ppermute | solution.py:20
  200.1 4.4 %collective-permute-start.3 = (bf16[4,1,256]{2,1,0:T(2,128)(2,1)S(1)}, bf16[4,1,256]{2,1,0:T(2,128)(2,1)S(1)}, u32[]{:S(2)}, u32[]{:S(2)}) collective-permute-start(bf16[4,1,256]{2,1,0:T(2,128)(2,1)S(1)} %get-tuple-element.298), channel_id=1, source_target_pairs={{1,0},{3,2},{5,4},{7,6},{9,8},{11,10},{13,12},{15,14},{17,16},{19,... | collective-permute-start | bytes 6152 | tf_op jit(solution)/shard_map/while/body/eval_jaxpr/ppermute | solution.py:23
  201.4 3.8 %collective-permute-start.4 = (bf16[4,1,256]{2,1,0:T(2,128)(2,1)S(1)}, bf16[4,1,256]{2,1,0:T(2,128)(2,1)S(1)}, u32[]{:S(2)}, u32[]{:S(2)}) collective-permute-start(bf16[4,1,256]{2,1,0:T(2,128)(2,1)S(1)} %get-tuple-element.299), channel_id=1, source_target_pairs={{0,1},{2,3},{4,5},{6,7},{8,9},{10,11},{12,13},{14,15},{16,17},{18,... | collective-permute-start | bytes 6152 | tf_op jit(solution)/shard_map/while/body/eval_jaxpr/ppermute | solution.py:20
  205.4 1.7 copy-start.2
  208.1 0.7 copy-start
  208.1 0.8 copy-start.1
where the time goes:
time: 213 us; the launch traced here: 209 us
  starting transfers between devices  106 us (50%)
  waiting for transfers between devices  67.9 us (32%)
  local copies, waits for them, and re-layouts  15.7 us (7%)
  other arithmetic  10.6 us (5%)
  matrix products  6.15 us (3%)
    ppermute x18, starting transfers between devices, padded_2(): lax.ppermute(lax.slice_in_dim(block, block.shape[dim] - width, None, axis...  71 us
    ppermute x9, waiting for transfers between devices, from_behind(): return lax.ppermute(block, axis, route)  44.2 us
    ppermute x18, starting transfers between devices, padded_2(): lax.ppermute(lax.slice_in_dim(block, 0, width, axis=dim), axis, backward)  23.3 us
    ppermute x18, waiting for transfers between devices, padded_2(): lax.ppermute(lax.slice_in_dim(block, block.shape[dim] - width, None, axis...  21.2 us
    cond x80, local copies, waits for them, and re-layouts  12.4 us
    ppermute x9, starting transfers between devices, from_behind(): return lax.ppermute(block, axis, route)  11.6 us
    select_n x9, other arithmetic, section(): x_map = jnp.where(layer_idx == 0, own_input, incoming)  7.64 us
    dot_general x8, matrix products, gate_values(): total = jnp.dot(slab, weights, preferred_element_type=jnp.float32)  6.15 us
  transfers between devices with their start and end apart: 45, of which 36 were waited for; matrix products, arithmetic and copies ran while one was open for 0% of the time, Pallas kernels for 0%

commit v1 on v0

v1 whole, which is shorter than its diff:
```python
import functools

import jax
import jax.numpy as jnp
from jax import lax
from jax.experimental import pallas as pl
from jax.experimental.pallas import tpu as pltpu
from jax.sharding import PartitionSpec as P

BF = jnp.bfloat16
F32 = jnp.float32


def round_up(value, unit):
    return -(-value // unit) * unit


def partner(index, hop, count):
    if count & (count - 1) == 0:
        return index ^ hop, index ^ hop
    return (index + hop) % count, (index + count - hop) % count


def sigmoid(value):
    return 0.5 * jnp.tanh(0.5 * value) + 0.5


def step_kernel(dims, step, first_layer, *refs):
    rows_n, band, width, wide, chans, steps, count, phase = dims
    place, refs = refs[0], list(refs[1:])
    maps_ref = None
    early = [refs.pop(0) for _ in range(count)] if step == 0 else None
    late = None
    if first_layer and step > 0:
        late = [refs.pop(0) for _ in range(count)]
    if not first_layer:
        maps_ref = refs.pop(0)
    hidden_ref = cell_ref = None
    if step > 0:
        hidden_ref, cell_ref = refs.pop(0), refs.pop(0)
    weights, bias, _ = refs[:3]
    hidden_out, cell_out, kept, slab = refs[3:]
    total = rows_n * width
    lip = (wide - width) // 2

    @pl.when(place[0] == phase)
    def _():
        blank = jnp.zeros((width, 6 * chans), BF)
        slab[0:width, :] = blank
        slab[total + width : total + 2 * width, :] = blank

        def spread(lane, value):
            value = value.astype(F32)
            for tap in range(3):
                moved = value if tap == 1 else pltpu.roll(value, (1 - tap) % total, 0)
                at = 2 * chans * tap + lane
                slab[width : width + total, at : at + chans] = moved.astype(BF)

        def spread_band(lane, value, source, extent):
            flat = value.reshape(band * extent, chans).astype(F32)
            edge = (extent - width) // 2
            for tap in range(3):
                moved = flat if tap == 1 else pltpu.roll(flat, (1 - tap) % (band * extent), 0)
                moved = moved.reshape(band, extent, chans)[:, edge : edge + width]
                moved = moved.reshape(band * width, chans).astype(BF)
                at = 2 * chans * tap + lane
                start = pl.multiple_of((source * band + 1) * width, 16)
                slab[pl.ds(start, band * width), at : at + chans] = moved

        if step == 0:
            for hop in range(count):
                source = place[2 + hop]
                spread_band(chans, early[hop][0], source, wide)
                if first_layer:
                    spread_band(0, early[hop][2], source, wide)
                start = pl.multiple_of(source * band * width, 16)
                cell = early[hop][1].astype(F32)[:, lip : lip + width]
                cell_out[pl.ds(start, band * width), :] = cell.reshape(band * width, chans)
        else:
            spread(chans, hidden_ref[...].reshape(total, chans))
            if first_layer:
                for hop in range(count):
                    spread_band(0, late[hop][...], place[2 + hop], width)
        if not first_layer:
            spread(0, maps_ref[...].reshape(total, chans))

        depth = 6 * chans
        gates = bias[...]
        for tap in range(3):
            gates = gates + jnp.dot(
                slab[tap * width : tap * width + total, :],
                weights[tap * depth : (tap + 1) * depth, :],
                preferred_element_type=F32,
            )
        cell = cell_out[...] if step == 0 else cell_ref[...]
        cell = sigmoid(gates[:, chans : 2 * chans]) * cell + sigmoid(gates[:, :chans]) * jnp.tanh(
            gates[:, 2 * chans : 3 * chans]
        )
        hidden = sigmoid(gates[:, 3 * chans :]) * jnp.tanh(cell)
        hidden = hidden.reshape(rows_n, width, chans)
        column = place[1] + lax.broadcasted_iota(jnp.int32, hidden.shape, 1)
        inside = jnp.logical_and(column >= 0, column < place[2 + count])
        hidden = jnp.where(inside, hidden, 0.0).astype(BF)
        hidden_out[...] = hidden
        cell_out[...] = cell
        kept[:, step] = hidden
        if step == steps - 1:
            high = cell.astype(BF)
            low = (cell - high.astype(F32)).astype(BF)
            kept[:, steps] = high.reshape(rows_n, width, chans)
            kept[:, steps + 1] = low.reshape(rows_n, width, chans)


def advance(dims, step, first_layer, place, sources, weights, bias, kept):
    rows_n, band, width, wide, chans, steps, count, phase = dims
    vmem = pl.BlockSpec(memory_space=pltpu.VMEM)
    operands = [place, *sources, weights, bias, kept]
    total = rows_n * width
    return pl.pallas_call(
        functools.partial(step_kernel, dims, step, first_layer),
        out_shape=(
            jax.ShapeDtypeStruct((rows_n, width, chans), BF),
            jax.ShapeDtypeStruct((total, chans), F32),
            jax.ShapeDtypeStruct(kept.shape, kept.dtype),
        ),
        in_specs=[pl.BlockSpec(memory_space=pltpu.SMEM)] + [vmem] * (len(operands) - 1),
        out_specs=(vmem, vmem, vmem),
        scratch_shapes=[pltpu.VMEM((total + 2 * width, 6 * chans), BF)],
        input_output_aliases={len(operands) - 1: 2},
        compiler_params=pltpu.CompilerParams(vmem_limit_bytes=40 * 1024 * 1024),
        cost_estimate=pl.CostEstimate(
            flops=2 * total * 18 * chans * 4 * chans,
            bytes_accessed=1000000,
            transcendentals=5 * total * chans,
        ),
    )(*operands)


def column_edges(block, extent):
    count = lax.axis_size("cols")
    place = lax.axis_index("cols")
    first, last = block[..., :extent, :], block[..., block.shape[-2] - extent :, :]
    if count == 2:
        got = lax.ppermute(jnp.where(place == 0, last, first), "cols", [(0, 1), (1, 0)])
        blank = jnp.zeros_like(got)
        left, right = jnp.where(place == 1, got, blank), jnp.where(place == 0, got, blank)
    else:
        left = lax.ppermute(last, "cols", [(n, n + 1) for n in range(count - 1)])
        right = lax.ppermute(first, "cols", [(n + 1, n) for n in range(count - 1)])
    return jnp.concatenate([left, block, right], axis=-2)


def exchange(piece_for, place, count):
    got = [piece_for(place)]
    for hop in range(1, count):
        target, _ = partner(place, hop, count)
        route = [(n, partner(n, hop, count)[0]) for n in range(count)]
        got.append(lax.ppermute(piece_for(target), "rows", route))
    return got


def shards(inputs, hidden_init, cell_init, kernels, biases):
    steps, band, columns, chans = inputs.shape
    count = lax.axis_size("rows")
    layers = lax.axis_size("pipe")
    place_row = lax.axis_index("rows")
    place_col = lax.axis_index("cols")
    layer = lax.axis_index("pipe")
    rows_n = band * count
    strip = columns // count
    pad = round_up(steps + layers - 2, 8)
    width = round_up(strip + 2 * pad, 16)
    wide = width + 16
    edge = round_up(max(pad + 8, width - pad + 8 - strip), 16)

    maps = jnp.concatenate([hidden_init, cell_init.astype(BF), inputs], axis=0)
    padded = column_edges(maps, edge)

    def cut(first, last, reach, extent):
        def piece_for(index):
            start = index * strip + (edge - reach)
            return lax.dynamic_slice_in_dim(padded[first:last], start, extent, axis=2)

        return exchange(piece_for, place_row, count)

    early = cut(0, 3, pad + 8, wide)
    middle = (steps + 1) // 2
    late_a = cut(3, 2 + middle, pad, width)
    late_b = cut(2 + middle, 2 + steps, pad, width)

    sources = [partner(place_row, hop, count)[1] for hop in range(count)]
    first_column = place_col * columns + place_row * strip - pad
    everything = columns * lax.axis_size("cols")
    place = jnp.stack([layer, first_column, *sources, jnp.asarray(everything)]).astype(jnp.int32)

    kept = jnp.zeros((rows_n, steps + 2, width, chans), BF)
    weights, bias = kernels[0], biases
    sent = []
    for phase in range(layers):
        dims = (rows_n, band, width, wide, chans, steps, count, phase)
        received = sent
        sent = []
        hidden = cell = None
        for step in range(steps):
            feed = []
            if step == 0:
                feed += early
            if phase == 0 and step > 0:
                late, at = (late_a, step - 1) if step < middle else (late_b, step - middle)
                feed += [piece[at] for piece in late]
            if phase > 0:
                feed.append(received[step])
            if step > 0:
                feed += [hidden, cell]
            hidden, cell, kept = advance(
                dims, step, phase == 0, place, feed, weights, bias, kept
            )
            if phase < layers - 1:
                sent.append(lax.ppermute(hidden, "pipe", [(phase, phase + 1)]))

    def out_piece(index):
        piece = lax.dynamic_slice_in_dim(kept, index * band, band, axis=0)
        return piece[:, :, pad : pad + strip]

    out = jnp.zeros((band, steps + 2, columns, chans), BF)
    for source, piece in zip(sources, exchange(out_piece, place_row, count)):
        out = lax.dynamic_update_slice_in_dim(out, piece, source * strip, axis=2)
    produced = jnp.swapaxes(out[:, :steps], 0, 1)
    final = out[:, steps].astype(F32) + out[:, steps + 1].astype(F32)
    return produced[None], final[None]


def solution(mesh):
    return jax.shard_map(
        shards,
        mesh=mesh,
        in_specs=(
            P(None, ("groups", "rows"), "cols", None),
            P("pipe", ("groups", "rows"), "cols", None),
            P("pipe", ("groups", "rows"), "cols", None),
            P("pipe", None, None),
            P("pipe", None),
        ),
        out_specs=(
            P("pipe", None, ("groups", "rows"), "cols", None),
            P("pipe", ("groups", "rows"), "cols", None),
        ),
        check_vma=False,
    )
```

time: 213 us -> 79.6 us (0.37); the launches traced: 209 us -> 78.5 us
  starting transfers between devices: 106 us -> 34.7 us
  waiting for transfers between devices: 67.9 us -> 17.9 us
  Pallas kernels: 0 us -> 19.7 us
  local copies, waits for them, and re-layouts: 15.7 us -> 1.56 us
  other arithmetic: 10.6 us -> 3.51 us
  matrix products: 6.15 us -> 0 us
    ppermute x45 -> x21, starting transfers between devices: 106 us -> 34.7 us  [the longest x12 24.3 us: exchange(): got.append(lax.ppermute(piece_for(target), 'rows', route))]
    ppermute x45 -> x21, waiting for transfers between devices: 67.9 us -> 17.9 us  [the longest x12 13.2 us: exchange(): got.append(lax.ppermute(piece_for(target), 'rows', route))]
    pallas_call x0 -> x16, Pallas kernels: none -> 19.7 us  [advance(): pl.pallas_call(functools.partial(step_kernel, dims, step, first_layer), o...]
    cond x80 -> x0, local copies, waits for them, and re-layouts: 12.4 us -> none
    select_n x9 -> x2, other arithmetic: 7.64 us -> 0.93 us  [the longest x1 0.91 us: column_edges(): jnp.where(place == 0, last, first)]
    dot_general x8 -> x0, matrix products: 6.15 us -> none  [gate_values(): total = jnp.dot(slab, weights, preferred_element_type=jnp.float32)]
    unnamed x6 -> x8, local copies, waits for them, and re-layouts: 2.57 us -> 0.02 us
  transfers between devices with their start and end apart: 45 -> 21, of which waited for: 36 -> 6; matrix products, arithmetic and copies ran while one was open for 0% -> 1% of each run, Pallas kernels for 0% -> 22%
where the time goes in v1:
time: 79.6 us; the launch traced here: 78.5 us
  starting transfers between devices  34.7 us (44%)
  Pallas kernels  19.7 us (25%)
  waiting for transfers between devices  17.9 us (22%)
  other arithmetic  3.51 us (4%)
  local copies, waits for them, and re-layouts  1.56 us (2%)
  between operations  1.17 us (1%)
    ppermute x12, starting transfers between devices, exchange(): got.append(lax.ppermute(piece_for(target), 'rows', route))  24.3 us
    pallas_call x16, Pallas kernels, advance(): pl.pallas_call(functools.partial(step_kernel, dims, step, first_layer), o...  19.7 us
    ppermute x12, waiting for transfers between devices, exchange(): got.append(lax.ppermute(piece_for(target), 'rows', route))  13.2 us
    ppermute x8, starting transfers between devices, shards(): sent.append(lax.ppermute(hidden, 'pipe', [(phase, phase + 1)]))  10.3 us
    ppermute x8, waiting for transfers between devices, shards(): sent.append(lax.ppermute(hidden, 'pipe', [(phase, phase + 1)]))  3.55 us
  transfers between devices with their start and end apart: 21, of which 6 were waited for; matrix products, arithmetic and copies ran while one was open for 1% of the time, Pallas kernels for 22%

profile of v1, /device:TPU:6, one launch (start us, length us, event | category | flops | bytes accessed | tf_op | source)
XLA Modules:
  0.0 78.5 jit_solution(5020312710208953836)
XLA Ops:
  0.6 0.0 copy-start.2
  0.6 0.0 copy-start.3
  0.7 1.0 %convert_element_type.25 = bf16[1,2,128,128]{3,2,1,0:T(8,128)(2,1)S(1)} convert(f32[1,2,128,128]{3,2,1,0:T(8,128)} %param.7) | non-fusion elementwise | flops 32768 | bytes 196608 | tf_op jit(solution)/shard_map/convert_element_type | solution.py:176
  1.6 0.9 %fusion = bf16[10,2,16,128]{3,2,1,0:T(8,128)(2,1)S(1)} fusion(bf16[8,2,128,128]{3,2,1,0:T(8,128)(2,1)} %param.5, bf16[1,2,128,128]{3,2,1,0:T(8,128)(2,1)S(1)} %convert_element_type.25, bf16[1,2,128,128]{3,2,1,0:T(8,128)(2,1)} %param.6, pred[]{:T(512)S(6)} %eq.8), kind=kLoop, calls=%fused_computation.10 | loop fusion | flops 532480 | bytes 737281 | tf_op jit(solution)/shard_map/jit(_where)/select_n | solution.py:144
  2.6 0.1 collective-permute-start
  2.7 0.1 stack.27.refs_0_
  2.8 1.1 %collective-permute-done = bf16[10,2,16,128]{3,2,1,0:T(8,128)(2,1)S(1)} collective-permute-done((bf16[10,2,16,128]{3,2,1,0:T(8,128)(2,1)S(1)}, bf16[10,2,16,128]{3,2,1,0:T(8,128)(2,1)S(1)}, u32[]{:S(2)}, u32[]{:S(2)}) %collective-permute-start) | collective-permute-done | bytes 81952 | tf_op jit(solution)/shard_map/ppermute | solution.py:144
  3.9 0.9 %pad_maximum_fusion.1 = (bf16[3,2,160,128]{3,2,1,0:T(8,128)(2,1)S(1)}, bf16[3,2,160,128]{3,2,1,0:T(8,128)(2,1)S(1)}) fusion(bf16[10,2,16,128]{3,2,1,0:T(8,128)(2,1)S(1)} %get-tuple-element.128, bf16[10,2,16,128]{3,2,1,0:T(8,128)(2,1)S(1)} %get-tuple-element.127, bf16[8,2,128,128]{3,2,1,0:T(8,128)(2,1)S(1)} %copy-done.2, ...), kind=kLoop, calls=%fused_computation.2 | loop fusion | flops 2457600 | bytes 1310720 | tf_op jit(solution)/shard_map/slice | solution.py:182
  4.8 0.1 pad_maximum_fusion
  4.9 0.1 constant_dynamic-slice_fusion.4
  4.9 1.6 %collective-permute-start.7 = (bf16[3,2,64,128]{3,2,1,0:T(8,128)(2,1)S(1)}, bf16[3,2,64,128]{3,2,1,0:T(8,128)(2,1)S(1)}, u32[]{:S(2)}, u32[]{:S(2)}) collective-permute-start(bf16[3,2,64,128]{3,2,1,0:T(8,128)(2,1)S(1)} %get-tuple-element.107), channel_id=1, source_target_pairs={{0,4},{4,0},{8,12},{12,8},{1,5},{5,1},{9,13},{13,9},{2,6},{6,2},{1... | collective-permute-start | bytes 294920 | tf_op jit(solution)/shard_map/ppermute | solution.py:158
  6.6 2.6 %collective-permute-start.8 = (bf16[3,2,64,128]{3,2,1,0:T(8,128)(2,1)S(1)}, bf16[3,2,64,128]{3,2,1,0:T(8,128)(2,1)S(1)}, u32[]{:S(2)}, u32[]{:S(2)}) collective-permute-start(bf16[3,2,64,128]{3,2,1,0:T(8,128)(2,1)S(1)} %get-tuple-element.106), channel_id=1, source_target_pairs={{0,8},{4,12},{8,0},{12,4},{1,9},{5,13},{9,1},{13,5},{2,10},{6,14},... | collective-permute-start | bytes 294920 | tf_op jit(solution)/shard_map/ppermute | solution.py:158
  9.2 0.2 collective-permute-start.9
  9.4 3.7 %collective-permute-start.6 = (bf16[3,2,48,128]{3,2,1,0:T(8,128)(2,1)S(1)}, bf16[3,2,48,128]{3,2,1,0:T(8,128)(2,1)S(1)}, u32[]{:S(2)}, u32[]{:S(2)}) collective-permute-start(bf16[3,2,48,128]{3,2,1,0:T(8,128)(2,1)S(1)} %get-tuple-element.112), channel_id=1, source_target_pairs={{0,12},{4,8},{8,4},{12,0},{1,13},{5,9},{9,5},{13,1},{2,14},{6,10},... | collective-permute-start | bytes 221192 | tf_op jit(solution)/shard_map/ppermute | solution.py:158
  13.1 0.0 collective-permute-start.5
  13.2 5.4 %collective-permute-done.6 = bf16[3,2,48,128]{3,2,1,0:T(8,128)(2,1)S(1)} collective-permute-done((bf16[3,2,48,128]{3,2,1,0:T(8,128)(2,1)S(1)}, bf16[3,2,48,128]{3,2,1,0:T(8,128)(2,1)S(1)}, u32[]{:S(2)}, u32[]{:S(2)}) %collective-permute-start.6) | collective-permute-done | bytes 73760 | tf_op jit(solution)/shard_map/ppermute | solution.py:158
  18.6 5.9 %collective-permute-start.4 = (bf16[3,2,48,128]{3,2,1,0:T(8,128)(2,1)S(1)}, bf16[3,2,48,128]{3,2,1,0:T(8,128)(2,1)S(1)}, u32[]{:S(2)}, u32[]{:S(2)}) collective-permute-start(bf16[3,2,48,128]{3,2,1,0:T(8,128)(2,1)S(1)} %get-tuple-element.114), channel_id=1, source_target_pairs={{0,4},{4,0},{8,12},{12,8},{1,5},{5,1},{9,13},{13,9},{2,6},{6,2},{1... | collective-permute-start | bytes 221192 | tf_op jit(solution)/shard_map/ppermute | solution.py:158
  24.5 0.3 collective-permute-done.5
  24.8 2.5 %collective-permute-start.3 = (bf16[4,2,48,128]{3,2,1,0:T(8,128)(2,1)S(1)}, bf16[4,2,48,128]{3,2,1,0:T(8,128)(2,1)S(1)}, u32[]{:S(2)}, u32[]{:S(2)}) collective-permute-start(bf16[4,2,48,128]{3,2,1,0:T(8,128)(2,1)S(1)} %get-tuple-element.102), channel_id=1, source_target_pairs={{0,12},{4,8},{8,4},{12,0},{1,13},{5,9},{9,5},{13,1},{2,14},{6,10},... | collective-permute-start | bytes 294920 | tf_op jit(solution)/shard_map/ppermute | solution.py:158
  27.3 0.0 collective-permute-done.4
  27.3 3.3 %collective-permute-start.2 = (bf16[4,2,48,128]{3,2,1,0:T(8,128)(2,1)S(1)}, bf16[4,2,48,128]{3,2,1,0:T(8,128)(2,1)S(1)}, u32[]{:S(2)}, u32[]{:S(2)}) collective-permute-start(bf16[4,2,48,128]{3,2,1,0:T(8,128)(2,1)S(1)} %get-tuple-element.103), channel_id=1, source_target_pairs={{0,8},{4,12},{8,0},{12,4},{1,9},{5,13},{9,1},{13,5},{2,10},{6,14},... | collective-permute-start | bytes 294920 | tf_op jit(solution)/shard_map/ppermute | solution.py:158
  30.6 0.0 collective-permute-done.7.refs_2_
  30.6 0.1 collective-permute-start.1
  30.7 0.0 collective-permute-done.8.refs_3_
  30.7 0.0 collective-permute-done.9.refs_4_
  30.7 0.1 broadcast_in_dim.15.refs_7_
  30.9 0.6 shard_map.68
  31.4 1.3 %collective-permute-start.17 = (bf16[8,48,128]{2,1,0:T(8,128)(2,1)S(1)}, bf16[8,48,128]{2,1,0:T(8,128)(2,1)S(1)}, u32[]{:S(2)}, u32[]{:S(2)}) collective-permute-start(bf16[8,48,128]{2,1,0:T(8,128)(2,1)S(1)} %get-tuple-element.47.refs_5_), channel_id=1, source_target_pairs={{0,2},{1,3},{4,6},{5,7},{8,10},{9,11},{12,14},{13,15},{16,18},{17,... | collective-permute-start | bytes 294920 | tf_op jit(solution)/shard_map/ppermute | solution.py:219
  32.7 0.6 shard_map.69
  33.3 1.3 %collective-permute-start.16 = (bf16[8,48,128]{2,1,0:T(8,128)(2,1)S(1)}, bf16[8,48,128]{2,1,0:T(8,128)(2,1)S(1)}, u32[]{:S(2)}, u32[]{:S(2)}) collective-permute-start(bf16[8,48,128]{2,1,0:T(8,128)(2,1)S(1)} %get-tuple-element.50.refs_5_), channel_id=1, source_target_pairs={{0,2},{1,3},{4,6},{5,7},{8,10},{9,11},{12,14},{13,15},{16,18},{17,... | collective-permute-start | bytes 294920 | tf_op jit(solution)/shard_map/ppermute | solution.py:219
  34.6 0.6 shard_map.70
  35.2 1.3 %collective-permute-start.15 = (bf16[8,48,128]{2,1,0:T(8,128)(2,1)S(1)}, bf16[8,48,128]{2,1,0:T(8,128)(2,1)S(1)}, u32[]{:S(2)}, u32[]{:S(2)}) collective-permute-start(bf16[8,48,128]{2,1,0:T(8,128)(2,1)S(1)} %get-tuple-element.53.refs_5_), channel_id=1, source_target_pairs={{0,2},{1,3},{4,6},{5,7},{8,10},{9,11},{12,14},{13,15},{16,18},{17,... | collective-permute-start | bytes 294920 | tf_op jit(solution)/shard_map/ppermute | solution.py:219
  36.5 0.6 shard_map.71
  37.0 1.3 %collective-permute-start.14 = (bf16[8,48,128]{2,1,0:T(8,128)(2,1)S(1)}, bf16[8,48,128]{2,1,0:T(8,128)(2,1)S(1)}, u32[]{:S(2)}, u32[]{:S(2)}) collective-permute-start(bf16[8,48,128]{2,1,0:T(8,128)(2,1)S(1)} %get-tuple-element.56.refs_5_), channel_id=1, source_target_pairs={{0,2},{1,3},{4,6},{5,7},{8,10},{9,11},{12,14},{13,15},{16,18},{17,... | collective-permute-start | bytes 294920 | tf_op jit(solution)/shard_map/ppermute | solution.py:219
  38.4 0.0 collective-permute-done.1
  38.4 0.6 shard_map.72
  38.9 1.3 %collective-permute-start.13 = (bf16[8,48,128]{2,1,0:T(8,128)(2,1)S(1)}, bf16[8,48,128]{2,1,0:T(8,128)(2,1)S(1)}, u32[]{:S(2)}, u32[]{:S(2)}) collective-permute-start(bf16[8,48,128]{2,1,0:T(8,128)(2,1)S(1)} %get-tuple-element.59.refs_5_), channel_id=1, source_target_pairs={{0,2},{1,3},{4,6},{5,7},{8,10},{9,11},{12,14},{13,15},{16,18},{17,... | collective-permute-start | bytes 294920 | tf_op jit(solution)/shard_map/ppermute | solution.py:219
  40.2 0.6 shard_map.73
  40.8 0.6 shard_map.74
  41.4 1.2 %shard_map.75 = (bf16[8,48,128]{2,1,0:T(8,128)(2,1)S(1)}, f32[384,128]{1,0:T(8,128)}, bf16[8,10,48,128]{3,2,1,0:T(8,128)(2,1)S(1)}) custom-call(s32[7]{0:T(128)S(1)} %stack.27.refs_0_, bf16[2,48,128]{2,1,0:T(8,128)(2,1)S(1)} %get-tuple-element.101.refs_1_, bf16[2,48,128]{2,1,0:T(8,128)(2,1)S(1)} %get-tuple-element.126.refs_2_, ...), custom_call_target="tpu_custom_call", output_to_operand_aliasing={{2}: (9, {})} | custom-call | flops 905969664 | bytes 1000000 | tf_op jit(solution)/shard_map/pallas_call | solution.py:119
  42.6 1.3 %collective-permute-start.12 = (bf16[8,48,128]{2,1,0:T(8,128)(2,1)S(1)}, bf16[8,48,128]{2,1,0:T(8,128)(2,1)S(1)}, u32[]{:S(2)}, u32[]{:S(2)}) collective-permute-start(bf16[8,48,128]{2,1,0:T(8,128)(2,1)S(1)} %get-tuple-element.62.refs_5_), channel_id=1, source_target_pairs={{0,2},{1,3},{4,6},{5,7},{8,10},{9,11},{12,14},{13,15},{16,18},{17,... | collective-permute-start | bytes 294920 | tf_op jit(solution)/shard_map/ppermute | solution.py:219
  43.9 1.7 %shard_map.76 = (bf16[8,48,128]{2,1,0:T(8,128)(2,1)S(1)}, f32[384,128]{1,0:T(8,128)S(1)}, bf16[8,10,48,128]{3,2,1,0:T(8,128)(2,1)S(1)}) custom-call(s32[7]{0:T(128)S(1)} %stack.27.refs_0_, bf16[3,2,64,128]{3,2,1,0:T(8,128)(2,1)S(1)} %get-tuple-element.108.refs_1_, ...), custom_call_target="tpu_custom_call", output_to_operand_aliasing={{2}: (8, {})} | custom-call | flops 905969664 | bytes 1000000 | tf_op jit(solution)/shard_map/pallas_call | solution.py:119
  45.6 1.3 %collective-permute-start.11 = (bf16[8,48,128]{2,1,0:T(8,128)(2,1)S(1)}, bf16[8,48,128]{2,1,0:T(8,128)(2,1)S(1)}, u32[]{:S(2)}, u32[]{:S(2)}) collective-permute-start(bf16[8,48,128]{2,1,0:T(8,128)(2,1)S(1)} %get-tuple-element.65.refs_5_), channel_id=1, source_target_pairs={{0,2},{1,3},{4,6},{5,7},{8,10},{9,11},{12,14},{13,15},{16,18},{17,... | collective-permute-start | bytes 294920 | tf_op jit(solution)/shard_map/ppermute | solution.py:219
  46.9 1.7 %shard_map.77 = (bf16[8,48,128]{2,1,0:T(8,128)(2,1)S(1)}, f32[384,128]{1,0:T(8,128)S(1)}, bf16[8,10,48,128]{3,2,1,0:T(8,128)(2,1)S(1)}) custom-call(s32[7]{0:T(128)S(1)} %stack.27.refs_0_, bf16[8,48,128]{2,1,0:T(8,128)(2,1)S(1)} %collective-permute-done.16.refs_1_, ...), custom_call_target="tpu_custom_call", output_to_operand_aliasing={{2}: (6, {})} | custom-call | flops 905969664 | bytes 1000000 | tf_op jit(solution)/shard_map/pallas_call | solution.py:119
  48.7 0.0 collective-permute-done.15.refs_1_
  48.7 1.3 %collective-permute-start.10 = (bf16[8,48,128]{2,1,0:T(8,128)(2,1)S(1)}, bf16[8,48,128]{2,1,0:T(8,128)(2,1)S(1)}, u32[]{:S(2)}, u32[]{:S(2)}) collective-permute-start(bf16[8,48,128]{2,1,0:T(8,128)(2,1)S(1)} %get-tuple-element.68), channel_id=1, source_target_pairs={{0,2},{1,3},{4,6},{5,7},{8,10},{9,11},{12,14},{13,15},{16,18},{17,... | collective-permute-start | bytes 294920 | tf_op jit(solution)/shard_map/ppermute | solution.py:219
  50.0 1.7 %shard_map.78 = (bf16[8,48,128]{2,1,0:T(8,128)(2,1)S(1)}, f32[384,128]{1,0:T(8,128)S(1)}, bf16[8,10,48,128]{3,2,1,0:T(8,128)(2,1)S(1)}) custom-call(s32[7]{0:T(128)S(1)} %stack.27.refs_0_, bf16[8,48,128]{2,1,0:T(8,128)(2,1)S(1)} %collective-permute-done.15.refs_1_, ...), custom_call_target="tpu_custom_call", output_to_operand_aliasing={{2}: (6, {})} | custom-call | flops 905969664 | bytes 1000000 | tf_op jit(solution)/shard_map/pallas_call | solution.py:119
  51.7 0.0 collective-permute-done.14.refs_1_
  51.7 1.7 %shard_map.79 = (bf16[8,48,128]{2,1,0:T(8,128)(2,1)S(1)}, f32[384,128]{1,0:T(8,128)S(1)}, bf16[8,10,48,128]{3,2,1,0:T(8,128)(2,1)S(1)}) custom-call(s32[7]{0:T(128)S(1)} %stack.27.refs_0_, bf16[8,48,128]{2,1,0:T(8,128)(2,1)S(1)} %collective-permute-done.14.refs_1_, ...), custom_call_target="tpu_custom_call", output_to_operand_aliasing={{2}: (6, {})} | custom-call | flops 905969664 | bytes 1000000 | tf_op jit(solution)/shard_map/pallas_call | solution.py:119
  53.4 0.0 collective-permute-done.13.refs_1_
  53.4 1.7 %shard_map.80 = (bf16[8,48,128]{2,1,0:T(8,128)(2,1)S(1)}, f32[384,128]{1,0:T(8,128)S(1)}, bf16[8,10,48,128]{3,2,1,0:T(8,128)(2,1)S(1)}) custom-call(s32[7]{0:T(128)S(1)} %stack.27.refs_0_, bf16[8,48,128]{2,1,0:T(8,128)(2,1)S(1)} %collective-permute-done.13.refs_1_, ...), custom_call_target="tpu_custom_call", output_to_operand_aliasing={{2}: (6, {})} | custom-call | flops 905969664 | bytes 1000000 | tf_op jit(solution)/shard_map/pallas_call | solution.py:119
  55.1 3.5 %collective-permute-done.12.refs_1_ = bf16[8,48,128]{2,1,0:T(8,128)(2,1)S(1)} collective-permute-done((bf16[8,48,128]{2,1,0:T(8,128)(2,1)S(1)}, bf16[8,48,128]{2,1,0:T(8,128)(2,1)S(1)}, u32[]{:S(2)}, u32[]{:S(2)}) %collective-permute-start.12) | collective-permute-done | bytes 98336 | tf_op jit(solution)/shard_map/ppermute | solution.py:219
  58.6 1.9 %shard_map.81 = (bf16[8,48,128]{2,1,0:T(8,128)(2,1)S(1)}, f32[384,128]{1,0:T(8,128)S(1)}, bf16[8,10,48,128]{3,2,1,0:T(8,128)(2,1)S(1)}) custom-call(s32[7]{0:T(128)S(1)} %stack.27.refs_0_, bf16[8,48,128]{2,1,0:T(8,128)(2,1)S(1)} %collective-permute-done.12.refs_1_, ...), custom_call_target="tpu_custom_call", output_to_operand_aliasing={{2}: (6, {})} | custom-call | flops 905969664 | bytes 1000000 | tf_op jit(solution)/shard_map/pallas_call | solution.py:119
  60.5 1.7 %shard_map.82 = (bf16[8,48,128]{2,1,0:T(8,128)(2,1)S(1)}, f32[384,128]{1,0:T(8,128)S(1)}, bf16[8,10,48,128]{3,2,1,0:T(8,128)(2,1)S(1)}) custom-call(s32[7]{0:T(128)S(1)} %stack.27.refs_0_, bf16[8,48,128]{2,1,0:T(8,128)(2,1)S(1)} %collective-permute-done.11.refs_1_, ...), custom_call_target="tpu_custom_call", output_to_operand_aliasing={{2}: (6, {})} | custom-call | flops 905969664 | bytes 1000000 | tf_op jit(solution)/shard_map/pallas_call | solution.py:119
  62.2 2.4 %shard_map.83 = (bf16[8,48,128]{2,1,0:T(8,128)(2,1)}, f32[384,128]{1,0:T(8,128)}, bf16[8,10,48,128]{3,2,1,0:T(8,128)(2,1)S(1)}) custom-call(s32[7]{0:T(128)S(1)} %stack.27.refs_0_, bf16[8,48,128]{2,1,0:T(8,128)(2,1)S(1)} %collective-permute-done.10.refs_1_, bf16[8,48,128]{2,1,0:T(8,128)(2,1)S(1)} %get-tuple-element.88.refs_2_, ...), custom_call_target="tpu_custom_call", output_to_operand_aliasing={{2}: (6, {})} | custom-call | flops 905969664 | bytes 1000000 | tf_op jit(solution)/shard_map/pallas_call | solution.py:119
  64.7 0.1 constant_dynamic-slice_fusion
  64.7 1.4 %collective-permute-start.18 = (bf16[2,10,32,128]{3,2,1,0:T(8,128)(2,1)S(1)}, bf16[2,10,32,128]{3,2,1,0:T(8,128)(2,1)S(1)}, u32[]{:S(2)}, u32[]{:S(2)}) collective-permute-start(bf16[2,10,32,128]{3,2,1,0:T(8,128)(2,1)S(1)} %get-tuple-element.94), channel_id=1, source_target_pairs={{0,4},{4,0},{8,12},{12,8},{1,5},{5,1},{9,13},{13,9},{2,6},{6,2},{1... | collective-permute-start | bytes 491528 | tf_op jit(solution)/shard_map/ppermute | solution.py:158
  66.2 0.6 collective-permute-start.19
  66.8 2.4 %collective-permute-start.20 = (bf16[2,10,32,128]{3,2,1,0:T(8,128)(2,1)S(1)}, bf16[2,10,32,128]{3,2,1,0:T(8,128)(2,1)S(1)}, u32[]{:S(2)}, u32[]{:S(2)}) collective-permute-start(bf16[2,10,32,128]{3,2,1,0:T(8,128)(2,1)S(1)} %get-tuple-element.92), channel_id=1, source_target_pairs={{0,12},{4,8},{8,4},{12,0},{1,13},{5,9},{9,5},{13,1},{2,14},{6,10},... | collective-permute-start | bytes 491528 | tf_op jit(solution)/shard_map/ppermute | solution.py:158
  69.2 0.1 broadcast_in_dim.13
  69.4 2.5 %collective-permute-done.18 = bf16[2,10,32,128]{3,2,1,0:T(8,128)(2,1)S(1)} collective-permute-done((bf16[2,10,32,128]{3,2,1,0:T(8,128)(2,1)S(1)}, bf16[2,10,32,128]{3,2,1,0:T(8,128)(2,1)S(1)}, u32[]{:S(2)}, u32[]{:S(2)}) %collective-permute-start.18) | collective-permute-done | bytes 163872 | tf_op jit(solution)/shard_map/ppermute | solution.py:158
  71.9 5.0 %collective-permute-done.19 = bf16[2,10,32,128]{3,2,1,0:T(8,128)(2,1)S(1)} collective-permute-done((bf16[2,10,32,128]{3,2,1,0:T(8,128)(2,1)S(1)}, bf16[2,10,32,128]{3,2,1,0:T(8,128)(2,1)S(1)}, u32[]{:S(2)}, u32[]{:S(2)}) %collective-permute-start.19) | collective-permute-done | bytes 163872 | tf_op jit(solution)/shard_map/ppermute | solution.py:158
  77.0 0.8 %slice_bitcast_fusion = bf16[1,8,2,128,128]{4,3,2,1,0:T(8,128)(2,1)} fusion(bf16[2,10,128,128]{3,2,0,1:T(8,128)(2,1)S(1)} %copy_dynamic-update-slice_fusion), kind=kLoop, calls=%fused_computation.1 | loop fusion | bytes 1048576 | tf_op jit(solution)/shard_map/broadcast_in_dim | solution.py:230
  77.8 0.7 add_bitcast_fusion
  (29 shorter events, 0.3 us)
Async XLA Ops:
  0.6 3.3 %copy-start.2 = (bf16[8,2,128,128]{3,2,1,0:T(8,128)(2,1)S(1)}, bf16[8,2,128,128]{3,2,1,0:T(8,128)(2,1)}, u32[]{:S(2)}) copy-start(bf16[8,2,128,128]{3,2,1,0:T(8,128)(2,1)} %param.5) | copy-start | bytes 1572868
  0.6 4.2 %copy-start.3 = (bf16[1,2,128,128]{3,2,1,0:T(8,128)(2,1)S(1)}, bf16[1,2,128,128]{3,2,1,0:T(8,128)(2,1)}, u32[]{:S(2)}) copy-start(bf16[1,2,128,128]{3,2,1,0:T(8,128)(2,1)} %param.6) | copy-start | bytes 196612
  2.6 1.3 %collective-permute-start = (bf16[10,2,16,128]{3,2,1,0:T(8,128)(2,1)S(1)}, bf16[10,2,16,128]{3,2,1,0:T(8,128)(2,1)S(1)}, u32[]{:S(2)}, u32[]{:S(2)}) collective-permute-start(bf16[10,2,16,128]{3,2,1,0:T(8,128)(2,1)S(1)} %fusion), channel_id=1, source_target_pairs={{0,1},{1,0},{2,3},{3,2},{4,5},{5,4},{6,7},{7,6},{8,9},{9,8},{10,11... | collective-permute-start | bytes 245768 | tf_op jit(solution)/shard_map/ppermute | solution.py:144
  4.9 25.7 %collective-permute-start.7 = (bf16[3,2,64,128]{3,2,1,0:T(8,128)(2,1)S(1)}, bf16[3,2,64,128]{3,2,1,0:T(8,128)(2,1)S(1)}, u32[]{:S(2)}, u32[]{:S(2)}) collective-permute-start(bf16[3,2,64,128]{3,2,1,0:T(8,128)(2,1)S(1)} %get-tuple-element.107), channel_id=1, source_target_pairs={{0,4},{4,0},{8,12},{12,8},{1,5},{5,1},{9,13},{13,9},{2,6},{6,2},{1... | collective-permute-start | bytes 294920 | tf_op jit(solution)/shard_map/ppermute | solution.py:158
  6.6 24.1 %collective-permute-start.8 = (bf16[3,2,64,128]{3,2,1,0:T(8,128)(2,1)S(1)}, bf16[3,2,64,128]{3,2,1,0:T(8,128)(2,1)S(1)}, u32[]{:S(2)}, u32[]{:S(2)}) collective-permute-start(bf16[3,2,64,128]{3,2,1,0:T(8,128)(2,1)S(1)} %get-tuple-element.106), channel_id=1, source_target_pairs={{0,8},{4,12},{8,0},{12,4},{1,9},{5,13},{9,1},{13,5},{2,10},{6,14},... | collective-permute-start | bytes 294920 | tf_op jit(solution)/shard_map/ppermute | solution.py:158
  9.2 21.5 %collective-permute-start.9 = (bf16[3,2,64,128]{3,2,1,0:T(8,128)(2,1)S(1)}, bf16[3,2,64,128]{3,2,1,0:T(8,128)(2,1)S(1)}, u32[]{:S(2)}, u32[]{:S(2)}) collective-permute-start(bf16[3,2,64,128]{3,2,1,0:T(8,128)(2,1)S(1)} %get-tuple-element.105), channel_id=1, source_target_pairs={{0,12},{4,8},{8,4},{12,0},{1,13},{5,9},{9,5},{13,1},{2,14},{6,10},... | collective-permute-start | bytes 294920 | tf_op jit(solution)/shard_map/ppermute | solution.py:158
  9.4 21.5 %copy-start = (bf16[1,2304,512]{2,1,0:T(8,128)(2,1)S(1)}, bf16[1,2304,512]{2,1,0:T(8,128)(2,1)}, u32[]{:S(2)}) copy-start(bf16[1,2304,512]{2,1,0:T(8,128)(2,1)} %param.8) | copy-start | bytes 7077892
  9.4 21.5 %copy-start.1 = (f32[1,512]{1,0:T(1,128)S(1)}, f32[1,512]{1,0:T(1,128)}, u32[]{:S(2)}) copy-start(f32[1,512]{1,0:T(1,128)} %refs_5_.13) | copy-start | bytes 6148
  9.4 9.1 %collective-permute-start.6 = (bf16[3,2,48,128]{3,2,1,0:T(8,128)(2,1)S(1)}, bf16[3,2,48,128]{3,2,1,0:T(8,128)(2,1)S(1)}, u32[]{:S(2)}, u32[]{:S(2)}) collective-permute-start(bf16[3,2,48,128]{3,2,1,0:T(8,128)(2,1)S(1)} %get-tuple-element.112), channel_id=1, source_target_pairs={{0,12},{4,8},{8,4},{12,0},{1,13},{5,9},{9,5},{13,1},{2,14},{6,10},... | collective-permute-start | bytes 221192 | tf_op jit(solution)/shard_map/ppermute | solution.py:158
  13.1 11.8 %collective-permute-start.5 = (bf16[3,2,48,128]{3,2,1,0:T(8,128)(2,1)S(1)}, bf16[3,2,48,128]{3,2,1,0:T(8,128)(2,1)S(1)}, u32[]{:S(2)}, u32[]{:S(2)}) collective-permute-start(bf16[3,2,48,128]{3,2,1,0:T(8,128)(2,1)S(1)} %get-tuple-element.113), channel_id=1, source_target_pairs={{0,8},{4,12},{8,0},{12,4},{1,9},{5,13},{9,1},{13,5},{2,10},{6,14},... | collective-permute-start | bytes 221192 | tf_op jit(solution)/shard_map/ppermute | solution.py:158
  18.6 8.8 %collective-permute-start.4 = (bf16[3,2,48,128]{3,2,1,0:T(8,128)(2,1)S(1)}, bf16[3,2,48,128]{3,2,1,0:T(8,128)(2,1)S(1)}, u32[]{:S(2)}, u32[]{:S(2)}) collective-permute-start(bf16[3,2,48,128]{3,2,1,0:T(8,128)(2,1)S(1)} %get-tuple-element.114), channel_id=1, source_target_pairs={{0,4},{4,0},{8,12},{12,8},{1,5},{5,1},{9,13},{13,9},{2,6},{6,2},{1... | collective-permute-start | bytes 221192 | tf_op jit(solution)/shard_map/ppermute | solution.py:158
  24.8 10.3 %collective-permute-start.3 = (bf16[4,2,48,128]{3,2,1,0:T(8,128)(2,1)S(1)}, bf16[4,2,48,128]{3,2,1,0:T(8,128)(2,1)S(1)}, u32[]{:S(2)}, u32[]{:S(2)}) collective-permute-start(bf16[4,2,48,128]{3,2,1,0:T(8,128)(2,1)S(1)} %get-tuple-element.102), channel_id=1, source_target_pairs={{0,12},{4,8},{8,4},{12,0},{1,13},{5,9},{9,5},{13,1},{2,14},{6,10},... | collective-permute-start | bytes 294920 | tf_op jit(solution)/shard_map/ppermute | solution.py:158
  27.3 9.7 %collective-permute-start.2 = (bf16[4,2,48,128]{3,2,1,0:T(8,128)(2,1)S(1)}, bf16[4,2,48,128]{3,2,1,0:T(8,128)(2,1)S(1)}, u32[]{:S(2)}, u32[]{:S(2)}) collective-permute-start(bf16[4,2,48,128]{3,2,1,0:T(8,128)(2,1)S(1)} %get-tuple-element.103), channel_id=1, source_target_pairs={{0,8},{4,12},{8,0},{12,4},{1,9},{5,13},{9,1},{13,5},{2,10},{6,14},... | collective-permute-start | bytes 294920 | tf_op jit(solution)/shard_map/ppermute | solution.py:158
  30.6 7.8 %collective-permute-start.1 = (bf16[4,2,48,128]{3,2,1,0:T(8,128)(2,1)S(1)}, bf16[4,2,48,128]{3,2,1,0:T(8,128)(2,1)S(1)}, u32[]{:S(2)}, u32[]{:S(2)}) collective-permute-start(bf16[4,2,48,128]{3,2,1,0:T(8,128)(2,1)S(1)} %get-tuple-element.104), channel_id=1, source_target_pairs={{0,4},{4,0},{8,12},{12,8},{1,5},{5,1},{9,13},{13,9},{2,6},{6,2},{1... | collective-permute-start | bytes 294920 | tf_op jit(solution)/shard_map/ppermute | solution.py:158
  31.4 11.2 %collective-permute-start.17 = (bf16[8,48,128]{2,1,0:T(8,128)(2,1)S(1)}, bf16[8,48,128]{2,1,0:T(8,128)(2,1)S(1)}, u32[]{:S(2)}, u32[]{:S(2)}) collective-permute-start(bf16[8,48,128]{2,1,0:T(8,128)(2,1)S(1)} %get-tuple-element.47.refs_5_), channel_id=1, source_target_pairs={{0,2},{1,3},{4,6},{5,7},{8,10},{9,11},{12,14},{13,15},{16,18},{17,... | collective-permute-start | bytes 294920 | tf_op jit(solution)/shard_map/ppermute | solution.py:219
  33.3 12.4 %collective-permute-start.16 = (bf16[8,48,128]{2,1,0:T(8,128)(2,1)S(1)}, bf16[8,48,128]{2,1,0:T(8,128)(2,1)S(1)}, u32[]{:S(2)}, u32[]{:S(2)}) collective-permute-start(bf16[8,48,128]{2,1,0:T(8,128)(2,1)S(1)} %get-tuple-element.50.refs_5_), channel_id=1, source_target_pairs={{0,2},{1,3},{4,6},{5,7},{8,10},{9,11},{12,14},{13,15},{16,18},{17,... | collective-permute-start | bytes 294920 | tf_op jit(solution)/shard_map/ppermute | solution.py:219
  35.2 13.5 %collective-permute-start.15 = (bf16[8,48,128]{2,1,0:T(8,128)(2,1)S(1)}, bf16[8,48,128]{2,1,0:T(8,128)(2,1)S(1)}, u32[]{:S(2)}, u32[]{:S(2)}) collective-permute-start(bf16[8,48,128]{2,1,0:T(8,128)(2,1)S(1)} %get-tuple-element.53.refs_5_), channel_id=1, source_target_pairs={{0,2},{1,3},{4,6},{5,7},{8,10},{9,11},{12,14},{13,15},{16,18},{17,... | collective-permute-start | bytes 294920 | tf_op jit(solution)/shard_map/ppermute | solution.py:219
  37.0 14.6 %collective-permute-start.14 = (bf16[8,48,128]{2,1,0:T(8,128)(2,1)S(1)}, bf16[8,48,128]{2,1,0:T(8,128)(2,1)S(1)}, u32[]{:S(2)}, u32[]{:S(2)}) collective-permute-start(bf16[8,48,128]{2,1,0:T(8,128)(2,1)S(1)} %get-tuple-element.56.refs_5_), channel_id=1, source_target_pairs={{0,2},{1,3},{4,6},{5,7},{8,10},{9,11},{12,14},{13,15},{16,18},{17,... | collective-permute-start | bytes 294920 | tf_op jit(solution)/shard_map/ppermute | solution.py:219
  38.9 14.4 %collective-permute-start.13 = (bf16[8,48,128]{2,1,0:T(8,128)(2,1)S(1)}, bf16[8,48,128]{2,1,0:T(8,128)(2,1)S(1)}, u32[]{:S(2)}, u32[]{:S(2)}) collective-permute-start(bf16[8,48,128]{2,1,0:T(8,128)(2,1)S(1)} %get-tuple-element.59.refs_5_), channel_id=1, source_target_pairs={{0,2},{1,3},{4,6},{5,7},{8,10},{9,11},{12,14},{13,15},{16,18},{17,... | collective-permute-start | bytes 294920 | tf_op jit(solution)/shard_map/ppermute | solution.py:219
  42.6 16.0 %collective-permute-start.12 = (bf16[8,48,128]{2,1,0:T(8,128)(2,1)S(1)}, bf16[8,48,128]{2,1,0:T(8,128)(2,1)S(1)}, u32[]{:S(2)}, u32[]{:S(2)}) collective-permute-start(bf16[8,48,128]{2,1,0:T(8,128)(2,1)S(1)} %get-tuple-element.62.refs_5_), channel_id=1, source_target_pairs={{0,2},{1,3},{4,6},{5,7},{8,10},{9,11},{12,14},{13,15},{16,18},{17,... | collective-permute-start | bytes 294920 | tf_op jit(solution)/shard_map/ppermute | solution.py:219
  45.6 14.9 %collective-permute-start.11 = (bf16[8,48,128]{2,1,0:T(8,128)(2,1)S(1)}, bf16[8,48,128]{2,1,0:T(8,128)(2,1)S(1)}, u32[]{:S(2)}, u32[]{:S(2)}) collective-permute-start(bf16[8,48,128]{2,1,0:T(8,128)(2,1)S(1)} %get-tuple-element.65.refs_5_), channel_id=1, source_target_pairs={{0,2},{1,3},{4,6},{5,7},{8,10},{9,11},{12,14},{13,15},{16,18},{17,... | collective-permute-start | bytes 294920 | tf_op jit(solution)/shard_map/ppermute | solution.py:219
  48.7 13.6 %collective-permute-start.10 = (bf16[8,48,128]{2,1,0:T(8,128)(2,1)S(1)}, bf16[8,48,128]{2,1,0:T(8,128)(2,1)S(1)}, u32[]{:S(2)}, u32[]{:S(2)}) collective-permute-start(bf16[8,48,128]{2,1,0:T(8,128)(2,1)S(1)} %get-tuple-element.68), channel_id=1, source_target_pairs={{0,2},{1,3},{4,6},{5,7},{8,10},{9,11},{12,14},{13,15},{16,18},{17,... | collective-permute-start | bytes 294920 | tf_op jit(solution)/shard_map/ppermute | solution.py:219
  64.7 7.2 %collective-permute-start.18 = (bf16[2,10,32,128]{3,2,1,0:T(8,128)(2,1)S(1)}, bf16[2,10,32,128]{3,2,1,0:T(8,128)(2,1)S(1)}, u32[]{:S(2)}, u32[]{:S(2)}) collective-permute-start(bf16[2,10,32,128]{3,2,1,0:T(8,128)(2,1)S(1)} %get-tuple-element.94), channel_id=1, source_target_pairs={{0,4},{4,0},{8,12},{12,8},{1,5},{5,1},{9,13},{13,9},{2,6},{6,2},{1... | collective-permute-start | bytes 491528 | tf_op jit(solution)/shard_map/ppermute | solution.py:158
  66.2 10.7 %collective-permute-start.19 = (bf16[2,10,32,128]{3,2,1,0:T(8,128)(2,1)S(1)}, bf16[2,10,32,128]{3,2,1,0:T(8,128)(2,1)S(1)}, u32[]{:S(2)}, u32[]{:S(2)}) collective-permute-start(bf16[2,10,32,128]{3,2,1,0:T(8,128)(2,1)S(1)} %get-tuple-element.93), channel_id=1, source_target_pairs={{0,8},{4,12},{8,0},{12,4},{1,9},{5,13},{9,1},{13,5},{2,10},{6,14},... | collective-permute-start | bytes 491528 | tf_op jit(solution)/shard_map/ppermute | solution.py:158
  66.8 10.1 %collective-permute-start.20 = (bf16[2,10,32,128]{3,2,1,0:T(8,128)(2,1)S(1)}, bf16[2,10,32,128]{3,2,1,0:T(8,128)(2,1)S(1)}, u32[]{:S(2)}, u32[]{:S(2)}) collective-permute-start(bf16[2,10,32,128]{3,2,1,0:T(8,128)(2,1)S(1)} %get-tuple-element.92), channel_id=1, source_target_pairs={{0,12},{4,8},{8,4},{12,0},{1,13},{5,9},{9,5},{13,1},{2,14},{6,10},... | collective-permute-start | bytes 491528 | tf_op jit(solution)/shard_map/ppermute | solution.py:158

commit v2 on v0

v2 whole, which is shorter than its diff:
```python
import functools

import jax
import jax.numpy as jnp
from jax import lax
from jax.experimental import pallas as pl
from jax.experimental.pallas import tpu as pltpu
from jax.sharding import PartitionSpec as P

BF = jnp.bfloat16
F32 = jnp.float32
CHUNK = 1
LAG = 3
FIRST = 3
VMEM_LIMIT = 24 * 1024 * 1024


def round_up(value, unit):
    return -(-value // unit) * unit


def partner(index, hop, count):
    if count & (count - 1) == 0:
        return index ^ hop, index ^ hop
    return (index + hop) % count, (index + count - hop) % count


def sigmoid(value):
    return 0.5 * jnp.tanh(0.5 * value) + 0.5


class Piece:
    def __init__(self, strip, need, begin, band):
        self.extent = round_up(strip + 2 * need, 8)
        self.left = (self.extent - strip) // 2
        self.begin = begin
        self.end = begin + band * self.extent


class Plan:
    def __init__(self, inputs):
        self.steps, self.band, self.columns, self.chans = inputs.shape
        self.count = lax.axis_size("rows")
        self.cols = lax.axis_size("cols")
        self.layers = lax.axis_size("pipe")
        self.grid_columns = self.columns * self.cols
        self.rows_n = self.band * self.count
        self.strip = self.columns // self.count
        most = self.steps + self.layers - 1
        self.pad = round_up(most - 1, 8)
        self.width = round_up(self.strip + 2 * self.pad, 16)
        self.edge = round_up(most + 8, 16)
        self.total = self.rows_n * self.width
        self.first = min(FIRST, self.steps)
        needs = [most, most - 1] + [most - step for step in range(self.steps)]
        split = 2 + self.first
        self.early, self.early_rows = self.pieces(needs[:split])
        self.late, self.late_rows = self.pieces(needs[split:])

    def pieces(self, needs):
        found, begin = [], 0
        for need in needs:
            found.append(Piece(self.strip, need, begin, self.band))
            begin = found[-1].end
        return found, begin


def edge_kernel(plan, hidden_in, cell_in, maps_in, out, hidden, cell, maps, sems):
    edge, columns = plan.edge, plan.columns
    copies = [
        pltpu.make_async_copy(hidden_in, hidden, sems.at[0]),
        pltpu.make_async_copy(cell_in, cell, sems.at[1]),
        pltpu.make_async_copy(maps_in, maps, sems.at[2]),
    ]
    for copy in copies:
        copy.start()
    for copy in copies:
        copy.wait()

    def take(begin):
        out[0] = hidden[0, :, begin : begin + edge]
        out[1] = cell[0, :, begin : begin + edge].astype(BF)
        for step in range(plan.steps):
            out[2 + step] = maps[step, :, begin : begin + edge]

    @pl.when(lax.axis_index("cols") == 0)
    def _():
        take(columns - edge)

    @pl.when(lax.axis_index("cols") != 0)
    def _():
        take(0)


def pack_kernel(plan, pieces, at_edge, hidden, cell, maps, left, right, *refs):
    outs, padded = refs[-1 - plan.count : -1], refs[-1]
    edge, columns, chans, band = plan.edge, plan.columns, plan.chans, plan.band
    place, col = lax.axis_index("rows"), lax.axis_index("cols")
    for number, piece in enumerate(pieces):
        source = at_edge + number
        if source == 0:
            whole = hidden[0]
        elif source == 1:
            whole = cell[0]
        else:
            whole = maps[source - 2]
        before = jnp.where(col > 0, left[source].astype(F32), 0.0)
        after = jnp.where(col < plan.cols - 1, right[source].astype(F32), 0.0)
        padded[number, :, 0:edge] = before
        padded[number, :, edge : edge + columns] = whole.astype(F32)
        padded[number, :, edge + columns : 2 * edge + columns] = after
    for hop in range(plan.count):
        target = partner(place, hop, plan.count)[0]
        for number, piece in enumerate(pieces):
            inset = edge - piece.left
            rest = inset % 8
            start = pl.multiple_of(target * plan.strip + (inset - rest), 8)
            loaded = piece.extent + (8 if rest else 0)
            value = padded[number, :, pl.ds(start, loaded), :]
            if rest:
                value = value.reshape(band * loaded, chans)
                value = pltpu.roll(value, band * loaded - rest, 0)
                value = value.reshape(band, loaded, chans)[:, : piece.extent]
            value = value.reshape(band * piece.extent, chans)
            outs[hop][piece.begin : piece.end] = value.astype(BF)


def takes_early(plan, phase, first_step):
    return first_step == 0 or (phase == 0 and first_step < plan.first)


def takes_late(plan, phase, last_step):
    return phase == 0 and last_step > plan.first


def chunk_kernel(plan, phase, first_step, last_step, *refs):
    refs = list(refs)
    rows_n, band, width, chans = plan.rows_n, plan.band, plan.width, plan.chans
    count, total, steps = plan.count, plan.total, plan.steps
    early = late = None
    if takes_early(plan, phase, first_step):
        early = [refs.pop(0) for _ in range(count)]
    if takes_late(plan, phase, last_step):
        late = [refs.pop(0) for _ in range(count)]
    maps_ref = None if phase == 0 else refs.pop(0)
    hidden_ref = cell_ref = None
    if first_step > 0:
        hidden_ref, cell_ref = refs.pop(0), refs.pop(0)
    weights, bias, _ = refs[:3]
    hidden_out, cell_out, kept, slab = refs[3:]

    @pl.when(lax.axis_index("pipe") == phase)
    def _():
        place = lax.axis_index("rows")
        sources = [partner(place, hop, count)[1] for hop in range(count)]
        start_column = (
            lax.axis_index("cols") * plan.columns + place * plan.strip - plan.pad
        )
        blank = jnp.zeros((width, 6 * chans), BF)
        slab[0:width, :] = blank
        slab[total + width : total + 2 * width, :] = blank

        def spread(lane, value):
            value = value.astype(F32)
            for tap in range(3):
                moved = value if tap == 1 else pltpu.roll(value, (1 - tap) % total, 0)
                at = 2 * chans * tap + lane
                slab[width : width + total, at : at + chans] = moved.astype(BF)

        def bands(lane, refs_in, piece):
            for hop in range(count):
                flat = refs_in[hop][piece.begin : piece.end].astype(F32)
                extent = piece.extent
                if extent < width:
                    flat = flat.reshape(band, extent, chans)
                    fill = jnp.zeros((band, width - extent, chans), F32)
                    flat = jnp.concatenate([flat, fill], axis=1).reshape(band * width, chans)
                    extent = width
                source = sources[hop]
                for tap in range(3) if lane is not None else (1,):
                    shift = (plan.pad - piece.left + 1 - tap) % (band * extent)
                    moved = pltpu.roll(flat, shift, 0) if shift else flat
                    moved = moved.reshape(band, extent, chans)[:, :width]
                    moved = moved.reshape(band * width, chans)
                    if lane is None:
                        start = pl.multiple_of(source * band * width, 16)
                        cell_out[pl.ds(start, band * width), :] = moved
                    else:
                        at = 2 * chans * tap + lane
                        start = pl.multiple_of((source * band + 1) * width, 16)
                        slab[pl.ds(start, band * width), at : at + chans] = moved.astype(BF)

        hidden = None
        cell = None
        for step in range(first_step, last_step):
            if step == 0:
                bands(chans, early, plan.early[0])
                bands(None, early, plan.early[1])
                cell = cell_out[...]
            elif step == first_step:
                spread(chans, hidden_ref[hidden_ref.shape[0] - 1].reshape(total, chans))
                cell = cell_ref[...]
            else:
                spread(chans, hidden.reshape(total, chans))
            if phase > 0:
                spread(0, maps_ref[step - first_step].reshape(total, chans))
            elif step < plan.first:
                bands(0, early, plan.early[2 + step])
            else:
                bands(0, late, plan.late[step - plan.first])

            depth = 6 * chans
            gates = bias[...]
            for tap in range(3):
                gates = gates + jnp.dot(
                    slab[tap * width : tap * width + total, :],
                    weights[tap * depth : (tap + 1) * depth, :],
                    preferred_element_type=F32,
                )
            cell = sigmoid(gates[:, chans : 2 * chans]) * cell + sigmoid(
                gates[:, :chans]
            ) * jnp.tanh(gates[:, 2 * chans : 3 * chans])
            hidden = sigmoid(gates[:, 3 * chans :]) * jnp.tanh(cell)
            hidden = hidden.reshape(rows_n, width, chans)
            column = start_column + lax.broadcasted_iota(jnp.int32, hidden.shape, 1)
            inside = jnp.logical_and(column >= 0, column < plan.grid_columns)
            hidden = jnp.where(inside, hidden, 0.0).astype(BF)
            hidden_out[step - first_step] = hidden
            kept[:, step] = hidden
        cell_out[...] = cell
        if last_step == steps:
            kept[:, steps] = cell.astype(BF).reshape(rows_n, width, chans)


def advance(plan, phase, first_step, last_step, feed, kept):
    vmem = pl.BlockSpec(memory_space=pltpu.VMEM)
    operands = [*feed, kept]
    chunk = last_step - first_step
    return pl.pallas_call(
        functools.partial(chunk_kernel, plan, phase, first_step, last_step),
        out_shape=(
            jax.ShapeDtypeStruct((chunk, plan.rows_n, plan.width, plan.chans), BF),
            jax.ShapeDtypeStruct((plan.total, plan.chans), F32),
            jax.ShapeDtypeStruct(kept.shape, kept.dtype),
        ),
        in_specs=[vmem] * len(operands),
        out_specs=(vmem, vmem, vmem),
        scratch_shapes=[pltpu.VMEM((plan.total + 2 * plan.width, 6 * plan.chans), BF)],
        input_output_aliases={len(operands) - 1: 2},
        compiler_params=pltpu.CompilerParams(vmem_limit_bytes=VMEM_LIMIT),
        cost_estimate=pl.CostEstimate(
            flops=2 * chunk * plan.total * 18 * plan.chans * 4 * plan.chans,
            bytes_accessed=1000000,
            transcendentals=5 * chunk * plan.total * plan.chans,
        ),
    )(*operands)


def pack(plan, pieces, rows, at_edge, arrays, after=()):
    vmem = pl.BlockSpec(memory_space=pltpu.VMEM)
    shape = (len(pieces), plan.band, plan.columns + 2 * plan.edge, plan.chans)
    return pl.pallas_call(
        functools.partial(pack_kernel, plan, pieces, at_edge),
        out_shape=(jax.ShapeDtypeStruct((rows, plan.chans), BF),) * plan.count,
        in_specs=[vmem] * len(arrays) + [pl.BlockSpec(memory_space=pl.ANY)] * len(after),
        out_specs=(vmem,) * plan.count,
        scratch_shapes=[pltpu.VMEM(shape, F32)],
        compiler_params=pltpu.CompilerParams(vmem_limit_bytes=VMEM_LIMIT),
    )(*arrays, *after)


def exchange(plan, pieces):
    got = [pieces[0]]
    for hop in range(1, plan.count):
        route = [(n, partner(n, hop, plan.count)[0]) for n in range(plan.count)]
        got.append(lax.ppermute(pieces[hop], "rows", route))
    return got


def shards(inputs, hidden_init, cell_init, kernels, biases):
    plan = Plan(inputs)
    place = lax.axis_index("rows")
    steps, band, chans, count, layers = (
        plan.steps,
        plan.band,
        plan.chans,
        plan.count,
        plan.layers,
    )
    weights, bias = kernels[0], biases

    if plan.cols == 2:
        vmem = pl.BlockSpec(memory_space=pltpu.VMEM)
        anywhere = pl.BlockSpec(memory_space=pl.ANY)
        sources = (hidden_init, cell_init, inputs)
        beside, *sources = pl.pallas_call(
            functools.partial(edge_kernel, plan),
            out_shape=[jax.ShapeDtypeStruct((2 + steps, band, plan.edge, chans), BF)]
            + [jax.ShapeDtypeStruct(source.shape, source.dtype) for source in sources],
            in_specs=[anywhere] * 3,
            out_specs=[vmem] * 4,
            scratch_shapes=[pltpu.SemaphoreType.DMA((3,))],
            compiler_params=pltpu.CompilerParams(vmem_limit_bytes=VMEM_LIMIT),
        )(*sources)
        left = right = lax.ppermute(beside, "cols", [(0, 1), (1, 0)])
    else:
        sources = (hidden_init, cell_init, inputs)
        maps = jnp.concatenate([hidden_init, cell_init.astype(BF), inputs], axis=0)
        ring = [(n, (n + 1) % plan.cols) for n in range(plan.cols)]
        left = lax.ppermute(maps[:, :, plan.columns - plan.edge :], "cols", ring)
        right = lax.ppermute(maps[:, :, : plan.edge], "cols", [(b, a) for a, b in ring])
    arrays = [*sources, left, right]
    early_pieces = pack(plan, plan.early, plan.early_rows, 0, arrays)
    early = exchange(plan, early_pieces)
    late_pieces = pack(
        plan, plan.late, plan.late_rows, len(plan.early), arrays, early_pieces[:1]
    )
    late = exchange(plan, late_pieces)

    kept = jnp.zeros((plan.rows_n, steps + 1, plan.width, chans), BF)
    chunks = [(first, min(first + CHUNK, steps)) for first in range(0, steps, CHUNK)]
    order = sorted(
        (number + LAG * phase, -phase, number)
        for phase in range(layers)
        for number in range(len(chunks))
    )
    state = [[] for _ in range(layers)]
    sent = {}
    for _, minus_phase, number in order:
        phase = -minus_phase
        first_step, last_step = chunks[number]
        feed = list(early) if takes_early(plan, phase, first_step) else []
        feed += late if takes_late(plan, phase, last_step) else []
        feed += [sent[phase - 1, number]] if phase > 0 else []
        feed += state[phase]
        hidden, cell, kept = advance(
            plan, phase, first_step, last_step, feed + [weights, bias], kept
        )
        state[phase] = [hidden, cell]
        if phase < layers - 1:
            ring = [(n, (n + 1) % layers) for n in range(layers)]
            sent[phase, number] = lax.ppermute(hidden, "pipe", ring)

    def out_piece(hop):
        target = partner(place, hop, count)[0]
        piece = lax.dynamic_slice_in_dim(kept, target * band, band, axis=0)
        return piece[:, :, plan.pad : plan.pad + plan.strip]

    out = jnp.zeros((band, steps + 1, plan.columns, chans), BF)
    for hop, piece in enumerate(exchange(plan, [out_piece(hop) for hop in range(count)])):
        source = partner(place, hop, count)[1]
        out = lax.dynamic_update_slice_in_dim(out, piece, source * plan.strip, axis=2)
    produced = jnp.swapaxes(out[:, :steps], 0, 1)
    final = out[:, steps].astype(F32)
    return produced[None], final[None]


def solution(mesh):
    return jax.shard_map(
        shards,
        mesh=mesh,
        in_specs=(
            P(None, ("groups", "rows"), "cols", None),
            P("pipe", ("groups", "rows"), "cols", None),
            P("pipe", ("groups", "rows"), "cols", None),
            P("pipe", None, None),
            P("pipe", None),
        ),
        out_specs=(
            P("pipe", None, ("groups", "rows"), "cols", None),
            P("pipe", ("groups", "rows"), "cols", None),
        ),
        check_vma=False,
    )
```

time: 213 us -> 66.8 us (0.31); the launches traced: 209 us -> 65.6 us
  starting transfers between devices: 106 us -> 31.9 us
  waiting for transfers between devices: 67.9 us -> 14.3 us
  Pallas kernels: 0 us -> 12 us
  other arithmetic: 10.6 us -> 0.66 us
  local copies, waits for them, and re-layouts: 15.7 us -> 5.85 us
  matrix products: 6.15 us -> 0 us
    ppermute x45 -> x18, starting transfers between devices: 106 us -> 31.9 us  [the longest x9 20.3 us: exchange(): got.append(lax.ppermute(pieces[hop], 'rows', route))]
    ppermute x45 -> x18, waiting for transfers between devices: 67.9 us -> 14.3 us  [the longest x9 11 us: exchange(): got.append(lax.ppermute(pieces[hop], 'rows', route))]
    cond x80 -> x0, local copies, waits for them, and re-layouts: 12.4 us -> none
    pallas_call x0 -> x19, Pallas kernels: none -> 12 us  [the longest x16 10.8 us: advance(): pl.pallas_call(functools.partial(chunk_kernel, plan, phase, first_step, l...]
    select_n x9 -> x0, other arithmetic: 7.64 us -> none  [section(): x_map = jnp.where(layer_idx == 0, own_input, incoming)]
    dot_general x8 -> x0, matrix products: 6.15 us -> none  [gate_values(): total = jnp.dot(slab, weights, preferred_element_type=jnp.float32)]
    unnamed x6 -> x14, local copies, waits for them, and re-layouts: 2.57 us -> 4.66 us
  transfers between devices with their start and end apart: 45 -> 18, of which waited for: 36 -> 8; matrix products, arithmetic and copies ran while one was open for 0% -> 0% of each run, Pallas kernels for 0% -> 14%
where the time goes in v2:
time: 66.8 us; the launch traced here: 65.6 us
  starting transfers between devices  31.9 us (48%)
  waiting for transfers between devices  14.3 us (21%)
  Pallas kernels  12 us (18%)
  local copies, waits for them, and re-layouts  5.85 us (9%)
  between operations  0.85 us (1%)
    ppermute x9, starting transfers between devices, exchange(): got.append(lax.ppermute(pieces[hop], 'rows', route))  20.3 us
    ppermute x8, starting transfers between devices, shards(): sent[phase, number] = lax.ppermute(hidden, 'pipe', ring)  11.6 us
    ppermute x9, waiting for transfers between devices, exchange(): got.append(lax.ppermute(pieces[hop], 'rows', route))  11 us
    pallas_call x16, Pallas kernels, advance(): pl.pallas_call(functools.partial(chunk_kernel, plan, phase, first_step, l...  10.8 us
    unnamed x14, local copies, waits for them, and re-layouts  4.66 us
    ppermute x8, waiting for transfers between devices, shards(): sent[phase, number] = lax.ppermute(hidden, 'pipe', ring)  1.93 us
    ppermute x1, waiting for transfers between devices, shards(): left = right = lax.ppermute(beside, 'cols', [(0, 1), (1, 0)])  1.38 us
  transfers between devices with their start and end apart: 18, of which 8 were waited for; matrix products, arithmetic and copies ran while one was open for 0% of the time, Pallas kernels for 14%

profile of v2, /device:TPU:6, one launch (start us, length us, event | category | flops | bytes accessed | tf_op | source)
XLA Modules:
  0.0 65.6 jit_solution(15692473219720161168)
XLA Ops:
  0.6 0.0 copy-start
  0.6 0.0 copy-start.4
  0.7 1.2 %copy-done.4 = bf16[8,2,128,128]{3,2,1,0:T(8,128)(2,1)S(1)} copy-done((bf16[8,2,128,128]{3,2,1,0:T(8,128)(2,1)S(1)}, bf16[8,2,128,128]{3,2,1,0:T(8,128)(2,1)}, u32[]{:S(2)}) %copy-start.4) | copy-done | bytes 524312
  1.8 0.0 copy-start.5
  1.8 0.9 %copy-done.5 = f32[1,2,128,128]{3,2,1,0:T(8,128)S(1)} copy-done((f32[1,2,128,128]{3,2,1,0:T(8,128)S(1)}, f32[1,2,128,128]{3,2,1,0:T(8,128)}, u32[]{:S(2)}) %copy-start.5) | copy-done | bytes 131096
  2.7 0.8 %copy-done.6 = bf16[1,2,128,128]{3,2,1,0:T(8,128)(2,1)S(1)} copy-done((bf16[1,2,128,128]{3,2,1,0:T(8,128)(2,1)S(1)}, bf16[1,2,128,128]{3,2,1,0:T(8,128)(2,1)}, u32[]{:S(2)}) %copy-start.6) | copy-done | bytes 65560
  3.6 0.3 shard_map.68
  3.9 0.0 copy-start.1
  3.9 0.1 collective-permute-start
  4.0 1.4 %collective-permute-done.left.right = bf16[10,2,32,128]{3,2,1,0:T(8,128)(2,1)S(1)} collective-permute-done((bf16[10,2,32,128]{3,2,1,0:T(8,128)(2,1)S(1)}, bf16[10,2,32,128]{3,2,1,0:T(8,128)(2,1)S(1)}, u32[]{:S(2)}, u32[]{:S(2)}) %collective-permute-start) | collective-permute-done | bytes 163872 | tf_op jit(solution)/shard_map/ppermute | solution.py:305
  5.4 0.8 %shard_map.69 = (bf16[512,128]{1,0:T(8,128)(2,1)S(1)}, bf16[512,128]{1,0:T(8,128)(2,1)}, bf16[512,128]{1,0:T(8,128)(2,1)S(1)}, bf16[512,128]{1,0:T(8,128)(2,1)S(1)}) custom-call(bf16[1,2,128,128]{3,2,1,0:T(8,128)(2,1)S(1)} %get-tuple-element.59.hidden, f32[1,2,128,128]{3,2,1,0:T(8,128)S(1)} %get-tuple-element.60.cell, ...), custom_call_target="tpu_custom_call" | custom-call | tf_op jit(solution)/shard_map/pallas_call | solution.py:262
  6.2 1.6 %collective-permute-start.4 = (bf16[512,128]{1,0:T(8,128)(2,1)}, bf16[512,128]{1,0:T(8,128)(2,1)S(1)}, u32[]{:S(2)}, u32[]{:S(2)}) collective-permute-start(bf16[512,128]{1,0:T(8,128)(2,1)} %get-tuple-element.68), channel_id=1, source_target_pairs={{0,4},{4,0},{8,12},{12,8},{1,5},{5,1},{9,13},{13,9},{2,6},{6,2},{1... | collective-permute-start | bytes 393224 | tf_op jit(solution)/shard_map/ppermute | solution.py:276
  7.7 2.6 %collective-permute-start.5 = (bf16[512,128]{1,0:T(8,128)(2,1)S(1)}, bf16[512,128]{1,0:T(8,128)(2,1)S(1)}, u32[]{:S(2)}, u32[]{:S(2)}) collective-permute-start(bf16[512,128]{1,0:T(8,128)(2,1)S(1)} %get-tuple-element.69), channel_id=1, source_target_pairs={{0,8},{4,12},{8,0},{12,4},{1,9},{5,13},{9,1},{13,5},{2,10},{6,14},... | collective-permute-start | bytes 393224 | tf_op jit(solution)/shard_map/ppermute | solution.py:276
  10.3 0.0 copy-done.1
  10.3 0.2 collective-permute-start.6
  10.5 1.0 %copy-done.2 = bf16[8,2,128,128]{3,2,1,0:T(8,128)(2,1)S(1)} copy-done((bf16[8,2,128,128]{3,2,1,0:T(8,128)(2,1)S(1)}, bf16[8,2,128,128]{3,2,1,0:T(8,128)(2,1)}, u32[]{:S(2)}) %copy-start.2) | copy-done | bytes 524312
  11.6 0.1 shard_map.70
  11.7 0.7 %collective-permute-start.1 = (bf16[432,128]{1,0:T(8,128)(2,1)S(1)}, bf16[432,128]{1,0:T(8,128)(2,1)S(1)}, u32[]{:S(2)}, u32[]{:S(2)}) collective-permute-start(bf16[432,128]{1,0:T(8,128)(2,1)S(1)} %get-tuple-element.65), channel_id=1, source_target_pairs={{0,4},{4,0},{8,12},{12,8},{1,5},{5,1},{9,13},{13,9},{2,6},{6,2},{1... | collective-permute-start | bytes 331784 | tf_op jit(solution)/shard_map/ppermute | solution.py:276
  12.5 3.5 %collective-permute-start.2 = (bf16[432,128]{1,0:T(8,128)(2,1)S(1)}, bf16[432,128]{1,0:T(8,128)(2,1)S(1)}, u32[]{:S(2)}, u32[]{:S(2)}) collective-permute-start(bf16[432,128]{1,0:T(8,128)(2,1)S(1)} %get-tuple-element.66), channel_id=1, source_target_pairs={{0,8},{4,12},{8,0},{12,4},{1,9},{5,13},{9,1},{13,5},{2,10},{6,14},... | collective-permute-start | bytes 331784 | tf_op jit(solution)/shard_map/ppermute | solution.py:276
  15.9 0.0 collective-permute-done.4.refs_1_
  15.9 1.3 %collective-permute-start.3 = (bf16[432,128]{1,0:T(8,128)(2,1)S(1)}, bf16[432,128]{1,0:T(8,128)(2,1)S(1)}, u32[]{:S(2)}, u32[]{:S(2)}) collective-permute-start(bf16[432,128]{1,0:T(8,128)(2,1)S(1)} %get-tuple-element.67), channel_id=1, source_target_pairs={{0,12},{4,8},{8,4},{12,0},{1,13},{5,9},{9,5},{13,1},{2,14},{6,10},... | collective-permute-start | bytes 331784 | tf_op jit(solution)/shard_map/ppermute | solution.py:276
  17.3 3.3 %collective-permute-done.5.refs_2_ = bf16[512,128]{1,0:T(8,128)(2,1)S(1)} collective-permute-done((bf16[512,128]{1,0:T(8,128)(2,1)S(1)}, bf16[512,128]{1,0:T(8,128)(2,1)S(1)}, u32[]{:S(2)}, u32[]{:S(2)}) %collective-permute-start.5) | collective-permute-done | bytes 131104 | tf_op jit(solution)/shard_map/ppermute | solution.py:276
  20.6 0.0 collective-permute-done.6.refs_3_
  20.6 0.1 broadcast_in_dim.11.refs_6_
  20.7 0.0 copy-done
  20.8 0.0 copy-start.3
  20.8 0.7 %copy-done.3 = f32[1,512]{1,0:T(1,128)S(1)} copy-done((f32[1,512]{1,0:T(1,128)S(1)}, f32[1,512]{1,0:T(1,128)}, u32[]{:S(2)}) %copy-start.3) | copy-done | bytes 2072
  21.4 1.9 %collective-permute-start.7 = (bf16[1,8,48,128]{3,2,1,0:T(8,128)(2,1)S(1)}, bf16[1,8,48,128]{3,2,1,0:T(8,128)(2,1)S(1)}, u32[]{:S(2)}, u32[]{:S(2)}) collective-permute-start(bf16[1,8,48,128]{3,2,1,0:T(8,128)(2,1)S(1)} %get-tuple-element.71.refs_4_), channel_id=1, source_target_pairs={{0,2},{2,0},{1,3},{3,1},{4,6},{6,4},{5,7},{7,5},{8,10},{10,8},{9,1... | collective-permute-start | bytes 294920 | tf_op jit(solution)/shard_map/ppermute | solution.py:342
  23.3 1.5 %collective-permute-start.8 = (bf16[1,8,48,128]{3,2,1,0:T(8,128)(2,1)S(1)}, bf16[1,8,48,128]{3,2,1,0:T(8,128)(2,1)S(1)}, u32[]{:S(2)}, u32[]{:S(2)}) collective-permute-start(bf16[1,8,48,128]{3,2,1,0:T(8,128)(2,1)S(1)} %get-tuple-element.74.refs_4_), channel_id=1, source_target_pairs={{0,2},{2,0},{1,3},{3,1},{4,6},{6,4},{5,7},{7,5},{8,10},{10,8},{9,1... | collective-permute-start | bytes 294920 | tf_op jit(solution)/shard_map/ppermute | solution.py:342
  24.8 1.4 %collective-permute-done.7.refs_4_ = bf16[1,8,48,128]{3,2,1,0:T(8,128)(2,1)S(1)} collective-permute-done((bf16[1,8,48,128]{3,2,1,0:T(8,128)(2,1)S(1)}, bf16[1,8,48,128]{3,2,1,0:T(8,128)(2,1)S(1)}, u32[]{:S(2)}, u32[]{:S(2)}) %collective-permute-start.7) | collective-permute-done | bytes 98336 | tf_op jit(solution)/shard_map/ppermute | solution.py:342
  26.2 2.0 %collective-permute-start.9 = (bf16[1,8,48,128]{3,2,1,0:T(8,128)(2,1)S(1)}, bf16[1,8,48,128]{3,2,1,0:T(8,128)(2,1)S(1)}, u32[]{:S(2)}, u32[]{:S(2)}) collective-permute-start(bf16[1,8,48,128]{3,2,1,0:T(8,128)(2,1)S(1)} %get-tuple-element.77.refs_4_), channel_id=1, source_target_pairs={{0,2},{2,0},{1,3},{3,1},{4,6},{6,4},{5,7},{7,5},{8,10},{10,8},{9,1... | collective-permute-start | bytes 294920 | tf_op jit(solution)/shard_map/ppermute | solution.py:342
  28.2 1.2 %shard_map.74 = (bf16[1,8,48,128]{3,2,1,0:T(8,128)(2,1)S(1)}, f32[384,128]{1,0:T(8,128)S(1)}, bf16[8,9,48,128]{3,2,1,0:T(8,128)(2,1)S(1)}) custom-call(bf16[512,128]{1,0:T(8,128)(2,1)S(1)} %get-tuple-element.63.refs_0_, bf16[512,128]{1,0:T(8,128)(2,1)S(1)} %collective-permute-done.4.refs_1_, ...), custom_call_target="tpu_custom_call", output_to_operand_aliasing={{2}: (7, {})} | custom-call | flops 905969664 | bytes 1000000 | tf_op jit(solution)/shard_map/pallas_call | solution.py:239
  29.4 0.0 collective-permute-done.1.refs_1_
  29.5 1.1 %collective-permute-done.2.refs_2_ = bf16[432,128]{1,0:T(8,128)(2,1)S(1)} collective-permute-done((bf16[432,128]{1,0:T(8,128)(2,1)S(1)}, bf16[432,128]{1,0:T(8,128)(2,1)S(1)}, u32[]{:S(2)}, u32[]{:S(2)}) %collective-permute-start.2) | collective-permute-done | bytes 110624 | tf_op jit(solution)/shard_map/ppermute | solution.py:276
  30.5 0.0 collective-permute-done.3.refs_3_
  30.5 1.9 %collective-permute-start.10 = (bf16[1,8,48,128]{3,2,1,0:T(8,128)(2,1)S(1)}, bf16[1,8,48,128]{3,2,1,0:T(8,128)(2,1)S(1)}, u32[]{:S(2)}, u32[]{:S(2)}) collective-permute-start(bf16[1,8,48,128]{3,2,1,0:T(8,128)(2,1)S(1)} %get-tuple-element.81.refs_4_), channel_id=1, source_target_pairs={{0,2},{2,0},{1,3},{3,1},{4,6},{6,4},{5,7},{7,5},{8,10},{10,8},{9,1... | collective-permute-start | bytes 294920 | tf_op jit(solution)/shard_map/ppermute | solution.py:342
  32.4 0.0 collective-permute-done.8.refs_0_
  32.4 1.2 %shard_map.76 = (bf16[1,8,48,128]{3,2,1,0:T(8,128)(2,1)S(1)}, f32[384,128]{1,0:T(8,128)S(1)}, bf16[8,9,48,128]{3,2,1,0:T(8,128)(2,1)S(1)}) custom-call(bf16[1,8,48,128]{3,2,1,0:T(8,128)(2,1)S(1)} %collective-permute-done.8.refs_0_, bf16[1,8,48,128]{3,2,1,0:T(8,128)(2,1)S(1)} %get-tuple-element.83.refs_1_, ...), custom_call_target="tpu_custom_call", output_to_operand_aliasing={{2}: (5, {})} | custom-call | flops 905969664 | bytes 1000000 | tf_op jit(solution)/shard_map/pallas_call | solution.py:239
  33.6 0.3 collective-permute-start.11
  33.9 0.0 collective-permute-done.9.refs_0_
  33.9 1.2 %shard_map.78 = (bf16[1,8,48,128]{3,2,1,0:T(8,128)(2,1)S(1)}, f32[384,128]{1,0:T(8,128)S(1)}, bf16[8,9,48,128]{3,2,1,0:T(8,128)(2,1)S(1)}) custom-call(bf16[1,8,48,128]{3,2,1,0:T(8,128)(2,1)S(1)} %collective-permute-done.9.refs_0_, bf16[1,8,48,128]{3,2,1,0:T(8,128)(2,1)S(1)} %get-tuple-element.89.refs_1_, ...), custom_call_target="tpu_custom_call", output_to_operand_aliasing={{2}: (5, {})} | custom-call | flops 905969664 | bytes 1000000 | tf_op jit(solution)/shard_map/pallas_call | solution.py:239
  35.1 1.9 %collective-permute-start.14 = (bf16[1,8,48,128]{3,2,1,0:T(8,128)(2,1)S(1)}, bf16[1,8,48,128]{3,2,1,0:T(8,128)(2,1)S(1)}, u32[]{:S(2)}, u32[]{:S(2)}) collective-permute-start(bf16[1,8,48,128]{3,2,1,0:T(8,128)(2,1)S(1)} %get-tuple-element.93.refs_4_), channel_id=1, source_target_pairs={{0,2},{2,0},{1,3},{3,1},{4,6},{6,4},{5,7},{7,5},{8,10},{10,8},{9,1... | collective-permute-start | bytes 294920 | tf_op jit(solution)/shard_map/ppermute | solution.py:342
  37.0 0.0 collective-permute-done.10.refs_0_
  37.0 1.2 %shard_map.80 = (bf16[1,8,48,128]{3,2,1,0:T(8,128)(2,1)S(1)}, f32[384,128]{1,0:T(8,128)S(1)}, bf16[8,9,48,128]{3,2,1,0:T(8,128)(2,1)S(1)}) custom-call(bf16[1,8,48,128]{3,2,1,0:T(8,128)(2,1)S(1)} %collective-permute-done.10.refs_0_, bf16[1,8,48,128]{3,2,1,0:T(8,128)(2,1)S(1)} %get-tuple-element.95.refs_1_, ...), custom_call_target="tpu_custom_call", output_to_operand_aliasing={{2}: (5, {})} | custom-call | flops 905969664 | bytes 1000000 | tf_op jit(solution)/shard_map/pallas_call | solution.py:239
  38.2 0.3 collective-permute-start.13
  38.5 0.1 collective-permute-done.11.refs_0_
  38.6 1.2 %shard_map.82 = (bf16[1,8,48,128]{3,2,1,0:T(8,128)(2,1)S(1)}, f32[384,128]{1,0:T(8,128)S(1)}, bf16[8,9,48,128]{3,2,1,0:T(8,128)(2,1)S(1)}) custom-call(bf16[1,8,48,128]{3,2,1,0:T(8,128)(2,1)S(1)} %collective-permute-done.11.refs_0_, bf16[1,8,48,128]{3,2,1,0:T(8,128)(2,1)S(1)} %get-tuple-element.101.refs_1_, ...), custom_call_target="tpu_custom_call", output_to_operand_aliasing={{2}: (5, {})} | custom-call | flops 905969664 | bytes 1000000 | tf_op jit(solution)/shard_map/pallas_call | solution.py:239
  39.7 0.7 %shard_map.83 = (bf16[1,8,48,128]{3,2,1,0:T(8,128)(2,1)S(1)}, f32[384,128]{1,0:T(8,128)}, bf16[8,9,48,128]{3,2,1,0:T(8,128)(2,1)S(1)}) custom-call(bf16[432,128]{1,0:T(8,128)(2,1)S(1)} %get-tuple-element.64.refs_0_, bf16[432,128]{1,0:T(8,128)(2,1)S(1)} %collective-permute-done.1.refs_1_, ...), custom_call_target="tpu_custom_call", output_to_operand_aliasing={{2}: (8, {})} | custom-call | flops 905969664 | bytes 1000000 | tf_op jit(solution)/shard_map/pallas_call | solution.py:239
  40.4 1.8 %collective-permute-start.12 = (bf16[1,8,48,128]{3,2,1,0:T(8,128)(2,1)S(1)}, bf16[1,8,48,128]{3,2,1,0:T(8,128)(2,1)S(1)}, u32[]{:S(2)}, u32[]{:S(2)}) collective-permute-start(bf16[1,8,48,128]{3,2,1,0:T(8,128)(2,1)S(1)} %get-tuple-element.105), channel_id=1, source_target_pairs={{0,2},{2,0},{1,3},{3,1},{4,6},{6,4},{5,7},{7,5},{8,10},{10,8},{9,1... | collective-permute-start | bytes 294920 | tf_op jit(solution)/shard_map/ppermute | solution.py:342
  42.3 0.0 collective-permute-done.14.refs_0_
  42.3 1.2 %shard_map.84 = (bf16[1,8,48,128]{3,2,1,0:T(8,128)(2,1)S(1)}, f32[384,128]{1,0:T(8,128)S(1)}, bf16[8,9,48,128]{3,2,1,0:T(8,128)(2,1)S(1)}) custom-call(bf16[1,8,48,128]{3,2,1,0:T(8,128)(2,1)S(1)} %collective-permute-done.14.refs_0_, bf16[1,8,48,128]{3,2,1,0:T(8,128)(2,1)S(1)} %get-tuple-element.106.refs_1_, ...), custom_call_target="tpu_custom_call", output_to_operand_aliasing={{2}: (5, {})} | custom-call | flops 905969664 | bytes 1000000 | tf_op jit(solution)/shard_map/pallas_call | solution.py:239
  43.4 0.0 collective-permute-done.13.refs_0_
  43.4 1.2 %shard_map.85 = (bf16[1,8,48,128]{3,2,1,0:T(8,128)(2,1)S(1)}, f32[384,128]{1,0:T(8,128)S(1)}, bf16[8,9,48,128]{3,2,1,0:T(8,128)(2,1)S(1)}) custom-call(bf16[1,8,48,128]{3,2,1,0:T(8,128)(2,1)S(1)} %collective-permute-done.13.refs_0_, bf16[1,8,48,128]{3,2,1,0:T(8,128)(2,1)S(1)} %get-tuple-element.109.refs_1_, ...), custom_call_target="tpu_custom_call", output_to_operand_aliasing={{2}: (5, {})} | custom-call | flops 905969664 | bytes 1000000 | tf_op jit(solution)/shard_map/pallas_call | solution.py:239
  44.6 0.4 collective-permute-done.12.refs_0_
  45.1 1.9 %shard_map.86 = (bf16[1,8,48,128]{3,2,1,0:T(8,128)(2,1)}, f32[384,128]{1,0:T(8,128)}, bf16[8,9,48,128]{3,2,1,0:T(8,128)(2,1)S(1)}) custom-call(bf16[1,8,48,128]{3,2,1,0:T(8,128)(2,1)S(1)} %collective-permute-done.12.refs_0_, bf16[1,8,48,128]{3,2,1,0:T(8,128)(2,1)S(1)} %get-tuple-element.112.refs_1_, ...), custom_call_target="tpu_custom_call", output_to_operand_aliasing={{2}: (5, {})} | custom-call | flops 905969664 | bytes 1000000 | tf_op jit(solution)/shard_map/pallas_call | solution.py:239
  47.0 7.9 %collective-permute-start.15 = (bf16[2,9,32,128]{3,2,1,0:T(8,128)(2,1)S(1)}, bf16[2,9,32,128]{3,2,1,0:T(8,128)(2,1)S(1)}, u32[]{:S(2)}, u32[]{:S(2)}) collective-permute-start(bf16[2,9,32,128]{3,2,1,0:T(8,128)(2,1)S(1)} %get-tuple-element.118), channel_id=1, source_target_pairs={{0,4},{4,0},{8,12},{12,8},{1,5},{5,1},{9,13},{13,9},{2,6},{6,2},{1... | collective-permute-start | bytes 442376 | tf_op jit(solution)/shard_map/ppermute | solution.py:276
  54.9 0.5 collective-permute-start.16
  55.3 2.0 %collective-permute-start.17 = (bf16[2,9,32,128]{3,2,1,0:T(8,128)(2,1)S(1)}, bf16[2,9,32,128]{3,2,1,0:T(8,128)(2,1)S(1)}, u32[]{:S(2)}, u32[]{:S(2)}) collective-permute-start(bf16[2,9,32,128]{3,2,1,0:T(8,128)(2,1)S(1)} %get-tuple-element.116), channel_id=1, source_target_pairs={{0,12},{4,8},{8,4},{12,0},{1,13},{5,9},{9,5},{13,1},{2,14},{6,10},... | collective-permute-start | bytes 442376 | tf_op jit(solution)/shard_map/ppermute | solution.py:276
  57.3 0.1 broadcast_in_dim.10
  57.5 1.3 %collective-permute-done.15 = bf16[2,9,32,128]{3,2,1,0:T(8,128)(2,1)S(1)} collective-permute-done((bf16[2,9,32,128]{3,2,1,0:T(8,128)(2,1)S(1)}, bf16[2,9,32,128]{3,2,1,0:T(8,128)(2,1)S(1)}, u32[]{:S(2)}, u32[]{:S(2)}) %collective-permute-start.15) | collective-permute-done | bytes 147488 | tf_op jit(solution)/shard_map/ppermute | solution.py:276
  58.8 5.3 %collective-permute-done.16 = bf16[2,9,32,128]{3,2,1,0:T(8,128)(2,1)S(1)} collective-permute-done((bf16[2,9,32,128]{3,2,1,0:T(8,128)(2,1)S(1)}, bf16[2,9,32,128]{3,2,1,0:T(8,128)(2,1)S(1)}, u32[]{:S(2)}, u32[]{:S(2)}) %collective-permute-start.16) | collective-permute-done | bytes 147488 | tf_op jit(solution)/shard_map/ppermute | solution.py:276
  64.1 0.0 collective-permute-done.17
  64.1 0.8 %slice_bitcast_fusion = bf16[1,8,2,128,128]{4,3,2,1,0:T(8,128)(2,1)} fusion(bf16[2,9,128,128]{3,2,0,1:T(8,128)(2,1)S(1)} %copy_dynamic-update-slice_fusion), kind=kLoop, calls=%fused_computation | loop fusion | bytes 1048576 | tf_op jit(solution)/shard_map/broadcast_in_dim | solution.py:355
  65.0 0.7 %fusion = f32[1,2,128,128]{3,2,1,0:T(8,128)} fusion(bf16[2,9,128,128]{3,2,0,1:T(8,128)(2,1)S(1)} %copy_dynamic-update-slice_fusion), kind=kLoop, calls=%fused_computation.6 | loop fusion | flops 32768 | bytes 196608 | tf_op jit(solution)/shard_map/convert_element_type | solution.py:354
  (14 shorter events, 0.2 us)
Async XLA Ops:
  0.6 20.1 %copy-start = (bf16[1,2304,512]{2,1,0:T(8,128)(2,1)S(1)}, bf16[1,2304,512]{2,1,0:T(8,128)(2,1)}, u32[]{:S(2)}) copy-start(bf16[1,2304,512]{2,1,0:T(8,128)(2,1)} %param.8) | copy-start | bytes 7077892
  0.6 1.2 %copy-start.4 = (bf16[8,2,128,128]{3,2,1,0:T(8,128)(2,1)S(1)}, bf16[8,2,128,128]{3,2,1,0:T(8,128)(2,1)}, u32[]{:S(2)}) copy-start(bf16[8,2,128,128]{3,2,1,0:T(8,128)(2,1)} %maps_in.1) | copy-start | bytes 1572868
  1.8 0.9 %copy-start.5 = (f32[1,2,128,128]{3,2,1,0:T(8,128)S(1)}, f32[1,2,128,128]{3,2,1,0:T(8,128)}, u32[]{:S(2)}) copy-start(f32[1,2,128,128]{3,2,1,0:T(8,128)} %cell_in.1) | copy-start | bytes 393220
  2.7 0.8 %copy-start.6 = (bf16[1,2,128,128]{3,2,1,0:T(8,128)(2,1)S(1)}, bf16[1,2,128,128]{3,2,1,0:T(8,128)(2,1)}, u32[]{:S(2)}) copy-start(bf16[1,2,128,128]{3,2,1,0:T(8,128)(2,1)} %hidden_in.1) | copy-start | bytes 196612
  3.9 6.4 %copy-start.1 = (bf16[8,2,128,128]{3,2,1,0:T(8,128)(2,1)}, bf16[8,2,128,128]{3,2,1,0:T(8,128)(2,1)S(1)}, u32[]{:S(2)}) copy-start(bf16[8,2,128,128]{3,2,1,0:T(8,128)(2,1)S(1)} %get-tuple-element.61.maps) | copy-start | bytes 1572868
  3.9 1.5 %collective-permute-start = (bf16[10,2,32,128]{3,2,1,0:T(8,128)(2,1)S(1)}, bf16[10,2,32,128]{3,2,1,0:T(8,128)(2,1)S(1)}, u32[]{:S(2)}, u32[]{:S(2)}) collective-permute-start(bf16[10,2,32,128]{3,2,1,0:T(8,128)(2,1)S(1)} %get-tuple-element.62), channel_id=1, source_target_pairs={{0,1},{1,0},{2,3},{3,2},{4,5},{5,4},{6,7},{7,6},{8,9},{9,8},{10,11... | collective-permute-start | bytes 491528 | tf_op jit(solution)/shard_map/ppermute | solution.py:305
  6.2 9.8 %collective-permute-start.4 = (bf16[512,128]{1,0:T(8,128)(2,1)}, bf16[512,128]{1,0:T(8,128)(2,1)S(1)}, u32[]{:S(2)}, u32[]{:S(2)}) collective-permute-start(bf16[512,128]{1,0:T(8,128)(2,1)} %get-tuple-element.68), channel_id=1, source_target_pairs={{0,4},{4,0},{8,12},{12,8},{1,5},{5,1},{9,13},{13,9},{2,6},{6,2},{1... | collective-permute-start | bytes 393224 | tf_op jit(solution)/shard_map/ppermute | solution.py:276
  7.7 12.9 %collective-permute-start.5 = (bf16[512,128]{1,0:T(8,128)(2,1)S(1)}, bf16[512,128]{1,0:T(8,128)(2,1)S(1)}, u32[]{:S(2)}, u32[]{:S(2)}) collective-permute-start(bf16[512,128]{1,0:T(8,128)(2,1)S(1)} %get-tuple-element.69), channel_id=1, source_target_pairs={{0,8},{4,12},{8,0},{12,4},{1,9},{5,13},{9,1},{13,5},{2,10},{6,14},... | collective-permute-start | bytes 393224 | tf_op jit(solution)/shard_map/ppermute | solution.py:276
  10.3 10.3 %collective-permute-start.6 = (bf16[512,128]{1,0:T(8,128)(2,1)S(1)}, bf16[512,128]{1,0:T(8,128)(2,1)S(1)}, u32[]{:S(2)}, u32[]{:S(2)}) collective-permute-start(bf16[512,128]{1,0:T(8,128)(2,1)S(1)} %get-tuple-element.70), channel_id=1, source_target_pairs={{0,12},{4,8},{8,4},{12,0},{1,13},{5,9},{9,5},{13,1},{2,14},{6,10},... | collective-permute-start | bytes 393224 | tf_op jit(solution)/shard_map/ppermute | solution.py:276
  10.5 1.0 %copy-start.2 = (bf16[8,2,128,128]{3,2,1,0:T(8,128)(2,1)S(1)}, bf16[8,2,128,128]{3,2,1,0:T(8,128)(2,1)}, u32[]{:S(2)}) copy-start(bf16[8,2,128,128]{3,2,1,0:T(8,128)(2,1)} %copy-done.1) | copy-start | bytes 1572868
  11.7 17.7 %collective-permute-start.1 = (bf16[432,128]{1,0:T(8,128)(2,1)S(1)}, bf16[432,128]{1,0:T(8,128)(2,1)S(1)}, u32[]{:S(2)}, u32[]{:S(2)}) collective-permute-start(bf16[432,128]{1,0:T(8,128)(2,1)S(1)} %get-tuple-element.65), channel_id=1, source_target_pairs={{0,4},{4,0},{8,12},{12,8},{1,5},{5,1},{9,13},{13,9},{2,6},{6,2},{1... | collective-permute-start | bytes 331784 | tf_op jit(solution)/shard_map/ppermute | solution.py:276
  12.5 18.1 %collective-permute-start.2 = (bf16[432,128]{1,0:T(8,128)(2,1)S(1)}, bf16[432,128]{1,0:T(8,128)(2,1)S(1)}, u32[]{:S(2)}, u32[]{:S(2)}) collective-permute-start(bf16[432,128]{1,0:T(8,128)(2,1)S(1)} %get-tuple-element.66), channel_id=1, source_target_pairs={{0,8},{4,12},{8,0},{12,4},{1,9},{5,13},{9,1},{13,5},{2,10},{6,14},... | collective-permute-start | bytes 331784 | tf_op jit(solution)/shard_map/ppermute | solution.py:276
  15.9 14.6 %collective-permute-start.3 = (bf16[432,128]{1,0:T(8,128)(2,1)S(1)}, bf16[432,128]{1,0:T(8,128)(2,1)S(1)}, u32[]{:S(2)}, u32[]{:S(2)}) collective-permute-start(bf16[432,128]{1,0:T(8,128)(2,1)S(1)} %get-tuple-element.67), channel_id=1, source_target_pairs={{0,12},{4,8},{8,4},{12,0},{1,13},{5,9},{9,5},{13,1},{2,14},{6,10},... | collective-permute-start | bytes 331784 | tf_op jit(solution)/shard_map/ppermute | solution.py:276
  20.8 0.7 %copy-start.3 = (f32[1,512]{1,0:T(1,128)S(1)}, f32[1,512]{1,0:T(1,128)}, u32[]{:S(2)}) copy-start(f32[1,512]{1,0:T(1,128)} %refs_4_.13) | copy-start | bytes 6148
  21.4 4.8 %collective-permute-start.7 = (bf16[1,8,48,128]{3,2,1,0:T(8,128)(2,1)S(1)}, bf16[1,8,48,128]{3,2,1,0:T(8,128)(2,1)S(1)}, u32[]{:S(2)}, u32[]{:S(2)}) collective-permute-start(bf16[1,8,48,128]{3,2,1,0:T(8,128)(2,1)S(1)} %get-tuple-element.71.refs_4_), channel_id=1, source_target_pairs={{0,2},{2,0},{1,3},{3,1},{4,6},{6,4},{5,7},{7,5},{8,10},{10,8},{9,1... | collective-permute-start | bytes 294920 | tf_op jit(solution)/shard_map/ppermute | solution.py:342
  23.3 9.1 %collective-permute-start.8 = (bf16[1,8,48,128]{3,2,1,0:T(8,128)(2,1)S(1)}, bf16[1,8,48,128]{3,2,1,0:T(8,128)(2,1)S(1)}, u32[]{:S(2)}, u32[]{:S(2)}) collective-permute-start(bf16[1,8,48,128]{3,2,1,0:T(8,128)(2,1)S(1)} %get-tuple-element.74.refs_4_), channel_id=1, source_target_pairs={{0,2},{2,0},{1,3},{3,1},{4,6},{6,4},{5,7},{7,5},{8,10},{10,8},{9,1... | collective-permute-start | bytes 294920 | tf_op jit(solution)/shard_map/ppermute | solution.py:342
  26.2 7.7 %collective-permute-start.9 = (bf16[1,8,48,128]{3,2,1,0:T(8,128)(2,1)S(1)}, bf16[1,8,48,128]{3,2,1,0:T(8,128)(2,1)S(1)}, u32[]{:S(2)}, u32[]{:S(2)}) collective-permute-start(bf16[1,8,48,128]{3,2,1,0:T(8,128)(2,1)S(1)} %get-tuple-element.77.refs_4_), channel_id=1, source_target_pairs={{0,2},{2,0},{1,3},{3,1},{4,6},{6,4},{5,7},{7,5},{8,10},{10,8},{9,1... | collective-permute-start | bytes 294920 | tf_op jit(solution)/shard_map/ppermute | solution.py:342
  30.5 6.5 %collective-permute-start.10 = (bf16[1,8,48,128]{3,2,1,0:T(8,128)(2,1)S(1)}, bf16[1,8,48,128]{3,2,1,0:T(8,128)(2,1)S(1)}, u32[]{:S(2)}, u32[]{:S(2)}) collective-permute-start(bf16[1,8,48,128]{3,2,1,0:T(8,128)(2,1)S(1)} %get-tuple-element.81.refs_4_), channel_id=1, source_target_pairs={{0,2},{2,0},{1,3},{3,1},{4,6},{6,4},{5,7},{7,5},{8,10},{10,8},{9,1... | collective-permute-start | bytes 294920 | tf_op jit(solution)/shard_map/ppermute | solution.py:342
  33.6 5.0 %collective-permute-start.11 = (bf16[1,8,48,128]{3,2,1,0:T(8,128)(2,1)S(1)}, bf16[1,8,48,128]{3,2,1,0:T(8,128)(2,1)S(1)}, u32[]{:S(2)}, u32[]{:S(2)}) collective-permute-start(bf16[1,8,48,128]{3,2,1,0:T(8,128)(2,1)S(1)} %get-tuple-element.87.refs_4_), channel_id=1, source_target_pairs={{0,2},{2,0},{1,3},{3,1},{4,6},{6,4},{5,7},{7,5},{8,10},{10,8},{9,1... | collective-permute-start | bytes 294920 | tf_op jit(solution)/shard_map/ppermute | solution.py:342
  35.1 7.2 %collective-permute-start.14 = (bf16[1,8,48,128]{3,2,1,0:T(8,128)(2,1)S(1)}, bf16[1,8,48,128]{3,2,1,0:T(8,128)(2,1)S(1)}, u32[]{:S(2)}, u32[]{:S(2)}) collective-permute-start(bf16[1,8,48,128]{3,2,1,0:T(8,128)(2,1)S(1)} %get-tuple-element.93.refs_4_), channel_id=1, source_target_pairs={{0,2},{2,0},{1,3},{3,1},{4,6},{6,4},{5,7},{7,5},{8,10},{10,8},{9,1... | collective-permute-start | bytes 294920 | tf_op jit(solution)/shard_map/ppermute | solution.py:342
  38.2 5.2 %collective-permute-start.13 = (bf16[1,8,48,128]{3,2,1,0:T(8,128)(2,1)S(1)}, bf16[1,8,48,128]{3,2,1,0:T(8,128)(2,1)S(1)}, u32[]{:S(2)}, u32[]{:S(2)}) collective-permute-start(bf16[1,8,48,128]{3,2,1,0:T(8,128)(2,1)S(1)} %get-tuple-element.99.refs_4_), channel_id=1, source_target_pairs={{0,2},{2,0},{1,3},{3,1},{4,6},{6,4},{5,7},{7,5},{8,10},{10,8},{9,1... | collective-permute-start | bytes 294920 | tf_op jit(solution)/shard_map/ppermute | solution.py:342
  40.4 4.6 %collective-permute-start.12 = (bf16[1,8,48,128]{3,2,1,0:T(8,128)(2,1)S(1)}, bf16[1,8,48,128]{3,2,1,0:T(8,128)(2,1)S(1)}, u32[]{:S(2)}, u32[]{:S(2)}) collective-permute-start(bf16[1,8,48,128]{3,2,1,0:T(8,128)(2,1)S(1)} %get-tuple-element.105), channel_id=1, source_target_pairs={{0,2},{2,0},{1,3},{3,1},{4,6},{6,4},{5,7},{7,5},{8,10},{10,8},{9,1... | collective-permute-start | bytes 294920 | tf_op jit(solution)/shard_map/ppermute | solution.py:342
  47.0 11.8 %collective-permute-start.15 = (bf16[2,9,32,128]{3,2,1,0:T(8,128)(2,1)S(1)}, bf16[2,9,32,128]{3,2,1,0:T(8,128)(2,1)S(1)}, u32[]{:S(2)}, u32[]{:S(2)}) collective-permute-start(bf16[2,9,32,128]{3,2,1,0:T(8,128)(2,1)S(1)} %get-tuple-element.118), channel_id=1, source_target_pairs={{0,4},{4,0},{8,12},{12,8},{1,5},{5,1},{9,13},{13,9},{2,6},{6,2},{1... | collective-permute-start | bytes 442376 | tf_op jit(solution)/shard_map/ppermute | solution.py:276
  54.9 9.2 %collective-permute-start.16 = (bf16[2,9,32,128]{3,2,1,0:T(8,128)(2,1)S(1)}, bf16[2,9,32,128]{3,2,1,0:T(8,128)(2,1)S(1)}, u32[]{:S(2)}, u32[]{:S(2)}) collective-permute-start(bf16[2,9,32,128]{3,2,1,0:T(8,128)(2,1)S(1)} %get-tuple-element.117), channel_id=1, source_target_pairs={{0,8},{4,12},{8,0},{12,4},{1,9},{5,13},{9,1},{13,5},{2,10},{6,14},... | collective-permute-start | bytes 442376 | tf_op jit(solution)/shard_map/ppermute | solution.py:276
  55.3 8.8 %collective-permute-start.17 = (bf16[2,9,32,128]{3,2,1,0:T(8,128)(2,1)S(1)}, bf16[2,9,32,128]{3,2,1,0:T(8,128)(2,1)S(1)}, u32[]{:S(2)}, u32[]{:S(2)}) collective-permute-start(bf16[2,9,32,128]{3,2,1,0:T(8,128)(2,1)S(1)} %get-tuple-element.116), channel_id=1, source_target_pairs={{0,12},{4,8},{8,4},{12,0},{1,13},{5,9},{9,5},{13,1},{2,14},{6,10},... | collective-permute-start | bytes 442376 | tf_op jit(solution)/shard_map/ppermute | solution.py:276

commit v3 on v2

v3 whole, which is shorter than its diff:
```python
import functools

import jax
import jax.numpy as jnp
from jax import lax
from jax.experimental import pallas as pl
from jax.experimental.pallas import tpu as pltpu
from jax.sharding import PartitionSpec as P

BF = jnp.bfloat16
F32 = jnp.float32
CHUNKS = (2, 2, 2, 2)
LAG = 3
FIRST = 2
LENT = 4
EARLY_OUT = 4
LEND_AFTER = False
SPREAD = True
MIB = 1024 * 1024


def round_up(value, unit):
    return -(-value // unit) * unit


def partner(index, hop, count):
    if count & (count - 1) == 0:
        return index ^ hop, index ^ hop
    return (index + hop) % count, (index + count - hop) % count


def hop_at(number, count):
    if not SPREAD or number == 0:
        return number
    return jnp.where(lax.axis_index("cols") % 2 == 0, number, count - number)


def sigmoid(value):
    return 0.5 * jnp.tanh(0.5 * value) + 0.5


class Piece:
    def __init__(self, strip, need, begin, band):
        self.extent = round_up(strip + 2 * need, 8)
        self.left = (self.extent - strip) // 2
        self.begin = begin
        self.end = begin + band * self.extent


class Plan:
    def __init__(self, inputs):
        self.steps, self.band, self.columns, self.chans = inputs.shape
        self.count = lax.axis_size("rows")
        self.cols = lax.axis_size("cols")
        self.layers = lax.axis_size("pipe")
        self.grid_columns = self.columns * self.cols
        self.rows_n = self.band * self.count
        self.strip = self.columns // self.count
        most = self.steps + self.layers - 1
        self.pad = round_up(most - 1, 8)
        self.width = round_up(self.strip + 2 * self.pad, 16)
        self.total = self.rows_n * self.width
        self.room = 4 * MIB + self.total * self.chans * (4 * 4 * 6 + 12)
        self.lent_steps = min(LENT, self.steps - 1) if self.layers > 1 else 0
        own = self.steps - self.lent_steps
        self.first = min(FIRST, own)
        needs = [most, most - 1] + [most - step for step in range(self.steps)]
        inputs_of = lambda begin, end: [2 + step for step in range(begin, end)]
        self.early, rows_a = self.pieces(needs, [0, 1] + inputs_of(0, self.first))
        self.late, rows_b = self.pieces(needs, inputs_of(self.first, own))
        self.lent, self.lent_rows = self.pieces(needs, inputs_of(own, self.steps))
        self.state, rows_c = self.pieces(needs, [0, 1])
        self.early_rows = max(rows_a, self.lent_rows)
        self.late_rows = max(rows_b, rows_c)
        half = min(EARLY_OUT, self.steps)
        self.bounds = [(0, half), (half, self.steps + 1)]
        self.edge = round_up(max((self.pieces(needs, [n])[0][n].left for n in range(len(needs)))) + 4, 16)

    def reach(self, phase, step):
        return (self.steps - 1 - step) + (self.layers - 1 - phase)

    def lends(self, phase, first_step):
        return LEND_AFTER and self.lent_steps > 0 and phase == 0 and first_step == 0

    def extent(self, phase, first_step, last_step):
        return min(round_up(self.strip + 2 * self.reach(phase, first_step), 8), self.width)

    def pieces(self, needs, numbers):
        found, begin = {}, 0
        for number in numbers:
            found[number] = Piece(self.strip, needs[number], begin, self.band)
            begin = found[number].end
        return found, begin


def edge_kernel(plan, maps, out):
    edge, columns = plan.edge, plan.columns

    @pl.when(lax.axis_index("cols") == 0)
    def _():
        out[...] = maps[:, :, columns - edge :]

    @pl.when(lax.axis_index("cols") != 0)
    def _():
        out[...] = maps[:, :, :edge]


def pack_kernel(plan, maps, left, right, *refs):
    early, late, padded = refs[: plan.count], refs[plan.count : -1], refs[-1]
    edge, columns, chans, band = plan.edge, plan.columns, plan.chans, plan.band
    place, col = lax.axis_index("rows"), lax.axis_index("cols")

    def fill(groups):
        for outs, pieces in groups:
            for number, piece in pieces.items():
                before = jnp.where(col > 0, left[number].astype(F32), 0.0)
                after = jnp.where(col < plan.cols - 1, right[number].astype(F32), 0.0)
                padded[number, :, 0:edge] = before
                padded[number, :, edge : edge + columns] = maps[number].astype(F32)
                padded[number, :, edge + columns : 2 * edge + columns] = after
        for outs, pieces in groups:
            for number, piece in pieces.items():
                for hop in range(plan.count):
                    target = partner(place, hop_at(hop, plan.count), plan.count)[0]
                    inset = edge - piece.left
                    rest = inset % 8
                    start = pl.multiple_of(target * plan.strip + (inset - rest), 8)
                    loaded = piece.extent + (8 if rest else 0)
                    value = padded[number, :, pl.ds(start, loaded), :]
                    if rest:
                        value = value.reshape(band * loaded, chans)
                        value = pltpu.roll(value, band * loaded - rest, 0)
                        value = value.reshape(band, loaded, chans)[:, : piece.extent]
                    value = value.reshape(band * piece.extent, chans)
                    outs[hop][piece.begin : piece.end] = value.astype(BF)

    @pl.when(lax.axis_index("pipe") == 0)
    def _():
        fill([(early, plan.early), (late, plan.late)])

    @pl.when(lax.axis_index("pipe") != 0)
    def _():
        fill([(early, plan.lent), (late, plan.state)])


def needed(plan, phase, first_step, last_step):
    if phase > 0:
        return [False, first_step == 0, False]
    own = plan.steps - plan.lent_steps
    return [
        first_step < plan.first,
        first_step < own and last_step > plan.first,
        last_step > own,
    ]


def chunk_kernel(plan, phase, first_step, last_step, parts, *refs):
    refs = list(refs)
    rows_n, band, width, chans = plan.rows_n, plan.band, plan.width, plan.chans
    count, total, steps = plan.count, plan.total, plan.steps
    early, late, lent = needed(plan, phase, first_step, last_step)
    early = [(refs.pop(0), 0) for _ in range(count)] if early else None
    late = [(refs.pop(0), 0) for _ in range(count)] if late else None
    if lent:
        lender = refs.pop(0)
        lent = [(lender, hop * plan.lent_rows) for hop in range(count)]
    maps_ref = None if phase == 0 else refs.pop(0)
    hidden_ref = cell_ref = None
    if first_step > 0:
        hidden_ref, cell_ref = refs.pop(0), refs.pop(0)
    weights, bias = refs[:2]
    outs, (slab, fresh) = refs[2 + parts : -2], refs[-2:]
    outs, kept = list(outs[:-parts]), outs[-parts:]
    hidden_out = outs.pop(0) if last_step < steps or phase < plan.layers - 1 else None
    cell_out = outs.pop(0) if last_step < steps else None
    if plan.lends(phase, first_step):
        borrowed = outs.pop(0)

        @pl.when(lax.axis_index("pipe") != phase)
        def _():
            for hop in range(count):
                begin = hop * plan.lent_rows
                borrowed[begin : begin + plan.lent_rows] = early[hop][0][: plan.lent_rows]

    bounds = plan.bounds[-len(kept) :]

    def keep(at, value):
        for ref, (begin, end) in zip(kept, bounds):
            if begin <= at < end:
                ref[:, at - begin] = value

    @pl.when(lax.axis_index("pipe") == phase)
    def _():
        place = lax.axis_index("rows")
        sources = [partner(place, hop_at(hop, count), count)[1] for hop in range(count)]
        start_column = (
            lax.axis_index("cols") * plan.columns + place * plan.strip - plan.pad
        )
        blank = jnp.zeros((width, 6 * chans), BF)
        slab[0:width, :] = blank
        slab[total + width : total + 2 * width, :] = blank

        def spread(lane, value):
            value = value.astype(F32)
            extent = value.shape[1]
            left = plan.pad if extent == width else (extent - plan.strip) // 2
            if extent < width:
                fill = jnp.zeros((rows_n, width - extent, chans), F32)
                value = jnp.concatenate([value, fill], axis=1)
            value = value.reshape(total, chans)
            for tap in range(3):
                shift = (plan.pad - left + 1 - tap) % total
                moved = pltpu.roll(value, shift, 0) if shift else value
                at = 2 * chans * tap + lane
                slab[width : width + total, at : at + chans] = moved.astype(BF)

        def bands(lane, refs_in, piece):
            for hop in range(count):
                ref, offset = refs_in[hop]
                flat = ref[offset + piece.begin : offset + piece.end].astype(F32)
                extent = piece.extent
                if extent < width:
                    flat = flat.reshape(band, extent, chans)
                    fill = jnp.zeros((band, width - extent, chans), F32)
                    flat = jnp.concatenate([flat, fill], axis=1).reshape(band * width, chans)
                    extent = width
                source = sources[hop]
                for tap in range(3) if lane is not None else (1,):
                    shift = (plan.pad - piece.left + 1 - tap) % (band * extent)
                    moved = pltpu.roll(flat, shift, 0) if shift else flat
                    moved = moved.reshape(band, extent, chans)[:, :width]
                    moved = moved.reshape(band * width, chans)
                    if lane is None:
                        start = pl.multiple_of(source * band * width, 16)
                        fresh[pl.ds(start, band * width), :] = moved
                    else:
                        at = 2 * chans * tap + lane
                        start = pl.multiple_of((source * band + 1) * width, 16)
                        slab[pl.ds(start, band * width), at : at + chans] = moved.astype(BF)

        hidden = None
        cell = None
        for step in range(first_step, last_step):
            if step == 0:
                pieces, from_refs = (plan.state, late) if phase > 0 else (plan.early, early)
                bands(chans, from_refs, pieces[0])
                bands(None, from_refs, pieces[1])
                cell = fresh[...]
            elif step == first_step:
                spread(chans, hidden_ref[hidden_ref.shape[0] - 1])
                cell = cell_ref[...]
            else:
                spread(chans, hidden)
            if phase > 0:
                spread(0, maps_ref[step - first_step])
            elif step < plan.first:
                bands(0, early, plan.early[2 + step])
            elif step < steps - plan.lent_steps:
                bands(0, late, plan.late[2 + step])
            else:
                bands(0, lent, plan.lent[2 + step])

            depth = 6 * chans
            gates = bias[0:1]
            for tap in range(3):
                gates = gates + jnp.dot(
                    slab[tap * width : tap * width + total, :],
                    weights[tap * depth : (tap + 1) * depth, :],
                    preferred_element_type=F32,
                )
            cell = sigmoid(gates[:, chans : 2 * chans]) * cell + sigmoid(
                gates[:, :chans]
            ) * jnp.tanh(gates[:, 2 * chans : 3 * chans])
            hidden = sigmoid(gates[:, 3 * chans :]) * jnp.tanh(cell)
            hidden = hidden.reshape(rows_n, width, chans)
            column = start_column + lax.broadcasted_iota(jnp.int32, hidden.shape, 1)
            inside = jnp.logical_and(column >= 0, column < plan.grid_columns)
            hidden = jnp.where(inside, hidden, 0.0)
            extent = hidden_out.shape[2] if hidden_out is not None else width
            if extent < width:
                shift = plan.pad - (extent - plan.strip) // 2
                moved = pltpu.roll(hidden.reshape(total, chans), total - shift, 0)
                moved = moved.reshape(rows_n, width, chans)[:, :extent]
                hidden_out[step - first_step] = moved.astype(BF)
            elif hidden_out is not None:
                hidden_out[step - first_step] = hidden.astype(BF)
            hidden = hidden.astype(BF)
            keep(step, hidden)
        if cell_out is not None:
            cell_out[...] = cell
        if last_step == steps:
            keep(steps, cell.astype(BF).reshape(rows_n, width, chans))


def advance(plan, phase, first_step, last_step, feed, kept):
    vmem = pl.BlockSpec(memory_space=pltpu.VMEM)
    operands = [*feed, *kept]
    chunk = last_step - first_step
    extent = plan.extent(phase, first_step, last_step)
    outs = []
    if last_step < plan.steps or phase < plan.layers - 1:
        outs.append(jax.ShapeDtypeStruct((chunk, plan.rows_n, extent, plan.chans), BF))
    if last_step < plan.steps:
        outs.append(jax.ShapeDtypeStruct((plan.total, plan.chans), F32))
    if plan.lends(phase, first_step):
        outs.append(jax.ShapeDtypeStruct((plan.count * plan.lent_rows, plan.chans), BF))
    aliases = {len(feed) + n: len(outs) + n for n in range(len(kept))}
    outs += [jax.ShapeDtypeStruct(part.shape, part.dtype) for part in kept]
    return pl.pallas_call(
        functools.partial(chunk_kernel, plan, phase, first_step, last_step, len(kept)),
        out_shape=outs,
        in_specs=[vmem] * len(operands),
        out_specs=[vmem] * len(outs),
        scratch_shapes=[
            pltpu.VMEM((plan.total + 2 * plan.width, 6 * plan.chans), BF),
            pltpu.VMEM((plan.total, plan.chans), F32),
        ],
        input_output_aliases=aliases,
        compiler_params=pltpu.CompilerParams(vmem_limit_bytes=plan.room),
        cost_estimate=pl.CostEstimate(
            flops=2 * chunk * plan.total * 18 * plan.chans * 4 * plan.chans,
            bytes_accessed=1000000,
            transcendentals=5 * chunk * plan.total * plan.chans,
        ),
    )(*operands)


def merge_kernel(plan, *refs):
    maps_out, cell_out = refs[-2:]
    place = lax.axis_index("rows")
    for hop in range(plan.count):
        source = partner(place, hop_at(hop, plan.count), plan.count)[1]
        columns = pl.ds(pl.multiple_of(source * plan.strip, plan.strip), plan.strip)
        for number, (begin, end) in enumerate(plan.bounds):
            part = refs[number * plan.count + hop]
            for step in range(begin, min(end, plan.steps)):
                maps_out[0, step, :, columns, :] = part[:, step - begin]
            if end > plan.steps:
                cell_out[0, :, columns, :] = part[:, plan.steps - begin].astype(F32)


def pack(plan, arrays):
    vmem = pl.BlockSpec(memory_space=pltpu.VMEM)
    shape = (2 + plan.steps, plan.band, plan.columns + 2 * plan.edge, plan.chans)
    rows = [plan.early_rows] * plan.count + [plan.late_rows] * plan.count
    return pl.pallas_call(
        functools.partial(pack_kernel, plan),
        out_shape=[jax.ShapeDtypeStruct((extent, plan.chans), BF) for extent in rows],
        in_specs=[vmem] * len(arrays),
        out_specs=[vmem] * len(rows),
        scratch_shapes=[pltpu.VMEM(shape, F32)],
        compiler_params=pltpu.CompilerParams(vmem_limit_bytes=plan.room),
    )(*arrays)


def load_kernel(weights_in, bias_in, _, weights, bias, sems):
    copies = [
        pltpu.make_async_copy(weights_in, weights, sems.at[0]),
        pltpu.make_async_copy(bias_in, bias, sems.at[1]),
    ]
    for copy in copies:
        copy.start()
    for copy in copies:
        copy.wait()


def settle(plan, parts, kept):
    vmem = pl.BlockSpec(memory_space=pltpu.VMEM)
    return pl.pallas_call(
        lambda *refs: None,
        out_shape=jax.ShapeDtypeStruct(kept.shape, kept.dtype),
        in_specs=[vmem] * (1 + len(parts)),
        out_specs=vmem,
        input_output_aliases={len(parts): 0},
        compiler_params=pltpu.CompilerParams(vmem_limit_bytes=plan.room),
    )(*parts, kept)


def exchange(plan, pieces):
    got = [pieces[0]]
    for number in range(1, plan.count):
        route = []
        for row in range(plan.count):
            for col in range(plan.cols):
                hop = plan.count - number if SPREAD and col % 2 else number
                target = partner(row, hop, plan.count)[0]
                route.append((row * plan.cols + col, target * plan.cols + col))
        got.append(lax.ppermute(pieces[number], ("rows", "cols"), route))
    return got


def shards(inputs, hidden_init, cell_init, kernels, biases):
    plan = Plan(inputs)
    place = lax.axis_index("rows")
    steps, band, chans, count, layers = (
        plan.steps,
        plan.band,
        plan.chans,
        plan.count,
        plan.layers,
    )
    vmem = pl.BlockSpec(memory_space=pltpu.VMEM)
    params = pltpu.CompilerParams(vmem_limit_bytes=plan.room)
    maps = jnp.concatenate([hidden_init, cell_init.astype(BF), inputs], axis=0)
    if plan.cols == 2:
        beside = pl.pallas_call(
            functools.partial(edge_kernel, plan),
            out_shape=jax.ShapeDtypeStruct((2 + steps, band, plan.edge, chans), BF),
            in_specs=[vmem],
            out_specs=vmem,
            compiler_params=params,
        )(maps)
        left = right = lax.ppermute(beside, "cols", [(0, 1), (1, 0)])
    else:
        ring = [(n, (n + 1) % plan.cols) for n in range(plan.cols)]
        left = lax.ppermute(maps[:, :, plan.columns - plan.edge :], "cols", ring)
        right = lax.ppermute(maps[:, :, : plan.edge], "cols", [(b, a) for a, b in ring])
    packed = pack(plan, [maps, left, right])
    weights, bias = pl.pallas_call(
        load_kernel,
        out_shape=[jax.ShapeDtypeStruct(part.shape, part.dtype) for part in (kernels[0], biases)],
        in_specs=[pl.BlockSpec(memory_space=pltpu.HBM)] * 2 + [vmem],
        out_specs=[vmem] * 2,
        scratch_shapes=[pltpu.SemaphoreType.DMA((2,))],
        compiler_params=params,
    )(kernels[0], biases, packed[0])
    early = exchange(plan, packed[:count])
    late = exchange(plan, packed[count:])
    lent = []
    back = [(n, (n - 1) % layers) for n in range(layers)]
    if plan.lent_steps and not LEND_AFTER:
        borrowed = jnp.concatenate([piece[: plan.lent_rows] for piece in early], axis=0)
        lent = [lax.ppermute(borrowed, "pipe", back)]

    kept = [
        jnp.zeros((plan.rows_n, end - begin, plan.width, chans), BF) for begin, end in plan.bounds
    ]

    def out_piece(part, hop):
        target = partner(place, hop_at(hop, count), count)[0]
        piece = lax.dynamic_slice_in_dim(part, target * band, band, axis=0)
        return piece[:, :, plan.pad : plan.pad + plan.strip]

    chunks = []
    while not chunks or chunks[-1][1] < steps:
        begin = chunks[-1][1] if chunks else 0
        size = CHUNKS[len(chunks)] if len(chunks) < len(CHUNKS) else 1
        chunks.append((begin, min(begin + size, steps)))
    order = sorted(
        (number + LAG * phase, -phase, number)
        for phase in range(layers)
        for number in range(len(chunks))
    )
    state = [[] for _ in range(layers)]
    sent = {}
    parts = []
    for _, minus_phase, number in order:
        phase = -minus_phase
        first_step, last_step = chunks[number]
        takes = needed(plan, phase, first_step, last_step)
        feed = []
        for wanted, arrays in zip(takes, (early, late, lent)):
            feed += arrays if wanted else []
        feed += [sent[phase - 1, number]] if phase > 0 else []
        feed += state[phase]
        results = advance(plan, phase, first_step, last_step, feed + [weights, bias], kept)
        results, kept = list(results[: -len(kept)]), list(results[-len(kept) :])
        if plan.lends(phase, first_step):
            lent = [lax.ppermute(results.pop(), "pipe", back)]
        if last_step < steps:
            state[phase] = results
        if phase < layers - 1:
            hidden = results[0]
            ring = [(n, (n + 1) % layers) for n in range(layers)]
            sent[phase, number] = lax.ppermute(hidden, "pipe", ring)
        if phase == layers - 1 and last_step >= plan.bounds[0][1] and len(kept) == 2:
            done = kept.pop(0)
            parts += exchange(plan, [out_piece(done, hop) for hop in range(count)])
    rest = settle(plan, parts[1:2], kept[0])
    parts += exchange(plan, [out_piece(rest, hop) for hop in range(count)])
    vmem = pl.BlockSpec(memory_space=pltpu.VMEM)
    return pl.pallas_call(
        functools.partial(merge_kernel, plan),
        out_shape=(
            jax.ShapeDtypeStruct((1, steps, band, plan.columns, chans), BF),
            jax.ShapeDtypeStruct((1, band, plan.columns, chans), F32),
        ),
        in_specs=[vmem] * len(parts),
        out_specs=(vmem, vmem),
        compiler_params=pltpu.CompilerParams(vmem_limit_bytes=plan.room),
    )(*parts)


def solution(mesh):
    return jax.shard_map(
        shards,
        mesh=mesh,
        in_specs=(
            P(None, ("groups", "rows"), "cols", None),
            P("pipe", ("groups", "rows"), "cols", None),
            P("pipe", ("groups", "rows"), "cols", None),
            P("pipe", None, None),
            P("pipe", None),
        ),
        out_specs=(
            P("pipe", None, ("groups", "rows"), "cols", None),
            P("pipe", ("groups", "rows"), "cols", None),
        ),
        check_vma=False,
    )
```

time: 66.8 us -> 60 us (0.90); the launches traced: 65.6 us -> 59.8 us
  local copies, waits for them, and re-layouts: 5.85 us -> 0.23 us
  starting transfers between devices: 31.9 us -> 28.1 us
  waiting for transfers between devices: 14.3 us -> 17 us
  other arithmetic: 0.66 us -> 2.92 us
  Pallas kernels: 12 us -> 10.7 us
    unnamed x14 -> x4, local copies, waits for them, and re-layouts: 4.66 us -> 0.01 us
    ppermute x9 -> x13, waiting for transfers between devices: 11 us -> 14.8 us  [the longest x12 14.8 us: exchange(): got.append(lax.ppermute(pieces[number], ('rows', 'cols'), route))]
    ppermute x9 -> x13, starting transfers between devices: 20.3 us -> 16.6 us  [the longest x12 16 us: exchange(): got.append(lax.ppermute(pieces[number], ('rows', 'cols'), route))]
    concatenate x0 -> x2, other arithmetic: none -> 1.85 us  [the longest x1 1.1 us: shards(): maps = jnp.concatenate([hidden_init, cell_init.astype(BF), inputs], axis=0)]
    pallas_call x16 -> x8, Pallas kernels: 10.8 us -> 9.44 us  [advance(): pl.pallas_call(functools.partial(chunk_kernel, plan, phase, first_step, l...]
    ppermute x8 -> x4, waiting for transfers between devices: 1.93 us -> 0.93 us  [shards(): sent[phase, number] = lax.ppermute(hidden, 'pipe', ring)]
    broadcast_in_dim x3 -> x2, local copies, waits for them, and re-layouts: 1.06 us -> 0.12 us  [shards(): jnp.zeros((plan.rows_n, end - begin, plan.width, chans), BF)]
    ppermute x8 -> x4, starting transfers between devices: 11.6 us -> 11.5 us  [shards(): sent[phase, number] = lax.ppermute(hidden, 'pipe', ring)]
  transfers between devices with their start and end apart: 18 -> 18, of which waited for: 8 -> 8; matrix products, arithmetic and copies ran while one was open for 0% -> 0% of each run, Pallas kernels for 14% -> 16%
where the time goes in v3:
time: 60 us; the launch traced here: 59.8 us
  starting transfers between devices  28.1 us (47%)
  waiting for transfers between devices  17 us (28%)
  Pallas kernels  10.7 us (18%)
  other arithmetic  2.92 us (5%)
  between operations  0.8 us (1%)
    ppermute x12, starting transfers between devices, exchange(): got.append(lax.ppermute(pieces[number], ('rows', 'cols'), route))  16 us
    ppermute x12, waiting for transfers between devices, exchange(): got.append(lax.ppermute(pieces[number], ('rows', 'cols'), route))  14.8 us
    ppermute x4, starting transfers between devices, shards(): sent[phase, number] = lax.ppermute(hidden, 'pipe', ring)  11.5 us
    pallas_call x8, Pallas kernels, advance(): pl.pallas_call(functools.partial(chunk_kernel, plan, phase, first_step, l...  9.44 us
    ppermute x1, waiting for transfers between devices, shards(): left = right = lax.ppermute(beside, 'cols', [(0, 1), (1, 0)])  1.26 us
  transfers between devices with their start and end apart: 18, of which 8 were waited for; matrix products, arithmetic and copies ran while one was open for 0% of the time, Pallas kernels for 16%

profile of v3, /device:TPU:6, one launch (start us, length us, event | category | flops | bytes accessed | tf_op | source)
XLA Modules:
  0.0 59.8 jit_solution(2583630239744575599)
XLA Ops:
  0.6 0.0 copy-start
  0.6 0.0 copy-start.1
  0.7 1.1 %convert_element_type.3 = bf16[1,2,128,128]{3,2,1,0:T(8,128)(2,1)S(1)} convert(f32[1,2,128,128]{3,2,1,0:T(8,128)} %param.7) | non-fusion elementwise | flops 32768 | bytes 196608 | tf_op jit(solution)/shard_map/convert_element_type | solution.py:404
  1.7 1.1 %pad_maximum_fusion.maps = bf16[10,2,128,128]{3,2,1,0:T(8,128)(2,1)S(1)} fusion(bf16[8,2,128,128]{3,2,1,0:T(8,128)(2,1)} %param.5, bf16[1,2,128,128]{3,2,1,0:T(8,128)(2,1)S(1)} %convert_element_type.3, bf16[1,2,128,128]{3,2,1,0:T(8,128)(2,1)} %param.6), kind=kLoop, calls=%fused_computation | loop fusion | flops 655360 | bytes 1310720 | tf_op jit(solution)/shard_map/concatenate | solution.py:404
  2.9 0.1 collective-permute-start
  2.9 1.3 %collective-permute-done.left.right = bf16[10,2,16,128]{3,2,1,0:T(8,128)(2,1)S(1)} collective-permute-done((bf16[10,2,16,128]{3,2,1,0:T(8,128)(2,1)S(1)}, bf16[10,2,16,128]{3,2,1,0:T(8,128)(2,1)S(1)}, u32[]{:S(2)}, u32[]{:S(2)}) %collective-permute-start) | collective-permute-done | bytes 81952 | tf_op jit(solution)/shard_map/ppermute | solution.py:413
  4.2 0.2 shard_map.69
  4.4 1.6 %collective-permute-start.4 = (bf16[416,128]{1,0:T(8,128)(2,1)S(1)}, bf16[416,128]{1,0:T(8,128)(2,1)S(1)}, u32[]{:S(2)}, u32[]{:S(2)}) collective-permute-start(bf16[416,128]{1,0:T(8,128)(2,1)S(1)} %get-tuple-element.43), channel_id=1, source_target_pairs={{0,4},{1,13},{4,0},{5,9},{8,12},{9,5},{12,8},{13,1},{2,6},{3,15},{... | collective-permute-start | bytes 319496 | tf_op jit(solution)/shard_map/ppermute | solution.py:388
  6.0 2.6 %collective-permute-start.5 = (bf16[416,128]{1,0:T(8,128)(2,1)S(1)}, bf16[416,128]{1,0:T(8,128)(2,1)S(1)}, u32[]{:S(2)}, u32[]{:S(2)}) collective-permute-start(bf16[416,128]{1,0:T(8,128)(2,1)S(1)} %get-tuple-element.44), channel_id=1, source_target_pairs={{0,8},{1,9},{4,12},{5,13},{8,0},{9,1},{12,4},{13,5},{2,10},{3,11},... | collective-permute-start | bytes 319496 | tf_op jit(solution)/shard_map/ppermute | solution.py:388
  8.6 0.2 collective-permute-start.6
  8.8 0.3 collective-permute-done.4.refs_1_
  9.1 5.5 %collective-permute-done.5.refs_2_ = bf16[416,128]{1,0:T(8,128)(2,1)S(1)} collective-permute-done((bf16[416,128]{1,0:T(8,128)(2,1)S(1)}, bf16[416,128]{1,0:T(8,128)(2,1)S(1)}, u32[]{:S(2)}, u32[]{:S(2)}) %collective-permute-start.5) | collective-permute-done | bytes 106528 | tf_op jit(solution)/shard_map/ppermute | solution.py:388
  14.6 1.3 %collective-permute-done.6.refs_3_ = bf16[416,128]{1,0:T(8,128)(2,1)S(1)} collective-permute-done((bf16[416,128]{1,0:T(8,128)(2,1)S(1)}, bf16[416,128]{1,0:T(8,128)(2,1)S(1)}, u32[]{:S(2)}, u32[]{:S(2)}) %collective-permute-start.6) | collective-permute-done | bytes 106528 | tf_op jit(solution)/shard_map/ppermute | solution.py:388
  15.9 0.8 %pad_maximum_fusion.1 = bf16[1344,128]{1,0:T(8,128)(2,1)} fusion(bf16[336,128]{1,0:T(8,128)(2,1)S(1)} %slice.50, bf16[336,128]{1,0:T(8,128)(2,1)S(1)} %slice.49, bf16[336,128]{1,0:T(8,128)(2,1)S(1)} %slice.48, bf16[336,128]{1,0:T(8,128)(2,1)S(1)} %slice.36), kind=kLoop, calls=%fused_computation.1 | loop fusion | flops 1376256 | bytes 688128 | tf_op jit(solution)/shard_map/concatenate | solution.py:432
  16.7 0.5 collective-permute-start.9
  17.2 2.0 %collective-permute-start.1 = (bf16[208,128]{1,0:T(8,128)(2,1)S(1)}, bf16[208,128]{1,0:T(8,128)(2,1)S(1)}, u32[]{:S(2)}, u32[]{:S(2)}) collective-permute-start(bf16[208,128]{1,0:T(8,128)(2,1)S(1)} %get-tuple-element.39), channel_id=1, source_target_pairs={{0,4},{1,13},{4,0},{5,9},{8,12},{9,5},{12,8},{13,1},{2,6},{3,15},{... | collective-permute-start | bytes 159752 | tf_op jit(solution)/shard_map/ppermute | solution.py:388
  19.2 1.4 %collective-permute-start.2 = (bf16[208,128]{1,0:T(8,128)(2,1)S(1)}, bf16[208,128]{1,0:T(8,128)(2,1)S(1)}, u32[]{:S(2)}, u32[]{:S(2)}) collective-permute-start(bf16[208,128]{1,0:T(8,128)(2,1)S(1)} %get-tuple-element.40), channel_id=1, source_target_pairs={{0,8},{1,9},{4,12},{5,13},{8,0},{9,1},{12,4},{13,5},{2,10},{3,11},... | collective-permute-start | bytes 159752 | tf_op jit(solution)/shard_map/ppermute | solution.py:388
  20.6 1.1 %collective-permute-start.3 = (bf16[208,128]{1,0:T(8,128)(2,1)S(1)}, bf16[208,128]{1,0:T(8,128)(2,1)S(1)}, u32[]{:S(2)}, u32[]{:S(2)}) collective-permute-start(bf16[208,128]{1,0:T(8,128)(2,1)S(1)} %get-tuple-element.41), channel_id=1, source_target_pairs={{0,12},{1,5},{4,8},{5,1},{8,4},{9,13},{12,0},{13,9},{2,14},{3,7},{... | collective-permute-start | bytes 159752 | tf_op jit(solution)/shard_map/ppermute | solution.py:388
  21.7 0.0 copy-done
  21.7 0.0 copy-done.1
  21.7 0.2 shard_map.70
  21.9 0.1 broadcast_in_dim.7.refs_7_
  22.0 0.1 broadcast_in_dim.6.refs_6_
  22.1 4.0 %collective-permute-start.8 = (bf16[2,8,48,128]{3,2,1,0:T(8,128)(2,1)S(1)}, bf16[2,8,48,128]{3,2,1,0:T(8,128)(2,1)S(1)}, u32[]{:S(2)}, u32[]{:S(2)}) collective-permute-start(bf16[2,8,48,128]{3,2,1,0:T(8,128)(2,1)S(1)} %get-tuple-element.48.refs_4_), channel_id=1, source_target_pairs={{0,2},{2,0},{1,3},{3,1},{4,6},{6,4},{5,7},{7,5},{8,10},{10,8},{9,1... | collective-permute-start | bytes 589832 | tf_op jit(solution)/shard_map/ppermute | solution.py:475
  26.1 0.0 collective-permute-done.1.refs_1_
  26.1 0.0 collective-permute-done.2.refs_2_
  26.1 0.4 collective-permute-done.3.refs_3_
  26.5 4.0 %collective-permute-start.7 = (bf16[2,8,48,128]{3,2,1,0:T(8,128)(2,1)S(1)}, bf16[2,8,48,128]{3,2,1,0:T(8,128)(2,1)S(1)}, u32[]{:S(2)}, u32[]{:S(2)}) collective-permute-start(bf16[2,8,48,128]{3,2,1,0:T(8,128)(2,1)S(1)} %get-tuple-element.52.refs_1_), channel_id=1, source_target_pairs={{0,2},{2,0},{1,3},{3,1},{4,6},{6,4},{5,7},{7,5},{8,10},{10,8},{9,1... | collective-permute-start | bytes 589832 | tf_op jit(solution)/shard_map/ppermute | solution.py:475
  30.5 0.0 collective-permute-done.9.refs_0_
  30.5 2.6 %collective-permute-start.14 = (bf16[2,8,40,128]{3,2,1,0:T(8,128)(2,1)S(1)}, bf16[2,8,40,128]{3,2,1,0:T(8,128)(2,1)S(1)}, u32[]{:S(2)}, u32[]{:S(2)}) collective-permute-start(bf16[2,8,40,128]{3,2,1,0:T(8,128)(2,1)S(1)} %get-tuple-element.60.refs_1_), channel_id=1, source_target_pairs={{0,2},{2,0},{1,3},{3,1},{4,6},{6,4},{5,7},{7,5},{8,10},{10,8},{9,1... | collective-permute-start | bytes 491528 | tf_op jit(solution)/shard_map/ppermute | solution.py:475
  33.2 0.0 collective-permute-done.8.refs_4_
  33.2 2.4 %shard_map.74 = (bf16[2,8,48,128]{3,2,1,0:T(8,128)(2,1)S(1)}, f32[384,128]{1,0:T(8,128)S(1)}, bf16[8,4,48,128]{3,2,1,0:T(8,128)(2,1)S(1)}, bf16[8,5,48,128]{3,2,1,0:T(8,128)(2,1)S(1)}) custom-call(bf16[208,128]{1,0:T(8,128)(2,1)S(1)} %get-tuple-element.38.refs_0_, ...), custom_call_target="tpu_custom_call", output_to_operand_aliasing={{2}: (7, {}), {3}: (8, {})} | custom-call | flops 1811939328 | bytes 1000000 | tf_op jit(solution)/shard_map/pallas_call | solution.py:309
  35.6 0.8 %collective-permute-start.13 = (bf16[2,8,40,128]{3,2,1,0:T(8,128)(2,1)S(1)}, bf16[2,8,40,128]{3,2,1,0:T(8,128)(2,1)S(1)}, u32[]{:S(2)}, u32[]{:S(2)}) collective-permute-start(bf16[2,8,40,128]{3,2,1,0:T(8,128)(2,1)S(1)} %get-tuple-element.67), channel_id=1, source_target_pairs={{0,2},{2,0},{1,3},{3,1},{4,6},{6,4},{5,7},{7,5},{8,10},{10,8},{9,1... | collective-permute-start | bytes 491528 | tf_op jit(solution)/shard_map/ppermute | solution.py:475
  36.4 0.0 collective-permute-done.7.refs_0_
  36.4 2.3 %shard_map.76 = (bf16[2,8,48,128]{3,2,1,0:T(8,128)(2,1)S(1)}, f32[384,128]{1,0:T(8,128)S(1)}, bf16[8,4,48,128]{3,2,1,0:T(8,128)(2,1)S(1)}, bf16[8,5,48,128]{3,2,1,0:T(8,128)(2,1)S(1)}) custom-call(bf16[2,8,48,128]{3,2,1,0:T(8,128)(2,1)S(1)} %collective-permute-done.7.refs_0_, ...), custom_call_target="tpu_custom_call", output_to_operand_aliasing={{2}: (5, {}), {3}: (6, {})} | custom-call | flops 1811939328 | bytes 1000000 | tf_op jit(solution)/shard_map/pallas_call | solution.py:309
  38.8 0.7 %collective-permute-start.10 = (bf16[2,4,32,128]{3,2,1,0:T(8,128)(2,1)S(1)}, bf16[2,4,32,128]{3,2,1,0:T(8,128)(2,1)S(1)}, u32[]{:S(2)}, u32[]{:S(2)}) collective-permute-start(bf16[2,4,32,128]{3,2,1,0:T(8,128)(2,1)S(1)} %get-tuple-element.80), channel_id=1, source_target_pairs={{0,4},{1,13},{4,0},{5,9},{8,12},{9,5},{12,8},{13,1},{2,6},{3,15},{... | collective-permute-start | bytes 196616 | tf_op jit(solution)/shard_map/ppermute | solution.py:388
  39.5 0.4 collective-permute-done.14.refs_0_
  39.9 2.4 %shard_map.77 = (bf16[2,8,40,128]{3,2,1,0:T(8,128)(2,1)S(1)}, f32[384,128]{1,0:T(8,128)S(1)}, bf16[8,5,48,128]{3,2,1,0:T(8,128)(2,1)S(1)}) custom-call(bf16[2,8,40,128]{3,2,1,0:T(8,128)(2,1)S(1)} %collective-permute-done.14.refs_0_, bf16[2,8,48,128]{3,2,1,0:T(8,128)(2,1)S(1)} %get-tuple-element.68.refs_1_, ...), custom_call_target="tpu_custom_call", output_to_operand_aliasing={{2}: (5, {})} | custom-call | flops 1811939328 | bytes 1000000 | tf_op jit(solution)/shard_map/pallas_call | solution.py:309
  42.2 0.6 collective-permute-done.13.refs_0_
  42.8 2.3 %shard_map.78.refs_1_ = bf16[8,5,48,128]{3,2,1,0:T(8,128)(2,1)S(1)} custom-call(bf16[2,8,40,128]{3,2,1,0:T(8,128)(2,1)S(1)} %collective-permute-done.13.refs_0_, bf16[2,8,40,128]{3,2,1,0:T(8,128)(2,1)S(1)} %get-tuple-element.71.refs_1_, f32[384,128]{1,0:T(8,128)S(1)} %get-tuple-element.72.refs_2_, ...), custom_call_target="tpu_custom_call", output_to_operand_aliasing={{}: (5, {})} | custom-call | flops 1811939328 | bytes 1000000 | tf_op jit(solution)/shard_map/pallas_call | solution.py:309
  45.2 0.0 collective-permute-done.10.refs_0_.refs_1_
  45.2 0.5 collective-permute-start.15
  45.7 2.0 %collective-permute-start.16 = (bf16[2,5,32,128]{3,2,1,0:T(8,128)(2,1)S(1)}, bf16[2,5,32,128]{3,2,1,0:T(8,128)(2,1)S(1)}, u32[]{:S(2)}, u32[]{:S(2)}) collective-permute-start(bf16[2,5,32,128]{3,2,1,0:T(8,128)(2,1)S(1)} %get-tuple-element.75), channel_id=1, source_target_pairs={{0,8},{1,9},{4,12},{5,13},{8,0},{9,1},{12,4},{13,5},{2,10},{3,11},... | collective-permute-start | bytes 245768 | tf_op jit(solution)/shard_map/ppermute | solution.py:388
  47.8 1.9 %collective-permute-start.17 = (bf16[2,5,32,128]{3,2,1,0:T(8,128)(2,1)S(1)}, bf16[2,5,32,128]{3,2,1,0:T(8,128)(2,1)S(1)}, u32[]{:S(2)}, u32[]{:S(2)}) collective-permute-start(bf16[2,5,32,128]{3,2,1,0:T(8,128)(2,1)S(1)} %get-tuple-element.74), channel_id=1, source_target_pairs={{0,12},{1,5},{4,8},{5,1},{8,4},{9,13},{12,0},{13,9},{2,14},{3,7},{... | collective-permute-start | bytes 245768 | tf_op jit(solution)/shard_map/ppermute | solution.py:388
  49.7 0.9 %collective-permute-start.11 = (bf16[2,4,32,128]{3,2,1,0:T(8,128)(2,1)S(1)}, bf16[2,4,32,128]{3,2,1,0:T(8,128)(2,1)S(1)}, u32[]{:S(2)}, u32[]{:S(2)}) collective-permute-start(bf16[2,4,32,128]{3,2,1,0:T(8,128)(2,1)S(1)} %get-tuple-element.79), channel_id=1, source_target_pairs={{0,8},{1,9},{4,12},{5,13},{8,0},{9,1},{12,4},{13,5},{2,10},{3,11},... | collective-permute-start | bytes 196616 | tf_op jit(solution)/shard_map/ppermute | solution.py:388
  50.5 1.0 %collective-permute-start.12 = (bf16[2,4,32,128]{3,2,1,0:T(8,128)(2,1)S(1)}, bf16[2,4,32,128]{3,2,1,0:T(8,128)(2,1)S(1)}, u32[]{:S(2)}, u32[]{:S(2)}) collective-permute-start(bf16[2,4,32,128]{3,2,1,0:T(8,128)(2,1)S(1)} %get-tuple-element.78), channel_id=1, source_target_pairs={{0,12},{1,5},{4,8},{5,1},{8,4},{9,13},{12,0},{13,9},{2,14},{3,7},{... | collective-permute-start | bytes 196616 | tf_op jit(solution)/shard_map/ppermute | solution.py:388
  51.6 7.3 %collective-permute-done.11.refs_2_ = bf16[2,4,32,128]{3,2,1,0:T(8,128)(2,1)S(1)} collective-permute-done((bf16[2,4,32,128]{3,2,1,0:T(8,128)(2,1)S(1)}, bf16[2,4,32,128]{3,2,1,0:T(8,128)(2,1)S(1)}, u32[]{:S(2)}, u32[]{:S(2)}) %collective-permute-start.11) | collective-permute-done | bytes 65568 | tf_op jit(solution)/shard_map/ppermute | solution.py:388
  58.9 0.0 collective-permute-done.12.refs_3_
  58.9 0.0 collective-permute-done.15.refs_5_
  58.9 0.0 collective-permute-done.16.refs_6_
  58.9 0.0 collective-permute-done.17.refs_7_
  58.9 0.9 %shard_map.80 = (bf16[1,8,2,128,128]{4,3,2,1,0:T(8,128)(2,1)}, f32[1,2,128,128]{3,2,1,0:T(8,128)}) custom-call(bf16[2,4,32,128]{3,2,1,0:T(8,128)(2,1)S(1)} %get-tuple-element.81.refs_0_, bf16[2,4,32,128]{3,2,1,0:T(8,128)(2,1)S(1)} %collective-permute-done.10.refs_0_.refs_1_, bf16[2,4,32,128]{3,2,1,0:T(8,128)(2,1)S(1)} %collective-permute-done.11.refs_2_, ...), custom_call_target="tpu_custom_call" | custom-call | tf_op jit(solution)/shard_map/pallas_call | solution.py:482
  (12 shorter events, 0.2 us)
Async XLA Ops:
  0.6 21.1 %copy-start = (bf16[1,2304,512]{2,1,0:T(8,128)(2,1)S(1)}, bf16[1,2304,512]{2,1,0:T(8,128)(2,1)}, u32[]{:S(2)}) copy-start(bf16[1,2304,512]{2,1,0:T(8,128)(2,1)} %param.8) | copy-start | bytes 7077892
  0.6 21.1 %copy-start.1 = (f32[1,512]{1,0:T(1,128)S(1)}, f32[1,512]{1,0:T(1,128)}, u32[]{:S(2)}) copy-start(f32[1,512]{1,0:T(1,128)} %bias_in.1) | copy-start | bytes 6148
  2.9 1.3 %collective-permute-start = (bf16[10,2,16,128]{3,2,1,0:T(8,128)(2,1)S(1)}, bf16[10,2,16,128]{3,2,1,0:T(8,128)(2,1)S(1)}, u32[]{:S(2)}, u32[]{:S(2)}) collective-permute-start(bf16[10,2,16,128]{3,2,1,0:T(8,128)(2,1)S(1)} %shard_map.68), channel_id=1, source_target_pairs={{0,1},{1,0},{2,3},{3,2},{4,5},{5,4},{6,7},{7,6},{8,9},{9,8},{10,11... | collective-permute-start | bytes 245768 | tf_op jit(solution)/shard_map/ppermute | solution.py:413
  4.4 4.8 %collective-permute-start.4 = (bf16[416,128]{1,0:T(8,128)(2,1)S(1)}, bf16[416,128]{1,0:T(8,128)(2,1)S(1)}, u32[]{:S(2)}, u32[]{:S(2)}) collective-permute-start(bf16[416,128]{1,0:T(8,128)(2,1)S(1)} %get-tuple-element.43), channel_id=1, source_target_pairs={{0,4},{1,13},{4,0},{5,9},{8,12},{9,5},{12,8},{13,1},{2,6},{3,15},{... | collective-permute-start | bytes 319496 | tf_op jit(solution)/shard_map/ppermute | solution.py:388
  6.0 8.6 %collective-permute-start.5 = (bf16[416,128]{1,0:T(8,128)(2,1)S(1)}, bf16[416,128]{1,0:T(8,128)(2,1)S(1)}, u32[]{:S(2)}, u32[]{:S(2)}) collective-permute-start(bf16[416,128]{1,0:T(8,128)(2,1)S(1)} %get-tuple-element.44), channel_id=1, source_target_pairs={{0,8},{1,9},{4,12},{5,13},{8,0},{9,1},{12,4},{13,5},{2,10},{3,11},... | collective-permute-start | bytes 319496 | tf_op jit(solution)/shard_map/ppermute | solution.py:388
  8.6 7.3 %collective-permute-start.6 = (bf16[416,128]{1,0:T(8,128)(2,1)S(1)}, bf16[416,128]{1,0:T(8,128)(2,1)S(1)}, u32[]{:S(2)}, u32[]{:S(2)}) collective-permute-start(bf16[416,128]{1,0:T(8,128)(2,1)S(1)} %get-tuple-element.45), channel_id=1, source_target_pairs={{0,12},{1,5},{4,8},{5,1},{8,4},{9,13},{12,0},{13,9},{2,14},{3,7},{... | collective-permute-start | bytes 319496 | tf_op jit(solution)/shard_map/ppermute | solution.py:388
  16.7 13.9 %collective-permute-start.9 = (bf16[1344,128]{1,0:T(8,128)(2,1)}, bf16[1344,128]{1,0:T(8,128)(2,1)S(1)}, u32[]{:S(2)}, u32[]{:S(2)}) collective-permute-start(bf16[1344,128]{1,0:T(8,128)(2,1)} %pad_maximum_fusion.1), channel_id=1, source_target_pairs={{0,2},{2,0},{1,3},{3,1},{4,6},{6,4},{5,7},{7,5},{8,10},{10,8},{9,1... | collective-permute-start | bytes 1032200 | tf_op jit(solution)/shard_map/ppermute | solution.py:433
  17.2 8.9 %collective-permute-start.1 = (bf16[208,128]{1,0:T(8,128)(2,1)S(1)}, bf16[208,128]{1,0:T(8,128)(2,1)S(1)}, u32[]{:S(2)}, u32[]{:S(2)}) collective-permute-start(bf16[208,128]{1,0:T(8,128)(2,1)S(1)} %get-tuple-element.39), channel_id=1, source_target_pairs={{0,4},{1,13},{4,0},{5,9},{8,12},{9,5},{12,8},{13,1},{2,6},{3,15},{... | collective-permute-start | bytes 159752 | tf_op jit(solution)/shard_map/ppermute | solution.py:388
  19.2 6.9 %collective-permute-start.2 = (bf16[208,128]{1,0:T(8,128)(2,1)S(1)}, bf16[208,128]{1,0:T(8,128)(2,1)S(1)}, u32[]{:S(2)}, u32[]{:S(2)}) collective-permute-start(bf16[208,128]{1,0:T(8,128)(2,1)S(1)} %get-tuple-element.40), channel_id=1, source_target_pairs={{0,8},{1,9},{4,12},{5,13},{8,0},{9,1},{12,4},{13,5},{2,10},{3,11},... | collective-permute-start | bytes 159752 | tf_op jit(solution)/shard_map/ppermute | solution.py:388
  20.6 5.9 %collective-permute-start.3 = (bf16[208,128]{1,0:T(8,128)(2,1)S(1)}, bf16[208,128]{1,0:T(8,128)(2,1)S(1)}, u32[]{:S(2)}, u32[]{:S(2)}) collective-permute-start(bf16[208,128]{1,0:T(8,128)(2,1)S(1)} %get-tuple-element.41), channel_id=1, source_target_pairs={{0,12},{1,5},{4,8},{5,1},{8,4},{9,13},{12,0},{13,9},{2,14},{3,7},{... | collective-permute-start | bytes 159752 | tf_op jit(solution)/shard_map/ppermute | solution.py:388
  22.1 11.1 %collective-permute-start.8 = (bf16[2,8,48,128]{3,2,1,0:T(8,128)(2,1)S(1)}, bf16[2,8,48,128]{3,2,1,0:T(8,128)(2,1)S(1)}, u32[]{:S(2)}, u32[]{:S(2)}) collective-permute-start(bf16[2,8,48,128]{3,2,1,0:T(8,128)(2,1)S(1)} %get-tuple-element.48.refs_4_), channel_id=1, source_target_pairs={{0,2},{2,0},{1,3},{3,1},{4,6},{6,4},{5,7},{7,5},{8,10},{10,8},{9,1... | collective-permute-start | bytes 589832 | tf_op jit(solution)/shard_map/ppermute | solution.py:475
  26.5 9.9 %collective-permute-start.7 = (bf16[2,8,48,128]{3,2,1,0:T(8,128)(2,1)S(1)}, bf16[2,8,48,128]{3,2,1,0:T(8,128)(2,1)S(1)}, u32[]{:S(2)}, u32[]{:S(2)}) collective-permute-start(bf16[2,8,48,128]{3,2,1,0:T(8,128)(2,1)S(1)} %get-tuple-element.52.refs_1_), channel_id=1, source_target_pairs={{0,2},{2,0},{1,3},{3,1},{4,6},{6,4},{5,7},{7,5},{8,10},{10,8},{9,1... | collective-permute-start | bytes 589832 | tf_op jit(solution)/shard_map/ppermute | solution.py:475
  30.5 9.3 %collective-permute-start.14 = (bf16[2,8,40,128]{3,2,1,0:T(8,128)(2,1)S(1)}, bf16[2,8,40,128]{3,2,1,0:T(8,128)(2,1)S(1)}, u32[]{:S(2)}, u32[]{:S(2)}) collective-permute-start(bf16[2,8,40,128]{3,2,1,0:T(8,128)(2,1)S(1)} %get-tuple-element.60.refs_1_), channel_id=1, source_target_pairs={{0,2},{2,0},{1,3},{3,1},{4,6},{6,4},{5,7},{7,5},{8,10},{10,8},{9,1... | collective-permute-start | bytes 491528 | tf_op jit(solution)/shard_map/ppermute | solution.py:475
  35.6 7.2 %collective-permute-start.13 = (bf16[2,8,40,128]{3,2,1,0:T(8,128)(2,1)S(1)}, bf16[2,8,40,128]{3,2,1,0:T(8,128)(2,1)S(1)}, u32[]{:S(2)}, u32[]{:S(2)}) collective-permute-start(bf16[2,8,40,128]{3,2,1,0:T(8,128)(2,1)S(1)} %get-tuple-element.67), channel_id=1, source_target_pairs={{0,2},{2,0},{1,3},{3,1},{4,6},{6,4},{5,7},{7,5},{8,10},{10,8},{9,1... | collective-permute-start | bytes 491528 | tf_op jit(solution)/shard_map/ppermute | solution.py:475
  38.8 6.4 %collective-permute-start.10 = (bf16[2,4,32,128]{3,2,1,0:T(8,128)(2,1)S(1)}, bf16[2,4,32,128]{3,2,1,0:T(8,128)(2,1)S(1)}, u32[]{:S(2)}, u32[]{:S(2)}) collective-permute-start(bf16[2,4,32,128]{3,2,1,0:T(8,128)(2,1)S(1)} %get-tuple-element.80), channel_id=1, source_target_pairs={{0,4},{1,13},{4,0},{5,9},{8,12},{9,5},{12,8},{13,1},{2,6},{3,15},{... | collective-permute-start | bytes 196616 | tf_op jit(solution)/shard_map/ppermute | solution.py:388
  45.2 13.7 %collective-permute-start.15 = (bf16[2,5,32,128]{3,2,1,0:T(8,128)(2,1)S(1)}, bf16[2,5,32,128]{3,2,1,0:T(8,128)(2,1)S(1)}, u32[]{:S(2)}, u32[]{:S(2)}) collective-permute-start(bf16[2,5,32,128]{3,2,1,0:T(8,128)(2,1)S(1)} %get-tuple-element.76), channel_id=1, source_target_pairs={{0,4},{1,13},{4,0},{5,9},{8,12},{9,5},{12,8},{13,1},{2,6},{3,15},{... | collective-permute-start | bytes 245768 | tf_op jit(solution)/shard_map/ppermute | solution.py:388
  45.7 13.2 %collective-permute-start.16 = (bf16[2,5,32,128]{3,2,1,0:T(8,128)(2,1)S(1)}, bf16[2,5,32,128]{3,2,1,0:T(8,128)(2,1)S(1)}, u32[]{:S(2)}, u32[]{:S(2)}) collective-permute-start(bf16[2,5,32,128]{3,2,1,0:T(8,128)(2,1)S(1)} %get-tuple-element.75), channel_id=1, source_target_pairs={{0,8},{1,9},{4,12},{5,13},{8,0},{9,1},{12,4},{13,5},{2,10},{3,11},... | collective-permute-start | bytes 245768 | tf_op jit(solution)/shard_map/ppermute | solution.py:388
  47.8 11.1 %collective-permute-start.17 = (bf16[2,5,32,128]{3,2,1,0:T(8,128)(2,1)S(1)}, bf16[2,5,32,128]{3,2,1,0:T(8,128)(2,1)S(1)}, u32[]{:S(2)}, u32[]{:S(2)}) collective-permute-start(bf16[2,5,32,128]{3,2,1,0:T(8,128)(2,1)S(1)} %get-tuple-element.74), channel_id=1, source_target_pairs={{0,12},{1,5},{4,8},{5,1},{8,4},{9,13},{12,0},{13,9},{2,14},{3,7},{... | collective-permute-start | bytes 245768 | tf_op jit(solution)/shard_map/ppermute | solution.py:388
  49.7 9.2 %collective-permute-start.11 = (bf16[2,4,32,128]{3,2,1,0:T(8,128)(2,1)S(1)}, bf16[2,4,32,128]{3,2,1,0:T(8,128)(2,1)S(1)}, u32[]{:S(2)}, u32[]{:S(2)}) collective-permute-start(bf16[2,4,32,128]{3,2,1,0:T(8,128)(2,1)S(1)} %get-tuple-element.79), channel_id=1, source_target_pairs={{0,8},{1,9},{4,12},{5,13},{8,0},{9,1},{12,4},{13,5},{2,10},{3,11},... | collective-permute-start | bytes 196616 | tf_op jit(solution)/shard_map/ppermute | solution.py:388
  50.5 8.3 %collective-permute-start.12 = (bf16[2,4,32,128]{3,2,1,0:T(8,128)(2,1)S(1)}, bf16[2,4,32,128]{3,2,1,0:T(8,128)(2,1)S(1)}, u32[]{:S(2)}, u32[]{:S(2)}) collective-permute-start(bf16[2,4,32,128]{3,2,1,0:T(8,128)(2,1)S(1)} %get-tuple-element.78), channel_id=1, source_target_pairs={{0,12},{1,5},{4,8},{5,1},{8,4},{9,13},{12,0},{13,9},{2,14},{3,7},{... | collective-permute-start | bytes 196616 | tf_op jit(solution)/shard_map/ppermute | solution.py:388

commit v4 on v3

--- a/solution.py
+++ b/solution.py
@@ -12,10 +12,12 @@
 CHUNKS = (2, 2, 2, 2)
 LAG = 3
 FIRST = 2
-LENT = 4
+LENT = 3
 EARLY_OUT = 4
 LEND_AFTER = False
 SPREAD = True
+LEND_ONE_WAY = True
+HAND_ONE_WAY = True
 MIB = 1024 * 1024
 
 
@@ -427,7 +429,7 @@
     early = exchange(plan, packed[:count])
     late = exchange(plan, packed[count:])
     lent = []
-    back = [(n, (n - 1) % layers) for n in range(layers)]
+    back = [(1, 0)] if LEND_ONE_WAY else [(n, (n - 1) % layers) for n in range(layers)]
     if plan.lent_steps and not LEND_AFTER:
         borrowed = jnp.concatenate([piece[: plan.lent_rows] for piece in early], axis=0)
         lent = [lax.ppermute(borrowed, "pipe", back)]
@@ -472,6 +474,8 @@
         if phase < layers - 1:
             hidden = results[0]
             ring = [(n, (n + 1) % layers) for n in range(layers)]
+            if HAND_ONE_WAY:
+                ring = [(phase, phase + 1)]
             sent[phase, number] = lax.ppermute(hidden, "pipe", ring)
         if phase == layers - 1 and last_step >= plan.bounds[0][1] and len(kept) == 2:
             done = kept.pop(0)

time: 60 us -> 58.6 us (0.977)
  waiting for transfers between devices: 17 us -> 13.6 us
  starting transfers between devices: 28.1 us -> 30.8 us
  other arithmetic: 2.92 us -> 2.18 us
    ppermute x12, starting transfers between devices: 16 us -> 23.1 us  [exchange(): got.append(lax.ppermute(pieces[number], ('rows', 'cols'), route))]
    ppermute x12, waiting for transfers between devices: 14.8 us -> 7.94 us  [exchange(): got.append(lax.ppermute(pieces[number], ('rows', 'cols'), route))]
    ppermute x4, starting transfers between devices: 11.5 us -> 5.15 us  [shards(): sent[phase, number] = lax.ppermute(hidden, 'pipe', ring)]
    ppermute x4, waiting for transfers between devices: 0.93 us -> 2.91 us  [shards(): sent[phase, number] = lax.ppermute(hidden, 'pipe', ring)]
    ppermute x1, starting transfers between devices: 0.54 us -> 2.49 us  [shards(): lent = [lax.ppermute(borrowed, 'pipe', back)]]
    ppermute x1, waiting for transfers between devices: 0.01 us -> 1.47 us  [shards(): lent = [lax.ppermute(borrowed, 'pipe', back)]]
    concatenate x1, other arithmetic: 0.75 us -> 0.02 us  [shards(): jnp.concatenate([piece[:plan.lent_rows] for piece in early], axis=0)]
where the time goes in v4:
time: 58.6 us; the launch traced here: 58.3 us
  starting transfers between devices  30.8 us (53%)
  waiting for transfers between devices  13.6 us (23%)
  Pallas kernels  10.7 us (18%)
  other arithmetic  2.18 us (4%)
  between operations  0.88 us (2%)
    ppermute x12, starting transfers between devices, exchange(): got.append(lax.ppermute(pieces[number], ('rows', 'cols'), route))  23.1 us
    pallas_call x8, Pallas kernels, advance(): pl.pallas_call(functools.partial(chunk_kernel, plan, phase, first_step, l...  9.44 us
    ppermute x12, waiting for transfers between devices, exchange(): got.append(lax.ppermute(pieces[number], ('rows', 'cols'), route))  7.94 us
    ppermute x4, starting transfers between devices, shards(): sent[phase, number] = lax.ppermute(hidden, 'pipe', ring)  5.15 us
    ppermute x4, waiting for transfers between devices, shards(): sent[phase, number] = lax.ppermute(hidden, 'pipe', ring)  2.91 us
    ppermute x1, starting transfers between devices, shards(): lent = [lax.ppermute(borrowed, 'pipe', back)]  2.49 us
    ppermute x1, waiting for transfers between devices, shards(): lent = [lax.ppermute(borrowed, 'pipe', back)]  1.47 us
    ppermute x1, waiting for transfers between devices, shards(): left = right = lax.ppermute(beside, 'cols', [(0, 1), (1, 0)])  1.26 us
  transfers between devices with their start and end apart: 18, of which 8 were waited for; matrix products, arithmetic and copies ran while one was open for 0% of the time, Pallas kernels for 16%

profile of v4, /device:TPU:6, one launch (start us, length us, event | category | flops | bytes accessed | tf_op | source)
XLA Modules:
  0.0 58.3 jit_solution(13999862426769465844)
XLA Ops:
  0.6 0.0 copy-start
  0.6 0.0 copy-start.1
  0.7 1.1 %convert_element_type.3 = bf16[1,2,128,128]{3,2,1,0:T(8,128)(2,1)S(1)} convert(f32[1,2,128,128]{3,2,1,0:T(8,128)} %param.7) | non-fusion elementwise | flops 32768 | bytes 196608 | tf_op jit(solution)/shard_map/convert_element_type | solution.py:406
  1.7 1.1 %pad_maximum_fusion.maps = bf16[10,2,128,128]{3,2,1,0:T(8,128)(2,1)S(1)} fusion(bf16[8,2,128,128]{3,2,1,0:T(8,128)(2,1)} %param.5, bf16[1,2,128,128]{3,2,1,0:T(8,128)(2,1)S(1)} %convert_element_type.3, bf16[1,2,128,128]{3,2,1,0:T(8,128)(2,1)} %param.6), kind=kLoop, calls=%fused_computation | loop fusion | flops 655360 | bytes 1310720 | tf_op jit(solution)/shard_map/concatenate | solution.py:406
  2.9 0.1 collective-permute-start
  2.9 1.3 %collective-permute-done.left.right = bf16[10,2,16,128]{3,2,1,0:T(8,128)(2,1)S(1)} collective-permute-done((bf16[10,2,16,128]{3,2,1,0:T(8,128)(2,1)S(1)}, bf16[10,2,16,128]{3,2,1,0:T(8,128)(2,1)S(1)}, u32[]{:S(2)}, u32[]{:S(2)}) %collective-permute-start) | collective-permute-done | bytes 81952 | tf_op jit(solution)/shard_map/ppermute | solution.py:415
  4.2 0.1 shard_map.69
  4.3 1.6 %collective-permute-start.4 = (bf16[416,128]{1,0:T(8,128)(2,1)S(1)}, bf16[416,128]{1,0:T(8,128)(2,1)S(1)}, u32[]{:S(2)}, u32[]{:S(2)}) collective-permute-start(bf16[416,128]{1,0:T(8,128)(2,1)S(1)} %get-tuple-element.43), channel_id=1, source_target_pairs={{0,4},{1,13},{4,0},{5,9},{8,12},{9,5},{12,8},{13,1},{2,6},{3,15},{... | collective-permute-start | bytes 319496 | tf_op jit(solution)/shard_map/ppermute | solution.py:390
  6.0 2.6 %collective-permute-start.5 = (bf16[416,128]{1,0:T(8,128)(2,1)S(1)}, bf16[416,128]{1,0:T(8,128)(2,1)S(1)}, u32[]{:S(2)}, u32[]{:S(2)}) collective-permute-start(bf16[416,128]{1,0:T(8,128)(2,1)S(1)} %get-tuple-element.44), channel_id=1, source_target_pairs={{0,8},{1,9},{4,12},{5,13},{8,0},{9,1},{12,4},{13,5},{2,10},{3,11},... | collective-permute-start | bytes 319496 | tf_op jit(solution)/shard_map/ppermute | solution.py:390
  8.6 0.2 collective-permute-start.6
  8.8 0.7 %collective-permute-start.1 = (bf16[288,128]{1,0:T(8,128)(2,1)S(1)}, bf16[288,128]{1,0:T(8,128)(2,1)S(1)}, u32[]{:S(2)}, u32[]{:S(2)}) collective-permute-start(bf16[288,128]{1,0:T(8,128)(2,1)S(1)} %get-tuple-element.39), channel_id=1, source_target_pairs={{0,4},{1,13},{4,0},{5,9},{8,12},{9,5},{12,8},{13,1},{2,6},{3,15},{... | collective-permute-start | bytes 221192 | tf_op jit(solution)/shard_map/ppermute | solution.py:390
  9.5 3.5 %collective-permute-start.2 = (bf16[288,128]{1,0:T(8,128)(2,1)S(1)}, bf16[288,128]{1,0:T(8,128)(2,1)S(1)}, u32[]{:S(2)}, u32[]{:S(2)}) collective-permute-start(bf16[288,128]{1,0:T(8,128)(2,1)S(1)} %get-tuple-element.40), channel_id=1, source_target_pairs={{0,8},{1,9},{4,12},{5,13},{8,0},{9,1},{12,4},{13,5},{2,10},{3,11},... | collective-permute-start | bytes 221192 | tf_op jit(solution)/shard_map/ppermute | solution.py:390
  13.0 0.0 copy-done
  13.0 0.0 copy-done.1
  13.0 0.2 shard_map.70
  13.2 0.0 collective-permute-done.4.refs_1_
  13.2 2.4 %collective-permute-start.3 = (bf16[288,128]{1,0:T(8,128)(2,1)S(1)}, bf16[288,128]{1,0:T(8,128)(2,1)S(1)}, u32[]{:S(2)}, u32[]{:S(2)}) collective-permute-start(bf16[288,128]{1,0:T(8,128)(2,1)S(1)} %get-tuple-element.41), channel_id=1, source_target_pairs={{0,12},{1,5},{4,8},{5,1},{8,4},{9,13},{12,0},{13,9},{2,14},{3,7},{... | collective-permute-start | bytes 221192 | tf_op jit(solution)/shard_map/ppermute | solution.py:390
  15.6 0.0 collective-permute-done.5.refs_2_
  15.6 1.3 %collective-permute-done.6.refs_3_ = bf16[416,128]{1,0:T(8,128)(2,1)S(1)} collective-permute-done((bf16[416,128]{1,0:T(8,128)(2,1)S(1)}, bf16[416,128]{1,0:T(8,128)(2,1)S(1)}, u32[]{:S(2)}, u32[]{:S(2)}) %collective-permute-start.6) | collective-permute-done | bytes 106528 | tf_op jit(solution)/shard_map/ppermute | solution.py:390
  16.9 2.5 %collective-permute-start.9 = (bf16[960,128]{1,0:T(8,128)(2,1)S(1)}, bf16[960,128]{1,0:T(8,128)(2,1)S(1)}, u32[]{:S(2)}, u32[]{:S(2)}) collective-permute-start(bf16[960,128]{1,0:T(8,128)(2,1)S(1)} %pad_maximum_fusion.1), channel_id=1, source_target_pairs={{2,0},{3,1},{6,4},{7,5},{10,8},{11,9},{14,12},{15,13},{18,16},{19,... | collective-permute-start | bytes 737288 | tf_op jit(solution)/shard_map/ppermute | solution.py:435
  19.4 0.1 broadcast_in_dim.7.refs_7_
  19.4 0.1 broadcast_in_dim.6.refs_6_
  19.5 1.3 %collective-permute-start.8 = (bf16[2,8,48,128]{3,2,1,0:T(8,128)(2,1)S(1)}, bf16[2,8,48,128]{3,2,1,0:T(8,128)(2,1)S(1)}, u32[]{:S(2)}, u32[]{:S(2)}) collective-permute-start(bf16[2,8,48,128]{3,2,1,0:T(8,128)(2,1)S(1)} %get-tuple-element.48.refs_4_), channel_id=1, source_target_pairs={{0,2},{1,3},{4,6},{5,7},{8,10},{9,11},{12,14},{13,15},{16,18},{17,... | collective-permute-start | bytes 589832 | tf_op jit(solution)/shard_map/ppermute | solution.py:479
  20.8 0.0 collective-permute-done.1.refs_1_
  20.8 1.9 %collective-permute-done.2.refs_2_ = bf16[288,128]{1,0:T(8,128)(2,1)S(1)} collective-permute-done((bf16[288,128]{1,0:T(8,128)(2,1)S(1)}, bf16[288,128]{1,0:T(8,128)(2,1)S(1)}, u32[]{:S(2)}, u32[]{:S(2)}) %collective-permute-start.2) | collective-permute-done | bytes 73760 | tf_op jit(solution)/shard_map/ppermute | solution.py:390
  22.8 0.0 collective-permute-done.3.refs_3_
  22.8 1.3 %collective-permute-start.7 = (bf16[2,8,48,128]{3,2,1,0:T(8,128)(2,1)S(1)}, bf16[2,8,48,128]{3,2,1,0:T(8,128)(2,1)S(1)}, u32[]{:S(2)}, u32[]{:S(2)}) collective-permute-start(bf16[2,8,48,128]{3,2,1,0:T(8,128)(2,1)S(1)} %get-tuple-element.52.refs_5_), channel_id=1, source_target_pairs={{0,2},{1,3},{4,6},{5,7},{8,10},{9,11},{12,14},{13,15},{16,18},{17,... | collective-permute-start | bytes 589832 | tf_op jit(solution)/shard_map/ppermute | solution.py:479
  24.0 1.5 %collective-permute-done.9.refs_4_.refs_0_ = bf16[960,128]{1,0:T(8,128)(2,1)S(1)} collective-permute-done((bf16[960,128]{1,0:T(8,128)(2,1)S(1)}, bf16[960,128]{1,0:T(8,128)(2,1)S(1)}, u32[]{:S(2)}, u32[]{:S(2)}) %collective-permute-start.9) | collective-permute-done | bytes 245792 | tf_op jit(solution)/shard_map/ppermute | solution.py:435
  25.5 1.3 %collective-permute-start.14 = (bf16[2,8,40,128]{3,2,1,0:T(8,128)(2,1)S(1)}, bf16[2,8,40,128]{3,2,1,0:T(8,128)(2,1)S(1)}, u32[]{:S(2)}, u32[]{:S(2)}) collective-permute-start(bf16[2,8,40,128]{3,2,1,0:T(8,128)(2,1)S(1)} %get-tuple-element.60.refs_1_), channel_id=1, source_target_pairs={{0,2},{1,3},{4,6},{5,7},{8,10},{9,11},{12,14},{13,15},{16,18},{17,... | collective-permute-start | bytes 491528 | tf_op jit(solution)/shard_map/ppermute | solution.py:479
  26.8 2.4 %collective-permute-done.8.refs_4_ = bf16[2,8,48,128]{3,2,1,0:T(8,128)(2,1)S(1)} collective-permute-done((bf16[2,8,48,128]{3,2,1,0:T(8,128)(2,1)S(1)}, bf16[2,8,48,128]{3,2,1,0:T(8,128)(2,1)S(1)}, u32[]{:S(2)}, u32[]{:S(2)}) %collective-permute-start.8) | collective-permute-done | bytes 196640 | tf_op jit(solution)/shard_map/ppermute | solution.py:479
  29.2 2.4 %shard_map.74 = (bf16[2,8,48,128]{3,2,1,0:T(8,128)(2,1)S(1)}, f32[384,128]{1,0:T(8,128)S(1)}, bf16[8,4,48,128]{3,2,1,0:T(8,128)(2,1)S(1)}, bf16[8,5,48,128]{3,2,1,0:T(8,128)(2,1)S(1)}) custom-call(bf16[288,128]{1,0:T(8,128)(2,1)S(1)} %get-tuple-element.38.refs_0_, ...), custom_call_target="tpu_custom_call", output_to_operand_aliasing={{2}: (7, {}), {3}: (8, {})} | custom-call | flops 1811939328 | bytes 1000000 | tf_op jit(solution)/shard_map/pallas_call | solution.py:311
  31.6 1.3 %collective-permute-start.13 = (bf16[2,8,40,128]{3,2,1,0:T(8,128)(2,1)S(1)}, bf16[2,8,40,128]{3,2,1,0:T(8,128)(2,1)S(1)}, u32[]{:S(2)}, u32[]{:S(2)}) collective-permute-start(bf16[2,8,40,128]{3,2,1,0:T(8,128)(2,1)S(1)} %get-tuple-element.67), channel_id=1, source_target_pairs={{0,2},{1,3},{4,6},{5,7},{8,10},{9,11},{12,14},{13,15},{16,18},{17,... | collective-permute-start | bytes 491528 | tf_op jit(solution)/shard_map/ppermute | solution.py:479
  32.9 0.5 collective-permute-done.7.refs_0_
  33.4 2.3 %shard_map.76 = (bf16[2,8,48,128]{3,2,1,0:T(8,128)(2,1)S(1)}, f32[384,128]{1,0:T(8,128)S(1)}, bf16[8,4,48,128]{3,2,1,0:T(8,128)(2,1)S(1)}, bf16[8,5,48,128]{3,2,1,0:T(8,128)(2,1)S(1)}) custom-call(bf16[2,8,48,128]{3,2,1,0:T(8,128)(2,1)S(1)} %collective-permute-done.7.refs_0_, ...), custom_call_target="tpu_custom_call", output_to_operand_aliasing={{2}: (5, {}), {3}: (6, {})} | custom-call | flops 1811939328 | bytes 1000000 | tf_op jit(solution)/shard_map/pallas_call | solution.py:311
  35.8 3.4 %collective-permute-start.10 = (bf16[2,4,32,128]{3,2,1,0:T(8,128)(2,1)S(1)}, bf16[2,4,32,128]{3,2,1,0:T(8,128)(2,1)S(1)}, u32[]{:S(2)}, u32[]{:S(2)}) collective-permute-start(bf16[2,4,32,128]{3,2,1,0:T(8,128)(2,1)S(1)} %get-tuple-element.80), channel_id=1, source_target_pairs={{0,4},{1,13},{4,0},{5,9},{8,12},{9,5},{12,8},{13,1},{2,6},{3,15},{... | collective-permute-start | bytes 196616 | tf_op jit(solution)/shard_map/ppermute | solution.py:390
  39.2 0.0 collective-permute-done.14.refs_0_
  39.2 2.3 %shard_map.77 = (bf16[2,8,40,128]{3,2,1,0:T(8,128)(2,1)S(1)}, f32[384,128]{1,0:T(8,128)S(1)}, bf16[8,5,48,128]{3,2,1,0:T(8,128)(2,1)S(1)}) custom-call(bf16[2,8,40,128]{3,2,1,0:T(8,128)(2,1)S(1)} %collective-permute-done.14.refs_0_, bf16[2,8,48,128]{3,2,1,0:T(8,128)(2,1)S(1)} %get-tuple-element.68.refs_1_, ...), custom_call_target="tpu_custom_call", output_to_operand_aliasing={{2}: (5, {})} | custom-call | flops 1811939328 | bytes 1000000 | tf_op jit(solution)/shard_map/pallas_call | solution.py:311
  41.5 0.0 collective-permute-done.13.refs_0_
  41.5 2.3 %shard_map.78.refs_1_ = bf16[8,5,48,128]{3,2,1,0:T(8,128)(2,1)S(1)} custom-call(bf16[2,8,40,128]{3,2,1,0:T(8,128)(2,1)S(1)} %collective-permute-done.13.refs_0_, bf16[2,8,40,128]{3,2,1,0:T(8,128)(2,1)S(1)} %get-tuple-element.71.refs_1_, f32[384,128]{1,0:T(8,128)S(1)} %get-tuple-element.72.refs_2_, ...), custom_call_target="tpu_custom_call", output_to_operand_aliasing={{}: (5, {})} | custom-call | flops 1811939328 | bytes 1000000 | tf_op jit(solution)/shard_map/pallas_call | solution.py:311
  43.9 0.0 collective-permute-done.10.refs_0_.refs_1_
  44.0 1.7 %collective-permute-start.15 = (bf16[2,5,32,128]{3,2,1,0:T(8,128)(2,1)S(1)}, bf16[2,5,32,128]{3,2,1,0:T(8,128)(2,1)S(1)}, u32[]{:S(2)}, u32[]{:S(2)}) collective-permute-start(bf16[2,5,32,128]{3,2,1,0:T(8,128)(2,1)S(1)} %get-tuple-element.76), channel_id=1, source_target_pairs={{0,4},{1,13},{4,0},{5,9},{8,12},{9,5},{12,8},{13,1},{2,6},{3,15},{... | collective-permute-start | bytes 245768 | tf_op jit(solution)/shard_map/ppermute | solution.py:390
  45.7 3.2 %collective-permute-start.16 = (bf16[2,5,32,128]{3,2,1,0:T(8,128)(2,1)S(1)}, bf16[2,5,32,128]{3,2,1,0:T(8,128)(2,1)S(1)}, u32[]{:S(2)}, u32[]{:S(2)}) collective-permute-start(bf16[2,5,32,128]{3,2,1,0:T(8,128)(2,1)S(1)} %get-tuple-element.75), channel_id=1, source_target_pairs={{0,8},{1,9},{4,12},{5,13},{8,0},{9,1},{12,4},{13,5},{2,10},{3,11},... | collective-permute-start | bytes 245768 | tf_op jit(solution)/shard_map/ppermute | solution.py:390
  48.9 0.4 collective-permute-start.17
  49.2 2.0 %collective-permute-start.11 = (bf16[2,4,32,128]{3,2,1,0:T(8,128)(2,1)S(1)}, bf16[2,4,32,128]{3,2,1,0:T(8,128)(2,1)S(1)}, u32[]{:S(2)}, u32[]{:S(2)}) collective-permute-start(bf16[2,4,32,128]{3,2,1,0:T(8,128)(2,1)S(1)} %get-tuple-element.79), channel_id=1, source_target_pairs={{0,8},{1,9},{4,12},{5,13},{8,0},{9,1},{12,4},{13,5},{2,10},{3,11},... | collective-permute-start | bytes 196616 | tf_op jit(solution)/shard_map/ppermute | solution.py:390
  51.3 1.4 %collective-permute-start.12 = (bf16[2,4,32,128]{3,2,1,0:T(8,128)(2,1)S(1)}, bf16[2,4,32,128]{3,2,1,0:T(8,128)(2,1)S(1)}, u32[]{:S(2)}, u32[]{:S(2)}) collective-permute-start(bf16[2,4,32,128]{3,2,1,0:T(8,128)(2,1)S(1)} %get-tuple-element.78), channel_id=1, source_target_pairs={{0,12},{1,5},{4,8},{5,1},{8,4},{9,13},{12,0},{13,9},{2,14},{3,7},{... | collective-permute-start | bytes 196616 | tf_op jit(solution)/shard_map/ppermute | solution.py:390
  52.7 3.6 %collective-permute-done.11.refs_2_ = bf16[2,4,32,128]{3,2,1,0:T(8,128)(2,1)S(1)} collective-permute-done((bf16[2,4,32,128]{3,2,1,0:T(8,128)(2,1)S(1)}, bf16[2,4,32,128]{3,2,1,0:T(8,128)(2,1)S(1)}, u32[]{:S(2)}, u32[]{:S(2)}) %collective-permute-start.11) | collective-permute-done | bytes 65568 | tf_op jit(solution)/shard_map/ppermute | solution.py:390
  56.3 1.1 %collective-permute-done.12.refs_3_ = bf16[2,4,32,128]{3,2,1,0:T(8,128)(2,1)S(1)} collective-permute-done((bf16[2,4,32,128]{3,2,1,0:T(8,128)(2,1)S(1)}, bf16[2,4,32,128]{3,2,1,0:T(8,128)(2,1)S(1)}, u32[]{:S(2)}, u32[]{:S(2)}) %collective-permute-start.12) | collective-permute-done | bytes 65568 | tf_op jit(solution)/shard_map/ppermute | solution.py:390
  57.4 0.0 collective-permute-done.15.refs_5_
  57.4 0.0 collective-permute-done.16.refs_6_
  57.4 0.0 collective-permute-done.17.refs_7_
  57.4 0.9 %shard_map.80 = (bf16[1,8,2,128,128]{4,3,2,1,0:T(8,128)(2,1)}, f32[1,2,128,128]{3,2,1,0:T(8,128)}) custom-call(bf16[2,4,32,128]{3,2,1,0:T(8,128)(2,1)S(1)} %get-tuple-element.81.refs_0_, bf16[2,4,32,128]{3,2,1,0:T(8,128)(2,1)S(1)} %collective-permute-done.10.refs_0_.refs_1_, bf16[2,4,32,128]{3,2,1,0:T(8,128)(2,1)S(1)} %collective-permute-done.11.refs_2_, ...), custom_call_target="tpu_custom_call" | custom-call | tf_op jit(solution)/shard_map/pallas_call | solution.py:486
  (13 shorter events, 0.2 us)
Async XLA Ops:
  0.6 12.3 %copy-start = (bf16[1,2304,512]{2,1,0:T(8,128)(2,1)S(1)}, bf16[1,2304,512]{2,1,0:T(8,128)(2,1)}, u32[]{:S(2)}) copy-start(bf16[1,2304,512]{2,1,0:T(8,128)(2,1)} %param.8) | copy-start | bytes 7077892
  0.6 12.3 %copy-start.1 = (f32[1,512]{1,0:T(1,128)S(1)}, f32[1,512]{1,0:T(1,128)}, u32[]{:S(2)}) copy-start(f32[1,512]{1,0:T(1,128)} %bias_in.1) | copy-start | bytes 6148
  2.9 1.3 %collective-permute-start = (bf16[10,2,16,128]{3,2,1,0:T(8,128)(2,1)S(1)}, bf16[10,2,16,128]{3,2,1,0:T(8,128)(2,1)S(1)}, u32[]{:S(2)}, u32[]{:S(2)}) collective-permute-start(bf16[10,2,16,128]{3,2,1,0:T(8,128)(2,1)S(1)} %shard_map.68), channel_id=1, source_target_pairs={{0,1},{1,0},{2,3},{3,2},{4,5},{5,4},{6,7},{7,6},{8,9},{9,8},{10,11... | collective-permute-start | bytes 245768 | tf_op jit(solution)/shard_map/ppermute | solution.py:415
  4.3 8.8 %collective-permute-start.4 = (bf16[416,128]{1,0:T(8,128)(2,1)S(1)}, bf16[416,128]{1,0:T(8,128)(2,1)S(1)}, u32[]{:S(2)}, u32[]{:S(2)}) collective-permute-start(bf16[416,128]{1,0:T(8,128)(2,1)S(1)} %get-tuple-element.43), channel_id=1, source_target_pairs={{0,4},{1,13},{4,0},{5,9},{8,12},{9,5},{12,8},{13,1},{2,6},{3,15},{... | collective-permute-start | bytes 319496 | tf_op jit(solution)/shard_map/ppermute | solution.py:390
  6.0 9.6 %collective-permute-start.5 = (bf16[416,128]{1,0:T(8,128)(2,1)S(1)}, bf16[416,128]{1,0:T(8,128)(2,1)S(1)}, u32[]{:S(2)}, u32[]{:S(2)}) collective-permute-start(bf16[416,128]{1,0:T(8,128)(2,1)S(1)} %get-tuple-element.44), channel_id=1, source_target_pairs={{0,8},{1,9},{4,12},{5,13},{8,0},{9,1},{12,4},{13,5},{2,10},{3,11},... | collective-permute-start | bytes 319496 | tf_op jit(solution)/shard_map/ppermute | solution.py:390
  8.6 8.3 %collective-permute-start.6 = (bf16[416,128]{1,0:T(8,128)(2,1)S(1)}, bf16[416,128]{1,0:T(8,128)(2,1)S(1)}, u32[]{:S(2)}, u32[]{:S(2)}) collective-permute-start(bf16[416,128]{1,0:T(8,128)(2,1)S(1)} %get-tuple-element.45), channel_id=1, source_target_pairs={{0,12},{1,5},{4,8},{5,1},{8,4},{9,13},{12,0},{13,9},{2,14},{3,7},{... | collective-permute-start | bytes 319496 | tf_op jit(solution)/shard_map/ppermute | solution.py:390
  8.8 12.0 %collective-permute-start.1 = (bf16[288,128]{1,0:T(8,128)(2,1)S(1)}, bf16[288,128]{1,0:T(8,128)(2,1)S(1)}, u32[]{:S(2)}, u32[]{:S(2)}) collective-permute-start(bf16[288,128]{1,0:T(8,128)(2,1)S(1)} %get-tuple-element.39), channel_id=1, source_target_pairs={{0,4},{1,13},{4,0},{5,9},{8,12},{9,5},{12,8},{13,1},{2,6},{3,15},{... | collective-permute-start | bytes 221192 | tf_op jit(solution)/shard_map/ppermute | solution.py:390
  9.5 13.3 %collective-permute-start.2 = (bf16[288,128]{1,0:T(8,128)(2,1)S(1)}, bf16[288,128]{1,0:T(8,128)(2,1)S(1)}, u32[]{:S(2)}, u32[]{:S(2)}) collective-permute-start(bf16[288,128]{1,0:T(8,128)(2,1)S(1)} %get-tuple-element.40), channel_id=1, source_target_pairs={{0,8},{1,9},{4,12},{5,13},{8,0},{9,1},{12,4},{13,5},{2,10},{3,11},... | collective-permute-start | bytes 221192 | tf_op jit(solution)/shard_map/ppermute | solution.py:390
  13.2 9.6 %collective-permute-start.3 = (bf16[288,128]{1,0:T(8,128)(2,1)S(1)}, bf16[288,128]{1,0:T(8,128)(2,1)S(1)}, u32[]{:S(2)}, u32[]{:S(2)}) collective-permute-start(bf16[288,128]{1,0:T(8,128)(2,1)S(1)} %get-tuple-element.41), channel_id=1, source_target_pairs={{0,12},{1,5},{4,8},{5,1},{8,4},{9,13},{12,0},{13,9},{2,14},{3,7},{... | collective-permute-start | bytes 221192 | tf_op jit(solution)/shard_map/ppermute | solution.py:390
  16.9 8.6 %collective-permute-start.9 = (bf16[960,128]{1,0:T(8,128)(2,1)S(1)}, bf16[960,128]{1,0:T(8,128)(2,1)S(1)}, u32[]{:S(2)}, u32[]{:S(2)}) collective-permute-start(bf16[960,128]{1,0:T(8,128)(2,1)S(1)} %pad_maximum_fusion.1), channel_id=1, source_target_pairs={{2,0},{3,1},{6,4},{7,5},{10,8},{11,9},{14,12},{15,13},{18,16},{19,... | collective-permute-start | bytes 737288 | tf_op jit(solution)/shard_map/ppermute | solution.py:435
  19.5 9.7 %collective-permute-start.8 = (bf16[2,8,48,128]{3,2,1,0:T(8,128)(2,1)S(1)}, bf16[2,8,48,128]{3,2,1,0:T(8,128)(2,1)S(1)}, u32[]{:S(2)}, u32[]{:S(2)}) collective-permute-start(bf16[2,8,48,128]{3,2,1,0:T(8,128)(2,1)S(1)} %get-tuple-element.48.refs_4_), channel_id=1, source_target_pairs={{0,2},{1,3},{4,6},{5,7},{8,10},{9,11},{12,14},{13,15},{16,18},{17,... | collective-permute-start | bytes 589832 | tf_op jit(solution)/shard_map/ppermute | solution.py:479
  22.8 10.7 %collective-permute-start.7 = (bf16[2,8,48,128]{3,2,1,0:T(8,128)(2,1)S(1)}, bf16[2,8,48,128]{3,2,1,0:T(8,128)(2,1)S(1)}, u32[]{:S(2)}, u32[]{:S(2)}) collective-permute-start(bf16[2,8,48,128]{3,2,1,0:T(8,128)(2,1)S(1)} %get-tuple-element.52.refs_5_), channel_id=1, source_target_pairs={{0,2},{1,3},{4,6},{5,7},{8,10},{9,11},{12,14},{13,15},{16,18},{17,... | collective-permute-start | bytes 589832 | tf_op jit(solution)/shard_map/ppermute | solution.py:479
  25.5 13.7 %collective-permute-start.14 = (bf16[2,8,40,128]{3,2,1,0:T(8,128)(2,1)S(1)}, bf16[2,8,40,128]{3,2,1,0:T(8,128)(2,1)S(1)}, u32[]{:S(2)}, u32[]{:S(2)}) collective-permute-start(bf16[2,8,40,128]{3,2,1,0:T(8,128)(2,1)S(1)} %get-tuple-element.60.refs_1_), channel_id=1, source_target_pairs={{0,2},{1,3},{4,6},{5,7},{8,10},{9,11},{12,14},{13,15},{16,18},{17,... | collective-permute-start | bytes 491528 | tf_op jit(solution)/shard_map/ppermute | solution.py:479
  31.6 9.9 %collective-permute-start.13 = (bf16[2,8,40,128]{3,2,1,0:T(8,128)(2,1)S(1)}, bf16[2,8,40,128]{3,2,1,0:T(8,128)(2,1)S(1)}, u32[]{:S(2)}, u32[]{:S(2)}) collective-permute-start(bf16[2,8,40,128]{3,2,1,0:T(8,128)(2,1)S(1)} %get-tuple-element.67), channel_id=1, source_target_pairs={{0,2},{1,3},{4,6},{5,7},{8,10},{9,11},{12,14},{13,15},{16,18},{17,... | collective-permute-start | bytes 491528 | tf_op jit(solution)/shard_map/ppermute | solution.py:479
  35.8 8.1 %collective-permute-start.10 = (bf16[2,4,32,128]{3,2,1,0:T(8,128)(2,1)S(1)}, bf16[2,4,32,128]{3,2,1,0:T(8,128)(2,1)S(1)}, u32[]{:S(2)}, u32[]{:S(2)}) collective-permute-start(bf16[2,4,32,128]{3,2,1,0:T(8,128)(2,1)S(1)} %get-tuple-element.80), channel_id=1, source_target_pairs={{0,4},{1,13},{4,0},{5,9},{8,12},{9,5},{12,8},{13,1},{2,6},{3,15},{... | collective-permute-start | bytes 196616 | tf_op jit(solution)/shard_map/ppermute | solution.py:390
  44.0 13.5 %collective-permute-start.15 = (bf16[2,5,32,128]{3,2,1,0:T(8,128)(2,1)S(1)}, bf16[2,5,32,128]{3,2,1,0:T(8,128)(2,1)S(1)}, u32[]{:S(2)}, u32[]{:S(2)}) collective-permute-start(bf16[2,5,32,128]{3,2,1,0:T(8,128)(2,1)S(1)} %get-tuple-element.76), channel_id=1, source_target_pairs={{0,4},{1,13},{4,0},{5,9},{8,12},{9,5},{12,8},{13,1},{2,6},{3,15},{... | collective-permute-start | bytes 245768 | tf_op jit(solution)/shard_map/ppermute | solution.py:390
  45.7 11.7 %collective-permute-start.16 = (bf16[2,5,32,128]{3,2,1,0:T(8,128)(2,1)S(1)}, bf16[2,5,32,128]{3,2,1,0:T(8,128)(2,1)S(1)}, u32[]{:S(2)}, u32[]{:S(2)}) collective-permute-start(bf16[2,5,32,128]{3,2,1,0:T(8,128)(2,1)S(1)} %get-tuple-element.75), channel_id=1, source_target_pairs={{0,8},{1,9},{4,12},{5,13},{8,0},{9,1},{12,4},{13,5},{2,10},{3,11},... | collective-permute-start | bytes 245768 | tf_op jit(solution)/shard_map/ppermute | solution.py:390
  48.9 8.6 %collective-permute-start.17 = (bf16[2,5,32,128]{3,2,1,0:T(8,128)(2,1)S(1)}, bf16[2,5,32,128]{3,2,1,0:T(8,128)(2,1)S(1)}, u32[]{:S(2)}, u32[]{:S(2)}) collective-permute-start(bf16[2,5,32,128]{3,2,1,0:T(8,128)(2,1)S(1)} %get-tuple-element.74), channel_id=1, source_target_pairs={{0,12},{1,5},{4,8},{5,1},{8,4},{9,13},{12,0},{13,9},{2,14},{3,7},{... | collective-permute-start | bytes 245768 | tf_op jit(solution)/shard_map/ppermute | solution.py:390
  49.2 7.1 %collective-permute-start.11 = (bf16[2,4,32,128]{3,2,1,0:T(8,128)(2,1)S(1)}, bf16[2,4,32,128]{3,2,1,0:T(8,128)(2,1)S(1)}, u32[]{:S(2)}, u32[]{:S(2)}) collective-permute-start(bf16[2,4,32,128]{3,2,1,0:T(8,128)(2,1)S(1)} %get-tuple-element.79), channel_id=1, source_target_pairs={{0,8},{1,9},{4,12},{5,13},{8,0},{9,1},{12,4},{13,5},{2,10},{3,11},... | collective-permute-start | bytes 196616 | tf_op jit(solution)/shard_map/ppermute | solution.py:390
  51.3 6.2 %collective-permute-start.12 = (bf16[2,4,32,128]{3,2,1,0:T(8,128)(2,1)S(1)}, bf16[2,4,32,128]{3,2,1,0:T(8,128)(2,1)S(1)}, u32[]{:S(2)}, u32[]{:S(2)}) collective-permute-start(bf16[2,4,32,128]{3,2,1,0:T(8,128)(2,1)S(1)} %get-tuple-element.78), channel_id=1, source_target_pairs={{0,12},{1,5},{4,8},{5,1},{8,4},{9,13},{12,0},{13,9},{2,14},{3,7},{... | collective-permute-start | bytes 196616 | tf_op jit(solution)/shard_map/ppermute | solution.py:390

commit v5 on v4

--- a/solution.py
+++ b/solution.py
@@ -13,7 +13,7 @@
 LAG = 3
 FIRST = 2
 LENT = 3
-EARLY_OUT = 4
+EARLY_OUT = 6
 LEND_AFTER = False
 SPREAD = True
 LEND_ONE_WAY = True

time: 58.6 us -> 58.5 us (level)
  starting transfers between devices: 30.8 us -> 29.8 us
  waiting for transfers between devices: 13.6 us -> 14.5 us
    ppermute x4, waiting for transfers between devices: 2.91 us -> 4.09 us  [shards(): sent[phase, number] = lax.ppermute(hidden, 'pipe', ring)]
    ppermute x12, starting transfers between devices: 23.1 us -> 22.1 us  [exchange(): got.append(lax.ppermute(pieces[number], ('rows', 'cols'), route))]
  transfers between devices with their start and end apart: 18 -> 18, of which waited for: 8 -> 10; matrix products, arithmetic and copies ran while one was open for 0% -> 0% of each run, Pallas kernels for 16% -> 17%
where the time goes in v5:
time: 58.5 us; the launch traced here: 58.2 us
  starting transfers between devices  29.8 us (51%)
  waiting for transfers between devices  14.5 us (25%)
  Pallas kernels  10.7 us (18%)
  other arithmetic  2.18 us (4%)
  between operations  0.87 us (1%)
    ppermute x12, starting transfers between devices, exchange(): got.append(lax.ppermute(pieces[number], ('rows', 'cols'), route))  22.1 us
    pallas_call x8, Pallas kernels, advance(): pl.pallas_call(functools.partial(chunk_kernel, plan, phase, first_step, l...  9.43 us
    ppermute x12, waiting for transfers between devices, exchange(): got.append(lax.ppermute(pieces[number], ('rows', 'cols'), route))  7.69 us
    ppermute x4, starting transfers between devices, shards(): sent[phase, number] = lax.ppermute(hidden, 'pipe', ring)  5.15 us
    ppermute x4, waiting for transfers between devices, shards(): sent[phase, number] = lax.ppermute(hidden, 'pipe', ring)  4.09 us
    ppermute x1, starting transfers between devices, shards(): lent = [lax.ppermute(borrowed, 'pipe', back)]  2.49 us
    ppermute x1, waiting for transfers between devices, shards(): lent = [lax.ppermute(borrowed, 'pipe', back)]  1.47 us
    ppermute x1, waiting for transfers between devices, shards(): left = right = lax.ppermute(beside, 'cols', [(0, 1), (1, 0)])  1.26 us
  transfers between devices with their start and end apart: 18, of which 10 were waited for; matrix products, arithmetic and copies ran while one was open for 0% of the time, Pallas kernels for 17%

profile of v5, /device:TPU:6, one launch (start us, length us, event | category | flops | bytes accessed | tf_op | source)
XLA Modules:
  0.0 58.2 jit_solution(9009202681630877134)
XLA Ops:
  0.6 0.0 copy-start
  0.6 0.0 copy-start.1
  0.7 1.1 %convert_element_type.3 = bf16[1,2,128,128]{3,2,1,0:T(8,128)(2,1)S(1)} convert(f32[1,2,128,128]{3,2,1,0:T(8,128)} %param.7) | non-fusion elementwise | flops 32768 | bytes 196608 | tf_op jit(solution)/shard_map/convert_element_type | solution.py:406
  1.7 1.1 %pad_maximum_fusion.maps = bf16[10,2,128,128]{3,2,1,0:T(8,128)(2,1)S(1)} fusion(bf16[8,2,128,128]{3,2,1,0:T(8,128)(2,1)} %param.5, bf16[1,2,128,128]{3,2,1,0:T(8,128)(2,1)S(1)} %convert_element_type.3, bf16[1,2,128,128]{3,2,1,0:T(8,128)(2,1)} %param.6), kind=kLoop, calls=%fused_computation | loop fusion | flops 655360 | bytes 1310720 | tf_op jit(solution)/shard_map/concatenate | solution.py:406
  2.9 0.1 collective-permute-start
  2.9 1.3 %collective-permute-done.left.right = bf16[10,2,16,128]{3,2,1,0:T(8,128)(2,1)S(1)} collective-permute-done((bf16[10,2,16,128]{3,2,1,0:T(8,128)(2,1)S(1)}, bf16[10,2,16,128]{3,2,1,0:T(8,128)(2,1)S(1)}, u32[]{:S(2)}, u32[]{:S(2)}) %collective-permute-start) | collective-permute-done | bytes 81952 | tf_op jit(solution)/shard_map/ppermute | solution.py:415
  4.2 0.1 shard_map.69
  4.3 1.6 %collective-permute-start.4 = (bf16[416,128]{1,0:T(8,128)(2,1)S(1)}, bf16[416,128]{1,0:T(8,128)(2,1)S(1)}, u32[]{:S(2)}, u32[]{:S(2)}) collective-permute-start(bf16[416,128]{1,0:T(8,128)(2,1)S(1)} %get-tuple-element.44), channel_id=1, source_target_pairs={{0,4},{1,13},{4,0},{5,9},{8,12},{9,5},{12,8},{13,1},{2,6},{3,15},{... | collective-permute-start | bytes 319496 | tf_op jit(solution)/shard_map/ppermute | solution.py:390
  6.0 2.6 %collective-permute-start.5 = (bf16[416,128]{1,0:T(8,128)(2,1)S(1)}, bf16[416,128]{1,0:T(8,128)(2,1)S(1)}, u32[]{:S(2)}, u32[]{:S(2)}) collective-permute-start(bf16[416,128]{1,0:T(8,128)(2,1)S(1)} %get-tuple-element.45), channel_id=1, source_target_pairs={{0,8},{1,9},{4,12},{5,13},{8,0},{9,1},{12,4},{13,5},{2,10},{3,11},... | collective-permute-start | bytes 319496 | tf_op jit(solution)/shard_map/ppermute | solution.py:390
  8.6 0.2 collective-permute-start.6
  8.8 0.7 %collective-permute-start.1 = (bf16[288,128]{1,0:T(8,128)(2,1)S(1)}, bf16[288,128]{1,0:T(8,128)(2,1)S(1)}, u32[]{:S(2)}, u32[]{:S(2)}) collective-permute-start(bf16[288,128]{1,0:T(8,128)(2,1)S(1)} %get-tuple-element.40), channel_id=1, source_target_pairs={{0,4},{1,13},{4,0},{5,9},{8,12},{9,5},{12,8},{13,1},{2,6},{3,15},{... | collective-permute-start | bytes 221192 | tf_op jit(solution)/shard_map/ppermute | solution.py:390
  9.5 3.5 %collective-permute-start.2 = (bf16[288,128]{1,0:T(8,128)(2,1)S(1)}, bf16[288,128]{1,0:T(8,128)(2,1)S(1)}, u32[]{:S(2)}, u32[]{:S(2)}) collective-permute-start(bf16[288,128]{1,0:T(8,128)(2,1)S(1)} %get-tuple-element.41), channel_id=1, source_target_pairs={{0,8},{1,9},{4,12},{5,13},{8,0},{9,1},{12,4},{13,5},{2,10},{3,11},... | collective-permute-start | bytes 221192 | tf_op jit(solution)/shard_map/ppermute | solution.py:390
  13.0 0.0 copy-done
  13.0 0.0 copy-done.1
  13.0 0.2 shard_map.70
  13.2 0.0 collective-permute-done.4.refs_1_
  13.2 2.4 %collective-permute-start.3 = (bf16[288,128]{1,0:T(8,128)(2,1)S(1)}, bf16[288,128]{1,0:T(8,128)(2,1)S(1)}, u32[]{:S(2)}, u32[]{:S(2)}) collective-permute-start(bf16[288,128]{1,0:T(8,128)(2,1)S(1)} %get-tuple-element.42), channel_id=1, source_target_pairs={{0,12},{1,5},{4,8},{5,1},{8,4},{9,13},{12,0},{13,9},{2,14},{3,7},{... | collective-permute-start | bytes 221192 | tf_op jit(solution)/shard_map/ppermute | solution.py:390
  15.6 0.0 collective-permute-done.5.refs_2_
  15.6 1.3 %collective-permute-done.6.refs_3_ = bf16[416,128]{1,0:T(8,128)(2,1)S(1)} collective-permute-done((bf16[416,128]{1,0:T(8,128)(2,1)S(1)}, bf16[416,128]{1,0:T(8,128)(2,1)S(1)}, u32[]{:S(2)}, u32[]{:S(2)}) %collective-permute-start.6) | collective-permute-done | bytes 106528 | tf_op jit(solution)/shard_map/ppermute | solution.py:390
  16.9 2.5 %collective-permute-start.7 = (bf16[960,128]{1,0:T(8,128)(2,1)S(1)}, bf16[960,128]{1,0:T(8,128)(2,1)S(1)}, u32[]{:S(2)}, u32[]{:S(2)}) collective-permute-start(bf16[960,128]{1,0:T(8,128)(2,1)S(1)} %pad_maximum_fusion.1), channel_id=1, source_target_pairs={{2,0},{3,1},{6,4},{7,5},{10,8},{11,9},{14,12},{15,13},{18,16},{19,... | collective-permute-start | bytes 737288 | tf_op jit(solution)/shard_map/ppermute | solution.py:435
  19.4 0.1 broadcast_in_dim.6.refs_6_
  19.5 1.3 %collective-permute-start.10 = (bf16[2,8,48,128]{3,2,1,0:T(8,128)(2,1)S(1)}, bf16[2,8,48,128]{3,2,1,0:T(8,128)(2,1)S(1)}, u32[]{:S(2)}, u32[]{:S(2)}) collective-permute-start(bf16[2,8,48,128]{3,2,1,0:T(8,128)(2,1)S(1)} %get-tuple-element.49.refs_4_), channel_id=1, source_target_pairs={{0,2},{1,3},{4,6},{5,7},{8,10},{9,11},{12,14},{13,15},{16,18},{17,... | collective-permute-start | bytes 589832 | tf_op jit(solution)/shard_map/ppermute | solution.py:479
  20.8 0.0 collective-permute-done.1.refs_1_
  20.8 1.9 %collective-permute-done.2.refs_2_ = bf16[288,128]{1,0:T(8,128)(2,1)S(1)} collective-permute-done((bf16[288,128]{1,0:T(8,128)(2,1)S(1)}, bf16[288,128]{1,0:T(8,128)(2,1)S(1)}, u32[]{:S(2)}, u32[]{:S(2)}) %collective-permute-start.2) | collective-permute-done | bytes 73760 | tf_op jit(solution)/shard_map/ppermute | solution.py:390
  22.8 0.0 collective-permute-done.3.refs_3_
  22.8 1.3 %collective-permute-start.9 = (bf16[2,8,48,128]{3,2,1,0:T(8,128)(2,1)S(1)}, bf16[2,8,48,128]{3,2,1,0:T(8,128)(2,1)S(1)}, u32[]{:S(2)}, u32[]{:S(2)}) collective-permute-start(bf16[2,8,48,128]{3,2,1,0:T(8,128)(2,1)S(1)} %get-tuple-element.53.refs_5_), channel_id=1, source_target_pairs={{0,2},{1,3},{4,6},{5,7},{8,10},{9,11},{12,14},{13,15},{16,18},{17,... | collective-permute-start | bytes 589832 | tf_op jit(solution)/shard_map/ppermute | solution.py:479
  24.0 1.5 %collective-permute-done.7.refs_4_.refs_0_ = bf16[960,128]{1,0:T(8,128)(2,1)S(1)} collective-permute-done((bf16[960,128]{1,0:T(8,128)(2,1)S(1)}, bf16[960,128]{1,0:T(8,128)(2,1)S(1)}, u32[]{:S(2)}, u32[]{:S(2)}) %collective-permute-start.7) | collective-permute-done | bytes 245792 | tf_op jit(solution)/shard_map/ppermute | solution.py:435
  25.5 1.3 %collective-permute-start.8 = (bf16[2,8,40,128]{3,2,1,0:T(8,128)(2,1)S(1)}, bf16[2,8,40,128]{3,2,1,0:T(8,128)(2,1)S(1)}, u32[]{:S(2)}, u32[]{:S(2)}) collective-permute-start(bf16[2,8,40,128]{3,2,1,0:T(8,128)(2,1)S(1)} %get-tuple-element.57.refs_1_), channel_id=1, source_target_pairs={{0,2},{1,3},{4,6},{5,7},{8,10},{9,11},{12,14},{13,15},{16,18},{17,... | collective-permute-start | bytes 491528 | tf_op jit(solution)/shard_map/ppermute | solution.py:479
  26.8 2.4 %collective-permute-done.10.refs_4_ = bf16[2,8,48,128]{3,2,1,0:T(8,128)(2,1)S(1)} collective-permute-done((bf16[2,8,48,128]{3,2,1,0:T(8,128)(2,1)S(1)}, bf16[2,8,48,128]{3,2,1,0:T(8,128)(2,1)S(1)}, u32[]{:S(2)}, u32[]{:S(2)}) %collective-permute-start.10) | collective-permute-done | bytes 196640 | tf_op jit(solution)/shard_map/ppermute | solution.py:479
  29.2 2.4 %shard_map.74 = (bf16[2,8,48,128]{3,2,1,0:T(8,128)(2,1)S(1)}, f32[384,128]{1,0:T(8,128)S(1)}, bf16[8,6,48,128]{3,2,1,0:T(8,128)(2,1)S(1)}, bf16[8,3,48,128]{3,2,1,0:T(8,128)(2,1)S(1)}) custom-call(bf16[288,128]{1,0:T(8,128)(2,1)S(1)} %get-tuple-element.39.refs_0_, ...), custom_call_target="tpu_custom_call", output_to_operand_aliasing={{2}: (7, {}), {3}: (8, {})} | custom-call | flops 1811939328 | bytes 1000000 | tf_op jit(solution)/shard_map/pallas_call | solution.py:311
  31.6 1.3 %collective-permute-start.14 = (bf16[2,8,40,128]{3,2,1,0:T(8,128)(2,1)S(1)}, bf16[2,8,40,128]{3,2,1,0:T(8,128)(2,1)S(1)}, u32[]{:S(2)}, u32[]{:S(2)}) collective-permute-start(bf16[2,8,40,128]{3,2,1,0:T(8,128)(2,1)S(1)} %get-tuple-element.72), channel_id=1, source_target_pairs={{0,2},{1,3},{4,6},{5,7},{8,10},{9,11},{12,14},{13,15},{16,18},{17,... | collective-permute-start | bytes 491528 | tf_op jit(solution)/shard_map/ppermute | solution.py:479
  32.9 0.5 collective-permute-done.9.refs_0_
  33.4 2.3 %shard_map.76 = (bf16[2,8,48,128]{3,2,1,0:T(8,128)(2,1)S(1)}, f32[384,128]{1,0:T(8,128)S(1)}, bf16[8,6,48,128]{3,2,1,0:T(8,128)(2,1)S(1)}, bf16[8,3,48,128]{3,2,1,0:T(8,128)(2,1)S(1)}) custom-call(bf16[2,8,48,128]{3,2,1,0:T(8,128)(2,1)S(1)} %collective-permute-done.9.refs_0_, ...), custom_call_target="tpu_custom_call", output_to_operand_aliasing={{2}: (5, {}), {3}: (6, {})} | custom-call | flops 1811939328 | bytes 1000000 | tf_op jit(solution)/shard_map/pallas_call | solution.py:311
  35.7 1.2 %collective-permute-done.8.refs_0_ = bf16[2,8,40,128]{3,2,1,0:T(8,128)(2,1)S(1)} collective-permute-done((bf16[2,8,40,128]{3,2,1,0:T(8,128)(2,1)S(1)}, bf16[2,8,40,128]{3,2,1,0:T(8,128)(2,1)S(1)}, u32[]{:S(2)}, u32[]{:S(2)}) %collective-permute-start.8) | collective-permute-done | bytes 163872 | tf_op jit(solution)/shard_map/ppermute | solution.py:479
  36.9 2.4 %shard_map.77 = (bf16[2,8,40,128]{3,2,1,0:T(8,128)(2,1)S(1)}, f32[384,128]{1,0:T(8,128)S(1)}, bf16[8,6,48,128]{3,2,1,0:T(8,128)(2,1)S(1)}, bf16[8,3,48,128]{3,2,1,0:T(8,128)(2,1)S(1)}) custom-call(bf16[2,8,40,128]{3,2,1,0:T(8,128)(2,1)S(1)} %collective-permute-done.8.refs_0_, ...), custom_call_target="tpu_custom_call", output_to_operand_aliasing={{2}: (5, {}), {3}: (6, {})} | custom-call | flops 1811939328 | bytes 1000000 | tf_op jit(solution)/shard_map/pallas_call | solution.py:311
  39.3 2.5 %collective-permute-start.11 = (bf16[2,6,32,128]{3,2,1,0:T(8,128)(2,1)S(1)}, bf16[2,6,32,128]{3,2,1,0:T(8,128)(2,1)S(1)}, u32[]{:S(2)}, u32[]{:S(2)}) collective-permute-start(bf16[2,6,32,128]{3,2,1,0:T(8,128)(2,1)S(1)} %get-tuple-element.78), channel_id=1, source_target_pairs={{0,4},{1,13},{4,0},{5,9},{8,12},{9,5},{12,8},{13,1},{2,6},{3,15},{... | collective-permute-start | bytes 294920 | tf_op jit(solution)/shard_map/ppermute | solution.py:390
  41.9 2.8 %collective-permute-start.12 = (bf16[2,6,32,128]{3,2,1,0:T(8,128)(2,1)S(1)}, bf16[2,6,32,128]{3,2,1,0:T(8,128)(2,1)S(1)}, u32[]{:S(2)}, u32[]{:S(2)}) collective-permute-start(bf16[2,6,32,128]{3,2,1,0:T(8,128)(2,1)S(1)} %get-tuple-element.77), channel_id=1, source_target_pairs={{0,8},{1,9},{4,12},{5,13},{8,0},{9,1},{12,4},{13,5},{2,10},{3,11},... | collective-permute-start | bytes 294920 | tf_op jit(solution)/shard_map/ppermute | solution.py:390
  44.6 1.4 %collective-permute-start.13 = (bf16[2,6,32,128]{3,2,1,0:T(8,128)(2,1)S(1)}, bf16[2,6,32,128]{3,2,1,0:T(8,128)(2,1)S(1)}, u32[]{:S(2)}, u32[]{:S(2)}) collective-permute-start(bf16[2,6,32,128]{3,2,1,0:T(8,128)(2,1)S(1)} %get-tuple-element.76), channel_id=1, source_target_pairs={{0,12},{1,5},{4,8},{5,1},{8,4},{9,13},{12,0},{13,9},{2,14},{3,7},{... | collective-permute-start | bytes 294920 | tf_op jit(solution)/shard_map/ppermute | solution.py:390
  46.0 0.0 collective-permute-done.14.refs_0_
  46.0 2.3 %shard_map.78.refs_1_ = bf16[8,3,48,128]{3,2,1,0:T(8,128)(2,1)S(1)} custom-call(bf16[2,8,40,128]{3,2,1,0:T(8,128)(2,1)S(1)} %collective-permute-done.14.refs_0_, bf16[2,8,40,128]{3,2,1,0:T(8,128)(2,1)S(1)} %get-tuple-element.73.refs_1_, f32[384,128]{1,0:T(8,128)S(1)} %get-tuple-element.74.refs_2_, ...), custom_call_target="tpu_custom_call", output_to_operand_aliasing={{}: (5, {})} | custom-call | flops 1811939328 | bytes 1000000 | tf_op jit(solution)/shard_map/pallas_call | solution.py:311
  48.4 0.0 collective-permute-done.11.refs_0_.refs_1_
  48.4 0.6 %collective-permute-start.15 = (bf16[2,3,32,128]{3,2,1,0:T(8,128)(2,1)S(1)}, bf16[2,3,32,128]{3,2,1,0:T(8,128)(2,1)S(1)}, u32[]{:S(2)}, u32[]{:S(2)}) collective-permute-start(bf16[2,3,32,128]{3,2,1,0:T(8,128)(2,1)S(1)} %get-tuple-element.82), channel_id=1, source_target_pairs={{0,4},{1,13},{4,0},{5,9},{8,12},{9,5},{12,8},{13,1},{2,6},{3,15},{... | collective-permute-start | bytes 147464 | tf_op jit(solution)/shard_map/ppermute | solution.py:390
  49.0 2.4 %collective-permute-start.16 = (bf16[2,3,32,128]{3,2,1,0:T(8,128)(2,1)S(1)}, bf16[2,3,32,128]{3,2,1,0:T(8,128)(2,1)S(1)}, u32[]{:S(2)}, u32[]{:S(2)}) collective-permute-start(bf16[2,3,32,128]{3,2,1,0:T(8,128)(2,1)S(1)} %get-tuple-element.81), channel_id=1, source_target_pairs={{0,8},{1,9},{4,12},{5,13},{8,0},{9,1},{12,4},{13,5},{2,10},{3,11},... | collective-permute-start | bytes 147464 | tf_op jit(solution)/shard_map/ppermute | solution.py:390
  51.5 1.4 %collective-permute-start.17 = (bf16[2,3,32,128]{3,2,1,0:T(8,128)(2,1)S(1)}, bf16[2,3,32,128]{3,2,1,0:T(8,128)(2,1)S(1)}, u32[]{:S(2)}, u32[]{:S(2)}) collective-permute-start(bf16[2,3,32,128]{3,2,1,0:T(8,128)(2,1)S(1)} %get-tuple-element.80), channel_id=1, source_target_pairs={{0,12},{1,5},{4,8},{5,1},{8,4},{9,13},{12,0},{13,9},{2,14},{3,7},{... | collective-permute-start | bytes 147464 | tf_op jit(solution)/shard_map/ppermute | solution.py:390
  52.9 0.0 collective-permute-done.12.refs_2_
  52.9 0.0 collective-permute-done.13.refs_3_
  52.9 0.1 collective-permute-done.15.refs_5_
  52.9 1.1 %collective-permute-done.16.refs_6_ = bf16[2,3,32,128]{3,2,1,0:T(8,128)(2,1)S(1)} collective-permute-done((bf16[2,3,32,128]{3,2,1,0:T(8,128)(2,1)S(1)}, bf16[2,3,32,128]{3,2,1,0:T(8,128)(2,1)S(1)}, u32[]{:S(2)}, u32[]{:S(2)}) %collective-permute-start.16) | collective-permute-done | bytes 49184 | tf_op jit(solution)/shard_map/ppermute | solution.py:390
  54.0 3.3 %collective-permute-done.17.refs_7_ = bf16[2,3,32,128]{3,2,1,0:T(8,128)(2,1)S(1)} collective-permute-done((bf16[2,3,32,128]{3,2,1,0:T(8,128)(2,1)S(1)}, bf16[2,3,32,128]{3,2,1,0:T(8,128)(2,1)S(1)}, u32[]{:S(2)}, u32[]{:S(2)}) %collective-permute-start.17) | collective-permute-done | bytes 49184 | tf_op jit(solution)/shard_map/ppermute | solution.py:390
  57.4 0.9 %shard_map.80 = (bf16[1,8,2,128,128]{4,3,2,1,0:T(8,128)(2,1)}, f32[1,2,128,128]{3,2,1,0:T(8,128)}) custom-call(bf16[2,6,32,128]{3,2,1,0:T(8,128)(2,1)S(1)} %get-tuple-element.79.refs_0_, bf16[2,6,32,128]{3,2,1,0:T(8,128)(2,1)S(1)} %collective-permute-done.11.refs_0_.refs_1_, bf16[2,6,32,128]{3,2,1,0:T(8,128)(2,1)S(1)} %collective-permute-done.12.refs_2_, ...), custom_call_target="tpu_custom_call" | custom-call | tf_op jit(solution)/shard_map/pallas_call | solution.py:486
  (14 shorter events, 0.2 us)
Async XLA Ops:
  0.6 12.3 %copy-start = (bf16[1,2304,512]{2,1,0:T(8,128)(2,1)S(1)}, bf16[1,2304,512]{2,1,0:T(8,128)(2,1)}, u32[]{:S(2)}) copy-start(bf16[1,2304,512]{2,1,0:T(8,128)(2,1)} %param.8) | copy-start | bytes 7077892
  0.6 12.3 %copy-start.1 = (f32[1,512]{1,0:T(1,128)S(1)}, f32[1,512]{1,0:T(1,128)}, u32[]{:S(2)}) copy-start(f32[1,512]{1,0:T(1,128)} %bias_in.1) | copy-start | bytes 6148
  2.9 1.3 %collective-permute-start = (bf16[10,2,16,128]{3,2,1,0:T(8,128)(2,1)S(1)}, bf16[10,2,16,128]{3,2,1,0:T(8,128)(2,1)S(1)}, u32[]{:S(2)}, u32[]{:S(2)}) collective-permute-start(bf16[10,2,16,128]{3,2,1,0:T(8,128)(2,1)S(1)} %shard_map.68), channel_id=1, source_target_pairs={{0,1},{1,0},{2,3},{3,2},{4,5},{5,4},{6,7},{7,6},{8,9},{9,8},{10,11... | collective-permute-start | bytes 245768 | tf_op jit(solution)/shard_map/ppermute | solution.py:415
  4.3 8.8 %collective-permute-start.4 = (bf16[416,128]{1,0:T(8,128)(2,1)S(1)}, bf16[416,128]{1,0:T(8,128)(2,1)S(1)}, u32[]{:S(2)}, u32[]{:S(2)}) collective-permute-start(bf16[416,128]{1,0:T(8,128)(2,1)S(1)} %get-tuple-element.44), channel_id=1, source_target_pairs={{0,4},{1,13},{4,0},{5,9},{8,12},{9,5},{12,8},{13,1},{2,6},{3,15},{... | collective-permute-start | bytes 319496 | tf_op jit(solution)/shard_map/ppermute | solution.py:390
  6.0 9.6 %collective-permute-start.5 = (bf16[416,128]{1,0:T(8,128)(2,1)S(1)}, bf16[416,128]{1,0:T(8,128)(2,1)S(1)}, u32[]{:S(2)}, u32[]{:S(2)}) collective-permute-start(bf16[416,128]{1,0:T(8,128)(2,1)S(1)} %get-tuple-element.45), channel_id=1, source_target_pairs={{0,8},{1,9},{4,12},{5,13},{8,0},{9,1},{12,4},{13,5},{2,10},{3,11},... | collective-permute-start | bytes 319496 | tf_op jit(solution)/shard_map/ppermute | solution.py:390
  8.6 8.3 %collective-permute-start.6 = (bf16[416,128]{1,0:T(8,128)(2,1)S(1)}, bf16[416,128]{1,0:T(8,128)(2,1)S(1)}, u32[]{:S(2)}, u32[]{:S(2)}) collective-permute-start(bf16[416,128]{1,0:T(8,128)(2,1)S(1)} %get-tuple-element.46), channel_id=1, source_target_pairs={{0,12},{1,5},{4,8},{5,1},{8,4},{9,13},{12,0},{13,9},{2,14},{3,7},{... | collective-permute-start | bytes 319496 | tf_op jit(solution)/shard_map/ppermute | solution.py:390
  8.8 12.0 %collective-permute-start.1 = (bf16[288,128]{1,0:T(8,128)(2,1)S(1)}, bf16[288,128]{1,0:T(8,128)(2,1)S(1)}, u32[]{:S(2)}, u32[]{:S(2)}) collective-permute-start(bf16[288,128]{1,0:T(8,128)(2,1)S(1)} %get-tuple-element.40), channel_id=1, source_target_pairs={{0,4},{1,13},{4,0},{5,9},{8,12},{9,5},{12,8},{13,1},{2,6},{3,15},{... | collective-permute-start | bytes 221192 | tf_op jit(solution)/shard_map/ppermute | solution.py:390
  9.5 13.3 %collective-permute-start.2 = (bf16[288,128]{1,0:T(8,128)(2,1)S(1)}, bf16[288,128]{1,0:T(8,128)(2,1)S(1)}, u32[]{:S(2)}, u32[]{:S(2)}) collective-permute-start(bf16[288,128]{1,0:T(8,128)(2,1)S(1)} %get-tuple-element.41), channel_id=1, source_target_pairs={{0,8},{1,9},{4,12},{5,13},{8,0},{9,1},{12,4},{13,5},{2,10},{3,11},... | collective-permute-start | bytes 221192 | tf_op jit(solution)/shard_map/ppermute | solution.py:390
  13.2 9.6 %collective-permute-start.3 = (bf16[288,128]{1,0:T(8,128)(2,1)S(1)}, bf16[288,128]{1,0:T(8,128)(2,1)S(1)}, u32[]{:S(2)}, u32[]{:S(2)}) collective-permute-start(bf16[288,128]{1,0:T(8,128)(2,1)S(1)} %get-tuple-element.42), channel_id=1, source_target_pairs={{0,12},{1,5},{4,8},{5,1},{8,4},{9,13},{12,0},{13,9},{2,14},{3,7},{... | collective-permute-start | bytes 221192 | tf_op jit(solution)/shard_map/ppermute | solution.py:390
  16.9 8.6 %collective-permute-start.7 = (bf16[960,128]{1,0:T(8,128)(2,1)S(1)}, bf16[960,128]{1,0:T(8,128)(2,1)S(1)}, u32[]{:S(2)}, u32[]{:S(2)}) collective-permute-start(bf16[960,128]{1,0:T(8,128)(2,1)S(1)} %pad_maximum_fusion.1), channel_id=1, source_target_pairs={{2,0},{3,1},{6,4},{7,5},{10,8},{11,9},{14,12},{15,13},{18,16},{19,... | collective-permute-start | bytes 737288 | tf_op jit(solution)/shard_map/ppermute | solution.py:435
  19.5 9.7 %collective-permute-start.10 = (bf16[2,8,48,128]{3,2,1,0:T(8,128)(2,1)S(1)}, bf16[2,8,48,128]{3,2,1,0:T(8,128)(2,1)S(1)}, u32[]{:S(2)}, u32[]{:S(2)}) collective-permute-start(bf16[2,8,48,128]{3,2,1,0:T(8,128)(2,1)S(1)} %get-tuple-element.49.refs_4_), channel_id=1, source_target_pairs={{0,2},{1,3},{4,6},{5,7},{8,10},{9,11},{12,14},{13,15},{16,18},{17,... | collective-permute-start | bytes 589832 | tf_op jit(solution)/shard_map/ppermute | solution.py:479
  22.8 10.7 %collective-permute-start.9 = (bf16[2,8,48,128]{3,2,1,0:T(8,128)(2,1)S(1)}, bf16[2,8,48,128]{3,2,1,0:T(8,128)(2,1)S(1)}, u32[]{:S(2)}, u32[]{:S(2)}) collective-permute-start(bf16[2,8,48,128]{3,2,1,0:T(8,128)(2,1)S(1)} %get-tuple-element.53.refs_5_), channel_id=1, source_target_pairs={{0,2},{1,3},{4,6},{5,7},{8,10},{9,11},{12,14},{13,15},{16,18},{17,... | collective-permute-start | bytes 589832 | tf_op jit(solution)/shard_map/ppermute | solution.py:479
  25.5 11.4 %collective-permute-start.8 = (bf16[2,8,40,128]{3,2,1,0:T(8,128)(2,1)S(1)}, bf16[2,8,40,128]{3,2,1,0:T(8,128)(2,1)S(1)}, u32[]{:S(2)}, u32[]{:S(2)}) collective-permute-start(bf16[2,8,40,128]{3,2,1,0:T(8,128)(2,1)S(1)} %get-tuple-element.57.refs_1_), channel_id=1, source_target_pairs={{0,2},{1,3},{4,6},{5,7},{8,10},{9,11},{12,14},{13,15},{16,18},{17,... | collective-permute-start | bytes 491528 | tf_op jit(solution)/shard_map/ppermute | solution.py:479
  31.6 14.4 %collective-permute-start.14 = (bf16[2,8,40,128]{3,2,1,0:T(8,128)(2,1)S(1)}, bf16[2,8,40,128]{3,2,1,0:T(8,128)(2,1)S(1)}, u32[]{:S(2)}, u32[]{:S(2)}) collective-permute-start(bf16[2,8,40,128]{3,2,1,0:T(8,128)(2,1)S(1)} %get-tuple-element.72), channel_id=1, source_target_pairs={{0,2},{1,3},{4,6},{5,7},{8,10},{9,11},{12,14},{13,15},{16,18},{17,... | collective-permute-start | bytes 491528 | tf_op jit(solution)/shard_map/ppermute | solution.py:479
  39.3 9.0 %collective-permute-start.11 = (bf16[2,6,32,128]{3,2,1,0:T(8,128)(2,1)S(1)}, bf16[2,6,32,128]{3,2,1,0:T(8,128)(2,1)S(1)}, u32[]{:S(2)}, u32[]{:S(2)}) collective-permute-start(bf16[2,6,32,128]{3,2,1,0:T(8,128)(2,1)S(1)} %get-tuple-element.78), channel_id=1, source_target_pairs={{0,4},{1,13},{4,0},{5,9},{8,12},{9,5},{12,8},{13,1},{2,6},{3,15},{... | collective-permute-start | bytes 294920 | tf_op jit(solution)/shard_map/ppermute | solution.py:390
  41.9 11.0 %collective-permute-start.12 = (bf16[2,6,32,128]{3,2,1,0:T(8,128)(2,1)S(1)}, bf16[2,6,32,128]{3,2,1,0:T(8,128)(2,1)S(1)}, u32[]{:S(2)}, u32[]{:S(2)}) collective-permute-start(bf16[2,6,32,128]{3,2,1,0:T(8,128)(2,1)S(1)} %get-tuple-element.77), channel_id=1, source_target_pairs={{0,8},{1,9},{4,12},{5,13},{8,0},{9,1},{12,4},{13,5},{2,10},{3,11},... | collective-permute-start | bytes 294920 | tf_op jit(solution)/shard_map/ppermute | solution.py:390
  44.6 8.2 %collective-permute-start.13 = (bf16[2,6,32,128]{3,2,1,0:T(8,128)(2,1)S(1)}, bf16[2,6,32,128]{3,2,1,0:T(8,128)(2,1)S(1)}, u32[]{:S(2)}, u32[]{:S(2)}) collective-permute-start(bf16[2,6,32,128]{3,2,1,0:T(8,128)(2,1)S(1)} %get-tuple-element.76), channel_id=1, source_target_pairs={{0,12},{1,5},{4,8},{5,1},{8,4},{9,13},{12,0},{13,9},{2,14},{3,7},{... | collective-permute-start | bytes 294920 | tf_op jit(solution)/shard_map/ppermute | solution.py:390
  48.4 4.5 %collective-permute-start.15 = (bf16[2,3,32,128]{3,2,1,0:T(8,128)(2,1)S(1)}, bf16[2,3,32,128]{3,2,1,0:T(8,128)(2,1)S(1)}, u32[]{:S(2)}, u32[]{:S(2)}) collective-permute-start(bf16[2,3,32,128]{3,2,1,0:T(8,128)(2,1)S(1)} %get-tuple-element.82), channel_id=1, source_target_pairs={{0,4},{1,13},{4,0},{5,9},{8,12},{9,5},{12,8},{13,1},{2,6},{3,15},{... | collective-permute-start | bytes 147464 | tf_op jit(solution)/shard_map/ppermute | solution.py:390
  49.0 5.0 %collective-permute-start.16 = (bf16[2,3,32,128]{3,2,1,0:T(8,128)(2,1)S(1)}, bf16[2,3,32,128]{3,2,1,0:T(8,128)(2,1)S(1)}, u32[]{:S(2)}, u32[]{:S(2)}) collective-permute-start(bf16[2,3,32,128]{3,2,1,0:T(8,128)(2,1)S(1)} %get-tuple-element.81), channel_id=1, source_target_pairs={{0,8},{1,9},{4,12},{5,13},{8,0},{9,1},{12,4},{13,5},{2,10},{3,11},... | collective-permute-start | bytes 147464 | tf_op jit(solution)/shard_map/ppermute | solution.py:390
  51.5 5.9 %collective-permute-start.17 = (bf16[2,3,32,128]{3,2,1,0:T(8,128)(2,1)S(1)}, bf16[2,3,32,128]{3,2,1,0:T(8,128)(2,1)S(1)}, u32[]{:S(2)}, u32[]{:S(2)}) collective-permute-start(bf16[2,3,32,128]{3,2,1,0:T(8,128)(2,1)S(1)} %get-tuple-element.80), channel_id=1, source_target_pairs={{0,12},{1,5},{4,8},{5,1},{8,4},{9,13},{12,0},{13,9},{2,14},{3,7},{... | collective-permute-start | bytes 147464 | tf_op jit(solution)/shard_map/ppermute | solution.py:390
